TPU v7x, 128 devices: a whole 4x4x4 slice. The times are simulated.
128 devices in a mesh: row: 8 (over y_hi, x), col: 4 (over y_lo, core), depth: 4 (over z).
Axes of the slice: x: 4, y: 4 (y_hi: 2, y_lo: 2; y = y_hi * 2 + y_lo), z: 4, core: 2. Of those that a mesh axis runs over, the one named last changes fastest.
Arguments:
- activations: bfloat16 [2048, 16384], P('depth', ('row', 'col')), may hold values from -6 to 6
- gradients: bfloat16 [2048, 16384], P('depth', ('row', 'col')), may hold values from -6 to 6
- act_factor: bfloat16 [16384, 16384], P('row', ('col', 'depth')), may hold values from -1.5 to 1.5
- grad_factor: bfloat16 [16384, 16384], P('row', ('col', 'depth')), may hold values from -1.5 to 1.5
Outputs:
- act_update: bfloat16 [16384, 16384], P('row', ('col', 'depth'))
- grad_update: bfloat16 [16384, 16384], P('row', ('col', 'depth'))
All inputs are finite; a program needn't handle non-finite values.
Results may differ from a plain program's by a relative error of at most 0.001.
Values may be sent and summed in bfloat16 or wider, within the bound.
No kernel may reach another device: no remote copies, remote signals or barrier semaphores. Data moves between devices by JAX's collectives and lax.ppermute only.
A program may use at most 128 MiB of HBM per device.

v0:
```python
import jax
import jax.numpy as jnp
from jax import lax
from jax.sharding import PartitionSpec as P

decay_rate = 0.5


def broadcast(block, axis, holder):
    block = jnp.where(lax.axis_index(axis) == holder, block, jnp.zeros_like(block))
    return lax.psum(block, axis)


def moving_average(previous, product, token_count):
    return (
        decay_rate * previous.astype(jnp.float32) + (1.0 - decay_rate) * (product / token_count)
    ).astype(jnp.bfloat16)


def shards(activations, gradients, act_factor, grad_factor):
    n_col = lax.axis_size("col")
    n_depth = lax.axis_size("depth")
    local_tokens, shard_width = activations.shape
    span_rows = shard_width * n_col
    span_cols = act_factor.shape[1]
    token_count = local_tokens * n_depth
    block_start = (lax.axis_index("col") * n_depth + lax.axis_index("depth")) * span_cols
    source_row = block_start // span_rows
    offset = block_start % span_rows
    stacked = (
        lax.all_gather(activations[None], ("col", "depth"), axis=0, tiled=True),
        lax.all_gather(gradients[None], ("col", "depth"), axis=0, tiled=True),
    )
    blocks = [member.reshape(n_col, n_depth, local_tokens, shard_width) for member in stacked]
    pieces = [
        lax.dynamic_slice_in_dim(member, offset // shard_width, span_cols // shard_width, 0)
        for member in blocks
    ]
    wanted = (broadcast(pieces[0], "row", source_row), broadcast(pieces[1], "row", source_row))
    products = [
        jnp.einsum(
            "cdtf,kdtg->cfkg", left_side, right_side, preferred_element_type=jnp.float32
        ).reshape(span_rows, span_cols)
        for left_side, right_side in zip(blocks, wanted)
    ]
    return (
        moving_average(act_factor, products[0], token_count),
        moving_average(grad_factor, products[1], token_count),
    )


def solution(mesh):
    return jax.shard_map(
        shards,
        mesh=mesh,
        in_specs=(
            P("depth", ("row", "col")),
            P("depth", ("row", "col")),
            P("row", ("col", "depth")),
            P("row", ("col", "depth")),
        ),
        out_specs=(P("row", ("col", "depth")), P("row", ("col", "depth"))),
        check_vma=False,
    )
```

profile of v0, /device:TPU:1, one launch (start us, length us, event | category | flops | bytes accessed | tf_op | source)
XLA Modules:
  0.0 402.9 jit_solution(13678679855882481802)
XLA Ops:
  7.2 0.0 all-gather.7.cloned.1.call-start
  7.2 0.7 all-gather.7.cloned.1.call-update
  7.9 0.0 all-gather.5.cloned.1.call-start
  7.9 0.7 all-gather.5.cloned.1.call-update
  8.6 0.0 all-reduce.3.cloned.1.call-start
  8.7 60.3 %all-gather.7.cloned.1.call-done = bf16[8192,512]{1,0:T(8,128)(2,1)} async-done(((bf16[512,512]{1,0:T(8,128)(2,1)}), bf16[8192,512]{1,0:T(8,128)(2,1)}) %all-gather.7.cloned.1.call-update) | async-done | bytes 8388624 | tf_op jit(solution)/shard_map/all_gather | solution.py:32
  69.1 4.5 %dynamic-slice_select_fusion = bf16[2,4,512,512]{3,2,1,0:T(8,128)(2,1)} fusion(bf16[4,4,512,512]{3,2,1,0:T(8,128)(2,1)} %bitcast.46, s32[]{:T(128)S(6)} %select_n.35, pred[]{:T(512)S(6)} %eq.6), kind=kLoop, calls=%fused_computation.10 | loop fusion | flops 2097152 | bytes 8388613 | tf_op jit(solution)/shard_map/jit(_where)/select_n | solution.py:10
  73.5 54.0 %all-gather.5.cloned.1.call-done = bf16[8192,512]{1,0:T(8,128)(2,1)} async-done(((bf16[512,512]{1,0:T(8,128)(2,1)}), bf16[8192,512]{1,0:T(8,128)(2,1)}) %all-gather.5.cloned.1.call-update) | async-done | bytes 8388624 | tf_op jit(solution)/shard_map/all_gather | solution.py:31
  127.5 4.5 %dynamic-slice_select_fusion.1 = bf16[2,4,512,512]{3,2,1,0:T(8,128)(2,1)} fusion(bf16[4,4,512,512]{3,2,1,0:T(8,128)(2,1)} %bitcast.48, s32[]{:T(128)S(6)} %select_n.35, pred[]{:T(512)S(6)} %eq.6), kind=kLoop, calls=%fused_computation.11 | loop fusion | flops 2097152 | bytes 8388613 | tf_op jit(solution)/shard_map/jit(_where)/select_n | solution.py:10
  132.0 0.0 all-reduce.3.cloned.1.call-update
  132.0 187.0 %all-reduce.3.cloned.1.call-done = (bf16[2,4,512,512]{3,2,1,0:T(8,128)(2,1)}, bf16[2,4,512,512]{3,2,1,0:T(8,128)(2,1)}) async-done(((bf16[2,4,512,512]{3,2,1,0:T(8,128)(2,1)}, bf16[2,4,512,512]{3,2,1,0:T(8,128)(2,1)}), (bf16[2,4,512,512]{3,2,1,0:T(8,128)(2,1)}, bf16[2,4,512,512]{3,2,1,0:T(8,128)(2,1)})) %all-reduce.3.cloned.1.call-update) | async-done | bytes 8388624 | tf_op jit(solution)/shard_map/psum | solution.py:11
  319.0 14.7 %fusion.1 = f32[4,512,2,512]{1,3,0,2:T(8,128)} fusion(bf16[4,4,512,512,1]{3,2,1,0,4:T(8,128)(2,1)} %bitcast.49, bf16[2,4,512,512]{3,2,1,0:T(8,128)(2,1)} %get-tuple-element.2), kind=kOutput, calls=%fused_computation.3 | convolution fusion | flops 8592031744 | bytes 20971520 | tf_op jit(solution)/shard_map/cdtf,kdtg->cfkg/dot_general | solution.py:41
  333.7 13.3 %copy.9 = f32[4,512,2,512]{3,2,1,0:T(2,128)} copy(f32[4,512,2,512]{1,3,0,2:T(8,128)} %fusion.1) | data formatting | bytes 16777216 | tf_op jit(solution)/shard_map/mul | solution.py:16
  347.0 0.0 copy-start.2
  347.0 8.9 %copy.20 = f32[256,8,2,512]{3,1,2,0:T(8,128)} copy(f32[256,8,2,512]{3,2,1,0:T(2,128)} %bitcast.42) | data formatting | bytes 16777216
  355.9 0.0 copy-done.2
  355.9 13.7 %fusion = f32[4,512,2,512]{1,3,0,2:T(8,128)} fusion(bf16[4,4,512,512,1]{3,2,1,0,4:T(8,128)(2,1)} %bitcast.47, bf16[2,4,512,512]{3,2,1,0:T(8,128)(2,1)S(1)} %copy-done.2), kind=kOutput, calls=%fused_computation.1 | convolution fusion | flops 8592031744 | bytes 20971520 | tf_op jit(solution)/shard_map/cdtf,kdtg->cfkg/dot_general | solution.py:41
  369.6 13.4 %copy.11 = f32[4,512,2,512]{3,2,1,0:T(2,128)} copy(f32[4,512,2,512]{1,3,0,2:T(8,128)} %fusion) | data formatting | bytes 16777216 | tf_op jit(solution)/shard_map/mul | solution.py:16
  383.0 0.0 copy-start
  383.0 0.0 copy-start.1
  383.0 5.7 %copy.21 = f32[256,8,2,512]{3,1,2,0:T(8,128)S(1)} copy(f32[256,8,2,512]{3,2,1,0:T(2,128)} %bitcast.43) | data formatting | bytes 16777216
  388.7 0.0 copy-done
  388.7 0.1 copy-done.1
  388.8 7.6 %add_convert_fusion = (bf16[2048,1024]{1,0:T(8,128)(2,1)}, bf16[2048,1024]{1,0:T(8,128)(2,1)}) fusion(f32[2048,1024]{1,0:T(8,128)S(1)} %bitcast.45, bf16[2048,1024]{1,0:T(8,128)(2,1)S(1)} %copy-done, f32[2048,1024]{1,0:T(8,128)} %bitcast.44, bf16[2048,1024]{1,0:T(8,128)(2,1)S(1)} %copy-done.1), kind=kLoop, calls=%fused_computation.4 | loop fusion | flops 16777216 | bytes 33554432 | tf_op jit(solution)/shard_map/convert_element_type | solution.py:17
Async XLA Ops:
  7.2 61.9 %all-gather.7.cloned.1.call-start = ((), (), s32[]{:S(2)}) async-start(), calls=%async_computation.1 | async-start | bytes 8912896 | tf_op jit(solution)/shard_map/all_gather | solution.py:32
  7.9 119.7 %all-gather.5.cloned.1.call-start = ((), (), s32[]{:S(2)}) async-start(), calls=%async_computation | async-start | bytes 8912896 | tf_op jit(solution)/shard_map/all_gather | solution.py:31
  8.6 310.4 %all-reduce.3.cloned.1.call-start = ((), (), s32[]{:S(2)}) async-start(), calls=%async_computation.2 | async-start | bytes 16777216 | tf_op jit(solution)/shard_map/psum | solution.py:11
  347.0 8.9 %copy-start.2 = (bf16[2,4,512,512]{3,2,1,0:T(8,128)(2,1)S(1)}, bf16[2,4,512,512]{3,2,1,0:T(8,128)(2,1)}, u32[]{:S(2)}) copy-start(bf16[2,4,512,512]{3,2,1,0:T(8,128)(2,1)} %get-tuple-element.3) | copy-start | bytes 12582916
  383.0 5.7 %copy-start = (bf16[2048,1024]{1,0:T(8,128)(2,1)S(1)}, bf16[2048,1024]{1,0:T(8,128)(2,1)}, u32[]{:S(2)}) copy-start(bf16[2048,1024]{1,0:T(8,128)(2,1)} %param.7) | copy-start | bytes 12582916
  383.0 5.9 %copy-start.1 = (bf16[2048,1024]{1,0:T(8,128)(2,1)S(1)}, bf16[2048,1024]{1,0:T(8,128)(2,1)}, u32[]{:S(2)}) copy-start(bf16[2048,1024]{1,0:T(8,128)(2,1)} %param.6) | copy-start | bytes 12582916
Sparse Core Ops, SparseCore 0:
  9.7 59.3 all-gather.6
  70.7 56.7 all-gather.4
  132.2 186.8 all-reduce.2
where the time goes:
time: 404 us; the launch traced here: 403 us
  waiting for transfers between devices  303 us (75%)
  local copies, waits for them, and re-layouts  41.4 us (10%)
  matrix products  28.4 us (7%)
  other arithmetic  16.5 us (4%)
  between operations  13.8 us (3%)
    psum x1, waiting for transfers between devices, broadcast(): return lax.psum(block, axis)  187 us
    all_gather x1, waiting for transfers between devices, shards(): lax.all_gather(gradients[None], ('col', 'depth'), axis=0, tiled=True)  60.3 us
    all_gather x1, waiting for transfers between devices, shards(): lax.all_gather(activations[None], ('col', 'depth'), axis=0, tiled=True)  54 us
    dot_general x2, matrix products, shards(): jnp.einsum('cdtf,kdtg->cfkg', left_side, right_side, preferred_element_ty...  28.4 us
    mul x2, local copies, waits for them, and re-layouts, moving_average(): (1.0 - decay_rate) * (product / token_count)  26.7 us
    unnamed x8, local copies, waits for them, and re-layouts  14.7 us
    select_n x2, other arithmetic, broadcast(): jnp.where(lax.axis_index(axis) == holder, block, jnp.zeros_like(block))  8.95 us
  transfers between devices with their start and end apart: 3, of which 3 were waited for; matrix products, arithmetic and copies ran while one was open for 1% of the time, Pallas kernels for 0%

commit v1 on v0

v1 whole, which is shorter than its diff:
```python
import functools

import jax
import jax.numpy as jnp
from jax import lax
from jax.experimental import pallas as pl
from jax.experimental.pallas import tpu as pltpu
from jax.sharding import Mesh, PartitionSpec as P

decay_rate = 0.5
AXES = ("yh", "x", "yl", "core", "z")
SIZES = (2, 4, 2, 2, 4)
PIECE = 512
ROW_TILE = 256


def index(yh, x, yl, core, z):
    return (((yh % 2 * 4 + x % 4) * 2 + yl % 2) * 2 + core % 2) * 4 + z % 4


def permutation(move):
    every = [
        (yh, x, yl, core, z)
        for yh in range(2)
        for x in range(4)
        for yl in range(2)
        for core in range(2)
        for z in range(4)
    ]
    return [(index(*place), index(*move(*place))) for place in every]


def scatter_move(yh, x, yl, core, z):
    depth = 2 * (x % 2) + yl
    return core, x + z - depth + 2 + 2 * core, yh, x // 2, depth


def y_move(yh, x, yl, core, z):
    y = (2 * yh + yl + 1 - 2 * core) % 4
    return y // 2, x, y % 2, core, z


SCATTER = permutation(scatter_move)
RING_X = permutation(lambda yh, x, yl, core, z: (yh, x + 1 - 2 * core, yl, core, z))
RING_Z = permutation(lambda yh, x, yl, core, z: (yh, x, yl, core, z + 1 - 2 * core))
RING_Y = permutation(y_move)
SWAP_YL = permutation(lambda yh, x, yl, core, z: (yh, x, 1 - yl, core, z))
SWAP_CORE = permutation(lambda yh, x, yl, core, z: (yh, x, yl, 1 - core, z))


def send(block, moves):
    return lax.ppermute(block, AXES, moves)


def update_kernel(tokens, place, *refs):
    left_refs, right_refs = refs[:8], refs[8:16]
    factor_ref, out_ref, left, right, left_sems, right_sems = refs[16:]
    yh, x, yl, core, z = (place[i] for i in range(5))
    step = pl.program_id(0)

    @pl.when(step == 0)
    def _():
        copies = []
        toward = 1 - 2 * core
        for s in range(4):
            for chain in range(2):
                source = lax.rem(x - s * toward + 4, 4)
                half = lax.rem(yh + chain, 2)
                token = lax.rem(source - 2 * core - z // 2 + z + 2 + 2 * half + 8, 4)
                copies.append(
                    pltpu.make_async_copy(
                        right_refs[4 * chain + s],
                        right.at[
                            pl.ds(pl.multiple_of(token * PIECE, PIECE), PIECE),
                            pl.ds(pl.multiple_of(half * PIECE, PIECE), PIECE),
                        ],
                        right_sems.at[4 * chain + s],
                    )
                )
        for s in range(4):
            for other in range(2):
                held_by = lax.rem(core + other, 2)
                token = lax.rem(z - s * (1 - 2 * held_by) + 4, 4)
                for partner in range(2):
                    block = 2 * lax.rem(yl + partner, 2) + held_by
                    copies.append(
                        pltpu.make_async_copy(
                            left_refs[4 * other + s].at[pl.ds(partner * PIECE, PIECE), :],
                            left.at[
                                pl.ds(pl.multiple_of(block * PIECE, PIECE), PIECE),
                                pl.ds(pl.multiple_of(token * PIECE, PIECE), PIECE),
                            ],
                            left_sems.at[8 * other + 2 * s + partner],
                        )
                    )
        for copy in copies:
            copy.start()
        for copy in copies:
            copy.wait()

    rows = pl.ds(pl.multiple_of(step * ROW_TILE, ROW_TILE), ROW_TILE)
    product = jnp.dot(left[rows, :], right[...], preferred_element_type=jnp.float32)
    out_ref[...] = (
        decay_rate * factor_ref[...].astype(jnp.float32)
        + (1.0 - decay_rate) * (product / tokens)
    ).astype(out_ref.dtype)


def update(place, lefts, rights, factor):
    rows, columns = factor.shape
    tokens = 4 * PIECE
    anywhere = pl.BlockSpec(memory_space=pl.ANY)
    tile = pl.BlockSpec((ROW_TILE, columns), lambda i, place: (i, 0))
    return pl.pallas_call(
        functools.partial(update_kernel, tokens),
        out_shape=jax.ShapeDtypeStruct((rows, columns), factor.dtype),
        grid_spec=pltpu.PrefetchScalarGridSpec(
            num_scalar_prefetch=1,
            grid=(rows // ROW_TILE,),
            in_specs=[anywhere] * 16 + [tile],
            out_specs=tile,
            scratch_shapes=[
                pltpu.VMEM((rows, tokens), jnp.bfloat16),
                pltpu.VMEM((tokens, columns), jnp.bfloat16),
                pltpu.SemaphoreType.DMA((16,)),
                pltpu.SemaphoreType.DMA((8,)),
            ],
        ),
        compiler_params=pltpu.CompilerParams(vmem_limit_bytes=28 * 2**20),
        cost_estimate=pl.CostEstimate(
            flops=2 * rows * columns * tokens,
            bytes_accessed=2 * (rows * tokens + tokens * columns + 2 * rows * columns),
            transcendentals=0,
        ),
    )(place, *lefts, *rights, factor)


def ring(block, moves):
    blocks = [block]
    for _ in range(3):
        blocks.append(send(blocks[-1], moves))
    return blocks


def refresh(place, samples, factor):
    scattered = send(samples, SCATTER)
    partner = send(samples, SWAP_YL)
    mine = ring(jnp.concatenate([samples.T, partner.T], axis=0), RING_Z)
    others = [send(block, SWAP_CORE) for block in mine]
    across = send(send(scattered, RING_Y), RING_Y)
    rights = ring(scattered, RING_X) + ring(across, RING_X)
    return update(place, mine + others, rights, factor)


def shards(activations, gradients, act_factor, grad_factor):
    place = jnp.stack([lax.axis_index(axis) for axis in AXES]).astype(jnp.int32)
    return (
        refresh(place, activations, act_factor),
        refresh(place, gradients, grad_factor),
    )


def solution(mesh):
    fine = Mesh(mesh.devices.reshape(SIZES), AXES)
    row, col, depth = ("yh", "x"), ("yl", "core"), "z"
    samples = P(depth, row + col)
    factor = P(row, col + (depth,))
    return jax.shard_map(
        shards,
        mesh=fine,
        in_specs=(samples, samples, factor, factor),
        out_specs=(factor, factor),
        check_vma=False,
    )
```

time: 404 us -> 169 us (0.42)
  waiting for transfers between devices: 303 us -> 54.6 us
  starting transfers between devices: 0.11 us -> 52.9 us
  Pallas kernels: 0 us -> 31.2 us
  matrix products: 28.4 us -> 0 us
  other arithmetic: 16.5 us -> 1.28 us
  local copies, waits for them, and re-layouts: 41.4 us -> 27.4 us
  between operations: 13.8 us -> 1.08 us
    psum x1 -> x0, waiting for transfers between devices: 187 us -> none  [broadcast(): return lax.psum(block, axis)]
    all_gather x2 -> x0, waiting for transfers between devices: 114 us -> none  [the longest x1 60.3 us: shards(): lax.all_gather(gradients[None], ('col', 'depth'), axis=0, tiled=True)]
    ppermute x0 -> x34, waiting for transfers between devices: none -> 54.6 us  [send(): return lax.ppermute(block, AXES, moves)]
    ppermute x0 -> x34, starting transfers between devices: none -> 52.9 us  [send(): return lax.ppermute(block, AXES, moves)]
    pallas_call x0 -> x2, Pallas kernels: none -> 31.2 us  [update(): pl.pallas_call(functools.partial(update_kernel, tokens), out_shape=jax.Sh...]
    dot_general x2 -> x0, matrix products: 28.4 us -> none  [shards(): jnp.einsum('cdtf,kdtg->cfkg', left_side, right_side, preferred_element_ty...]
    mul x2 -> x0, local copies, waits for them, and re-layouts: 26.7 us -> none  [moving_average(): (1.0 - decay_rate) * (product / token_count)]
    unnamed x8 -> x72, local copies, waits for them, and re-layouts: 14.7 us -> 27.3 us
  transfers between devices with their start and end apart: 3 -> 34, of which waited for: 3 -> 11; matrix products, arithmetic and copies ran while one was open for 1% -> 2% of each run, Pallas kernels for 0% -> 9%
where the time goes in v1:
time: 169 us; the launch traced here: 168 us
  waiting for transfers between devices  54.6 us (32%)
  starting transfers between devices  52.9 us (31%)
  Pallas kernels  31.2 us (18%)
  local copies, waits for them, and re-layouts  27.4 us (16%)
    ppermute x34, waiting for transfers between devices, send(): return lax.ppermute(block, AXES, moves)  54.6 us
    ppermute x34, starting transfers between devices, send(): return lax.ppermute(block, AXES, moves)  52.9 us
    pallas_call x2, Pallas kernels, update(): pl.pallas_call(functools.partial(update_kernel, tokens), out_shape=jax.Sh...  31.2 us
    unnamed x72, local copies, waits for them, and re-layouts  27.3 us
  transfers between devices with their start and end apart: 34, of which 11 were waited for; matrix products, arithmetic and copies ran while one was open for 2% of the time, Pallas kernels for 9%

profile of v1, /device:TPU:1, one launch (start us, length us, event | category | flops | bytes accessed | tf_op | source)
XLA Modules:
  0.0 168.3 jit_solution(3927959021097145590)
XLA Ops:
  0.6 1.3 copy.8
  1.9 2.2 %collective-permute-start.17 = (bf16[512,512]{0,1:T(8,128)(2,1)S(1)}, bf16[512,512]{0,1:T(8,128)(2,1)S(1)}, u32[]{:S(2)}, u32[]{:S(2)}) collective-permute-start(bf16[512,512]{0,1:T(8,128)(2,1)S(1)} %copy.8), channel_id=1, source_target_pairs={{0,8},{1,9},{2,10},{3,11},{4,12},{5,13},{6,14},{7,15},{8,0},{9,1},... | collective-permute-start | bytes 1572872 | tf_op jit(solution)/shard_map/ppermute | solution.py:52
  4.1 5.4 %collective-permute-start.25 = (bf16[512,512]{1,0:T(8,128)(2,1)}, bf16[512,512]{1,0:T(8,128)(2,1)S(1)}, u32[]{:S(2)}, u32[]{:S(2)}) collective-permute-start(bf16[512,512]{1,0:T(8,128)(2,1)} %param.5), channel_id=1, source_target_pairs={{0,32},{1,48},{2,0},{3,16},{4,64},{5,80},{6,96},{7,112},{8,17},{9,... | collective-permute-start | bytes 1572872 | tf_op jit(solution)/shard_map/ppermute | solution.py:52
  9.5 4.0 %collective-permute-start.8 = (bf16[512,512]{1,0:T(8,128)(2,1)}, bf16[512,512]{1,0:T(8,128)(2,1)}, u32[]{:S(2)}, u32[]{:S(2)}) collective-permute-start(bf16[512,512]{1,0:T(8,128)(2,1)} %param.4), channel_id=1, source_target_pairs={{0,32},{1,48},{2,0},{3,16},{4,64},{5,80},{6,96},{7,112},{8,17},{9,... | collective-permute-start | bytes 1572872 | tf_op jit(solution)/shard_map/ppermute | solution.py:52
  13.5 1.3 copy.6
  14.7 1.3 collective-permute-start
  16.0 10.6 %collective-permute-done.17 = bf16[512,512]{0,1:T(8,128)(2,1)S(1)} collective-permute-done((bf16[512,512]{0,1:T(8,128)(2,1)S(1)}, bf16[512,512]{0,1:T(8,128)(2,1)S(1)}, u32[]{:S(2)}, u32[]{:S(2)}) %collective-permute-start.17) | collective-permute-done | bytes 524320 | tf_op jit(solution)/shard_map/ppermute | solution.py:52
  26.7 1.1 collective-permute-done.25.refs_8_
  27.8 0.2 collective-permute-start.29
  28.0 8.0 %collective-permute-start.26 = (bf16[512,512]{1,0:T(8,128)(2,1)S(1)}, bf16[512,512]{1,0:T(8,128)(2,1)S(1)}, u32[]{:S(2)}, u32[]{:S(2)}) collective-permute-start(bf16[512,512]{1,0:T(8,128)(2,1)S(1)} %collective-permute-done.25.refs_8_), channel_id=1, source_target_pairs={{0,16},{1,17},{2,18},{3,19},{4,52},{5,53},{6,54},{7,55},{8,24},{9,... | collective-permute-start | bytes 1572872 | tf_op jit(solution)/shard_map/ppermute | solution.py:52
  36.0 0.8 copy-done.8
  36.9 1.3 collective-permute-done.8.refs_8_
  38.2 11.1 %collective-permute-done = bf16[512,512]{0,1:T(8,128)(2,1)S(1)} collective-permute-done((bf16[512,512]{0,1:T(8,128)(2,1)S(1)}, bf16[512,512]{0,1:T(8,128)(2,1)S(1)}, u32[]{:S(2)}, u32[]{:S(2)}) %collective-permute-start) | collective-permute-done | bytes 524320 | tf_op jit(solution)/shard_map/ppermute | solution.py:52
  49.4 1.2 pad_maximum_fusion.refs_0_
  50.7 4.3 %collective-permute-start.1 = (bf16[1024,512]{1,0:T(8,128)(2,1)S(1)}, bf16[1024,512]{1,0:T(8,128)(2,1)}, u32[]{:S(2)}, u32[]{:S(2)}) collective-permute-start(bf16[1024,512]{1,0:T(8,128)(2,1)S(1)} %pad_maximum_fusion.refs_0_), channel_id=1, source_target_pairs={{0,1},{1,2},{2,3},{3,0},{4,7},{5,4},{6,5},{7,6},{8,9},{9,10},{10,1... | collective-permute-start | bytes 3145736 | tf_op jit(solution)/shard_map/ppermute | solution.py:52
  55.0 0.1 collective-permute-start.19
  55.1 2.8 %collective-permute-done.9.refs_9_ = bf16[512,512]{1,0:T(8,128)(2,1)S(1)} collective-permute-done((bf16[512,512]{1,0:T(8,128)(2,1)}, bf16[512,512]{1,0:T(8,128)(2,1)S(1)}, u32[]{:S(2)}, u32[]{:S(2)}) %collective-permute-start.9) | collective-permute-done | bytes 524320 | tf_op jit(solution)/shard_map/ppermute | solution.py:52
  57.9 2.6 %collective-permute-start.4 = (bf16[1024,512]{1,0:T(8,128)(2,1)S(1)}, bf16[1024,512]{1,0:T(8,128)(2,1)S(1)}, u32[]{:S(2)}, u32[]{:S(2)}) collective-permute-start(bf16[1024,512]{1,0:T(8,128)(2,1)S(1)} %pad_maximum_fusion.refs_0_), channel_id=1, source_target_pairs={{0,4},{1,5},{2,6},{3,7},{4,0},{5,1},{6,2},{7,3},{8,12},{9,13},{10,... | collective-permute-start | bytes 3145736 | tf_op jit(solution)/shard_map/ppermute | solution.py:52
  60.5 1.0 copy-done.2
  61.4 7.4 %collective-permute-done.27.refs_10_ = bf16[512,512]{1,0:T(8,128)(2,1)S(1)} collective-permute-done((bf16[512,512]{1,0:T(8,128)(2,1)S(1)}, bf16[512,512]{1,0:T(8,128)(2,1)S(1)}, u32[]{:S(2)}, u32[]{:S(2)}) %collective-permute-start.27) | collective-permute-done | bytes 524320 | tf_op jit(solution)/shard_map/ppermute | solution.py:52
  68.9 1.2 collective-permute-start.10
  70.1 0.8 copy-done.10
  70.9 4.5 %collective-permute-start.2 = (bf16[1024,512]{1,0:T(8,128)(2,1)}, bf16[1024,512]{1,0:T(8,128)(2,1)}, u32[]{:S(2)}, u32[]{:S(2)}) collective-permute-start(bf16[1024,512]{1,0:T(8,128)(2,1)} %collective-permute-done.1.refs_1_), channel_id=1, source_target_pairs={{0,1},{1,2},{2,3},{3,0},{4,7},{5,4},{6,5},{7,6},{8,9},{9,10},{10,1... | collective-permute-start | bytes 3145736 | tf_op jit(solution)/shard_map/ppermute | solution.py:52
  75.4 0.8 copy-done.14
  76.2 4.6 %collective-permute-done.19.refs_2_ = bf16[1024,512]{1,0:T(8,128)(2,1)} collective-permute-done((bf16[1024,512]{1,0:T(8,128)(2,1)S(1)}, bf16[1024,512]{1,0:T(8,128)(2,1)}, u32[]{:S(2)}, u32[]{:S(2)}) %collective-permute-start.19) | collective-permute-done | bytes 1048608 | tf_op jit(solution)/shard_map/ppermute | solution.py:52
  80.8 0.6 collective-permute-start.20
  81.4 1.0 copy-done.4
  82.4 2.9 %collective-permute-start.28 = (bf16[512,512]{1,0:T(8,128)(2,1)S(1)}, bf16[512,512]{1,0:T(8,128)(2,1)S(1)}, u32[]{:S(2)}, u32[]{:S(2)}) collective-permute-start(bf16[512,512]{1,0:T(8,128)(2,1)S(1)} %collective-permute-done.27.refs_10_), channel_id=1, source_target_pairs={{0,16},{1,17},{2,18},{3,19},{4,52},{5,53},{6,54},{7,55},{8,24},{9,... | collective-permute-start | bytes 1572872 | tf_op jit(solution)/shard_map/ppermute | solution.py:52
  85.3 0.8 copy-done.20
  86.1 0.9 collective-permute-start.14
  87.0 0.8 copy-done.16
  87.7 3.7 %collective-permute-done.28.refs_11_ = bf16[512,512]{1,0:T(8,128)(2,1)S(1)} collective-permute-done((bf16[512,512]{1,0:T(8,128)(2,1)S(1)}, bf16[512,512]{1,0:T(8,128)(2,1)S(1)}, u32[]{:S(2)}, u32[]{:S(2)}) %collective-permute-start.28) | collective-permute-done | bytes 524320 | tf_op jit(solution)/shard_map/ppermute | solution.py:52
  91.4 0.8 copy-done.26
  92.2 3.5 %collective-permute-start.32 = (bf16[512,512]{1,0:T(8,128)(2,1)S(1)}, bf16[512,512]{1,0:T(8,128)(2,1)S(1)}, u32[]{:S(2)}, u32[]{:S(2)}) collective-permute-start(bf16[512,512]{1,0:T(8,128)(2,1)S(1)} %collective-permute-done.31.refs_13_), channel_id=1, source_target_pairs={{0,16},{1,17},{2,18},{3,19},{4,52},{5,53},{6,54},{7,55},{8,24},{9,... | collective-permute-start | bytes 1572872 | tf_op jit(solution)/shard_map/ppermute | solution.py:52
  95.7 0.8 copy-done.24
  96.5 2.1 %collective-permute-start.3 = (bf16[1024,512]{1,0:T(8,128)(2,1)}, bf16[1024,512]{1,0:T(8,128)(2,1)}, u32[]{:S(2)}, u32[]{:S(2)}) collective-permute-start(bf16[1024,512]{1,0:T(8,128)(2,1)} %collective-permute-done.2.refs_2_), channel_id=1, source_target_pairs={{0,1},{1,2},{2,3},{3,0},{4,7},{5,4},{6,5},{7,6},{8,9},{9,10},{10,1... | collective-permute-start | bytes 3145736 | tf_op jit(solution)/shard_map/ppermute | solution.py:52
  98.6 0.3 collective-permute-start.23
  98.9 4.4 %collective-permute-done.20.refs_3_ = bf16[1024,512]{1,0:T(8,128)(2,1)} collective-permute-done((bf16[1024,512]{1,0:T(8,128)(2,1)}, bf16[1024,512]{1,0:T(8,128)(2,1)}, u32[]{:S(2)}, u32[]{:S(2)}) %collective-permute-start.20) | collective-permute-done | bytes 1048608 | tf_op jit(solution)/shard_map/ppermute | solution.py:52
  103.3 0.1 collective-permute-start.24
  103.4 1.0 copy-done.6
  104.4 2.9 %collective-permute-start.15 = (bf16[512,512]{1,0:T(8,128)(2,1)S(1)}, bf16[512,512]{1,0:T(8,128)(2,1)S(1)}, u32[]{:S(2)}, u32[]{:S(2)}) collective-permute-start(bf16[512,512]{1,0:T(8,128)(2,1)S(1)} %collective-permute-done.14.refs_13_), channel_id=1, source_target_pairs={{0,16},{1,17},{2,18},{3,19},{4,52},{5,53},{6,54},{7,55},{8,24},{9,... | collective-permute-start | bytes 1572872 | tf_op jit(solution)/shard_map/ppermute | solution.py:52
  107.3 0.8 copy-done.22
  108.1 0.8 copy-done.30
  108.9 4.5 %collective-permute-done.15.refs_14_ = bf16[512,512]{1,0:T(8,128)(2,1)S(1)} collective-permute-done((bf16[512,512]{1,0:T(8,128)(2,1)S(1)}, bf16[512,512]{1,0:T(8,128)(2,1)S(1)}, u32[]{:S(2)}, u32[]{:S(2)}) %collective-permute-start.15) | collective-permute-done | bytes 524320 | tf_op jit(solution)/shard_map/ppermute | solution.py:52
  113.4 0.8 copy-done.28
  114.2 1.8 %collective-permute-start.5 = (bf16[1024,512]{1,0:T(8,128)(2,1)}, bf16[1024,512]{1,0:T(8,128)(2,1)}, u32[]{:S(2)}, u32[]{:S(2)}) collective-permute-start(bf16[1024,512]{1,0:T(8,128)(2,1)} %collective-permute-done.1.refs_1_), channel_id=1, source_target_pairs={{0,4},{1,5},{2,6},{3,7},{4,0},{5,1},{6,2},{7,3},{8,12},{9,13},{10,... | collective-permute-start | bytes 3145736 | tf_op jit(solution)/shard_map/ppermute | solution.py:52
  116.0 3.0 %collective-permute-done.33.refs_15_ = bf16[512,512]{1,0:T(8,128)(2,1)S(1)} collective-permute-done((bf16[512,512]{1,0:T(8,128)(2,1)S(1)}, bf16[512,512]{1,0:T(8,128)(2,1)S(1)}, u32[]{:S(2)}, u32[]{:S(2)}) %collective-permute-start.33) | collective-permute-done | bytes 524320 | tf_op jit(solution)/shard_map/ppermute | solution.py:52
  119.0 0.8 copy-done.32
  119.8 1.8 %collective-permute-start.6 = (bf16[1024,512]{1,0:T(8,128)(2,1)}, bf16[1024,512]{1,0:T(8,128)(2,1)}, u32[]{:S(2)}, u32[]{:S(2)}) collective-permute-start(bf16[1024,512]{1,0:T(8,128)(2,1)} %collective-permute-done.2.refs_2_), channel_id=1, source_target_pairs={{0,4},{1,5},{2,6},{3,7},{4,0},{5,1},{6,2},{7,3},{8,12},{9,13},{10,... | collective-permute-start | bytes 3145736 | tf_op jit(solution)/shard_map/ppermute | solution.py:52
  121.7 1.9 %collective-permute-start.11 = (bf16[512,512]{1,0:T(8,128)(2,1)}, bf16[512,512]{1,0:T(8,128)(2,1)S(1)}, u32[]{:S(2)}, u32[]{:S(2)}) collective-permute-start(bf16[512,512]{1,0:T(8,128)(2,1)} %copy-done.18), channel_id=1, source_target_pairs={{0,16},{1,17},{2,18},{3,19},{4,52},{5,53},{6,54},{7,55},{8,24},{9,... | collective-permute-start | bytes 1572872 | tf_op jit(solution)/shard_map/ppermute | solution.py:52
  123.6 0.3 collective-permute-start.16
  123.8 2.2 %copy-done = bf16[2048,1024]{1,0:T(8,128)(2,1)S(1)} copy-done((bf16[2048,1024]{1,0:T(8,128)(2,1)S(1)}, bf16[2048,1024]{1,0:T(8,128)(2,1)}, u32[]{:S(2)}) %copy-start) | copy-done | bytes 4194328
  126.0 1.2 copy-done.3
  127.3 1.2 copy-done.7
  128.5 1.0 copy-done.9
  129.5 1.0 copy-done.13
  130.6 1.0 copy-done.15
  131.6 1.0 copy-done.21
  132.6 1.0 copy-done.25
  133.7 1.0 copy-done.27
  134.7 1.0 copy-done.31
  135.8 1.0 copy-done.33
  136.9 15.6 %shard_map.60 = bf16[2048,1024]{1,0:T(8,128)(2,1)} custom-call(s32[5]{0:T(128)S(1)} %stack.23.place, bf16[1024,512]{1,0:T(8,128)(2,1)S(1)} %pad_maximum_fusion.1.refs_0_, bf16[1024,512]{1,0:T(8,128)(2,1)S(1)} %collective-permute-done.18.refs_1_, bf16[1024,512]{1,0:T(8,128)(2,1)} %collective-permute-done.19.refs_2_, ...), custom_call_target="tpu_custom_call" | custom-call | flops 8589934592 | bytes 20971520 | tf_op jit(solution)/shard_map/pallas_call | solution.py:114
  152.6 15.6 %shard_map.59 = bf16[2048,1024]{1,0:T(8,128)(2,1)} custom-call(s32[5]{0:T(128)S(1)} %stack.23.place, bf16[1024,512]{1,0:T(8,128)(2,1)S(1)} %pad_maximum_fusion.refs_0_, bf16[1024,512]{1,0:T(8,128)(2,1)} %collective-permute-done.1.refs_1_, bf16[1024,512]{1,0:T(8,128)(2,1)} %collective-permute-done.2.refs_2_, ...), custom_call_target="tpu_custom_call" | custom-call | flops 8589934592 | bytes 20971520 | tf_op jit(solution)/shard_map/pallas_call | solution.py:114
  (81 shorter events, 0.5 us)
Async XLA Ops:
  1.9 24.7 %collective-permute-start.17 = (bf16[512,512]{0,1:T(8,128)(2,1)S(1)}, bf16[512,512]{0,1:T(8,128)(2,1)S(1)}, u32[]{:S(2)}, u32[]{:S(2)}) collective-permute-start(bf16[512,512]{0,1:T(8,128)(2,1)S(1)} %copy.8), channel_id=1, source_target_pairs={{0,8},{1,9},{2,10},{3,11},{4,12},{5,13},{6,14},{7,15},{8,0},{9,1},... | collective-permute-start | bytes 1572872 | tf_op jit(solution)/shard_map/ppermute | solution.py:52
  4.1 23.7 %collective-permute-start.25 = (bf16[512,512]{1,0:T(8,128)(2,1)}, bf16[512,512]{1,0:T(8,128)(2,1)S(1)}, u32[]{:S(2)}, u32[]{:S(2)}) collective-permute-start(bf16[512,512]{1,0:T(8,128)(2,1)} %param.5), channel_id=1, source_target_pairs={{0,32},{1,48},{2,0},{3,16},{4,64},{5,80},{6,96},{7,112},{8,17},{9,... | collective-permute-start | bytes 1572872 | tf_op jit(solution)/shard_map/ppermute | solution.py:52
  9.5 28.7 %collective-permute-start.8 = (bf16[512,512]{1,0:T(8,128)(2,1)}, bf16[512,512]{1,0:T(8,128)(2,1)}, u32[]{:S(2)}, u32[]{:S(2)}) collective-permute-start(bf16[512,512]{1,0:T(8,128)(2,1)} %param.4), channel_id=1, source_target_pairs={{0,32},{1,48},{2,0},{3,16},{4,64},{5,80},{6,96},{7,112},{8,17},{9,... | collective-permute-start | bytes 1572872 | tf_op jit(solution)/shard_map/ppermute | solution.py:52
  14.7 34.7 %copy-start.34 = (bf16[512,512]{0,1:T(8,128)(2,1)}, bf16[512,512]{0,1:T(8,128)(2,1)S(1)}, u32[]{:S(2)}) copy-start(bf16[512,512]{0,1:T(8,128)(2,1)S(1)} %copy.6) | copy-start | bytes 1572868
  14.7 34.6 %collective-permute-start = (bf16[512,512]{0,1:T(8,128)(2,1)S(1)}, bf16[512,512]{0,1:T(8,128)(2,1)S(1)}, u32[]{:S(2)}, u32[]{:S(2)}) collective-permute-start(bf16[512,512]{0,1:T(8,128)(2,1)S(1)} %copy.6), channel_id=1, source_target_pairs={{0,8},{1,9},{2,10},{3,11},{4,12},{5,13},{6,14},{7,15},{8,0},{9,1},... | collective-permute-start | bytes 1572872 | tf_op jit(solution)/shard_map/ppermute | solution.py:52
  26.6 28.4 %collective-permute-start.18 = (bf16[1024,512]{1,0:T(8,128)(2,1)S(1)}, bf16[1024,512]{1,0:T(8,128)(2,1)S(1)}, u32[]{:S(2)}, u32[]{:S(2)}) collective-permute-start(bf16[1024,512]{1,0:T(8,128)(2,1)S(1)} %pad_maximum_fusion.1.refs_0_), channel_id=1, source_target_pairs={{0,1},{1,2},{2,3},{3,0},{4,7},{5,4},{6,5},{7,6},{8,9},{9,10},{10,1... | collective-permute-start | bytes 3145736 | tf_op jit(solution)/shard_map/ppermute | solution.py:52
  27.8 21.5 %collective-permute-start.29 = (bf16[512,512]{1,0:T(8,128)(2,1)S(1)}, bf16[512,512]{1,0:T(8,128)(2,1)S(1)}, u32[]{:S(2)}, u32[]{:S(2)}) collective-permute-start(bf16[512,512]{1,0:T(8,128)(2,1)S(1)} %collective-permute-done.25.refs_8_), channel_id=1, source_target_pairs={{0,8},{1,9},{2,10},{3,11},{4,76},{5,77},{6,78},{7,79},{8,64},{9,65... | collective-permute-start | bytes 1572872 | tf_op jit(solution)/shard_map/ppermute | solution.py:52
  28.0 21.3 %collective-permute-start.26 = (bf16[512,512]{1,0:T(8,128)(2,1)S(1)}, bf16[512,512]{1,0:T(8,128)(2,1)S(1)}, u32[]{:S(2)}, u32[]{:S(2)}) collective-permute-start(bf16[512,512]{1,0:T(8,128)(2,1)S(1)} %collective-permute-done.25.refs_8_), channel_id=1, source_target_pairs={{0,16},{1,17},{2,18},{3,19},{4,52},{5,53},{6,54},{7,55},{8,24},{9,... | collective-permute-start | bytes 1572872 | tf_op jit(solution)/shard_map/ppermute | solution.py:52
  36.0 0.8 copy-start.8
  38.2 12.5 %collective-permute-start.12 = (bf16[512,512]{1,0:T(8,128)(2,1)}, bf16[512,512]{1,0:T(8,128)(2,1)S(1)}, u32[]{:S(2)}, u32[]{:S(2)}) collective-permute-start(bf16[512,512]{1,0:T(8,128)(2,1)} %collective-permute-done.8.refs_8_), channel_id=1, source_target_pairs={{0,8},{1,9},{2,10},{3,11},{4,76},{5,77},{6,78},{7,79},{8,64},{9,65... | collective-permute-start | bytes 1572872 | tf_op jit(solution)/shard_map/ppermute | solution.py:52
  49.3 11.1 %collective-permute-start.21 = (bf16[1024,512]{1,0:T(8,128)(2,1)S(1)}, bf16[1024,512]{1,0:T(8,128)(2,1)S(1)}, u32[]{:S(2)}, u32[]{:S(2)}) collective-permute-start(bf16[1024,512]{1,0:T(8,128)(2,1)S(1)} %pad_maximum_fusion.1.refs_0_), channel_id=1, source_target_pairs={{0,4},{1,5},{2,6},{3,7},{4,0},{5,1},{6,2},{7,3},{8,12},{9,13},{10,... | collective-permute-start | bytes 3145736 | tf_op jit(solution)/shard_map/ppermute | solution.py:52
  49.3 8.5 %collective-permute-start.9 = (bf16[512,512]{1,0:T(8,128)(2,1)}, bf16[512,512]{1,0:T(8,128)(2,1)S(1)}, u32[]{:S(2)}, u32[]{:S(2)}) collective-permute-start(bf16[512,512]{1,0:T(8,128)(2,1)} %collective-permute-done.8.refs_8_), channel_id=1, source_target_pairs={{0,16},{1,17},{2,18},{3,19},{4,52},{5,53},{6,54},{7,55},{8,24},{9,... | collective-permute-start | bytes 1572872 | tf_op jit(solution)/shard_map/ppermute | solution.py:52
  49.3 54.1 %copy-start.12 = (bf16[512,512]{1,0:T(8,128)(2,1)}, bf16[512,512]{1,0:T(8,128)(2,1)S(1)}, u32[]{:S(2)}) copy-start(bf16[512,512]{1,0:T(8,128)(2,1)S(1)} %collective-permute-done.26.refs_9_) | copy-start | bytes 1572868
  49.4 11.1 %collective-permute-start.30 = (bf16[512,512]{1,0:T(8,128)(2,1)S(1)}, bf16[512,512]{1,0:T(8,128)(2,1)S(1)}, u32[]{:S(2)}, u32[]{:S(2)}) collective-permute-start(bf16[512,512]{1,0:T(8,128)(2,1)S(1)} %collective-permute-done.29), channel_id=1, source_target_pairs={{0,8},{1,9},{2,10},{3,11},{4,76},{5,77},{6,78},{7,79},{8,64},{9,65... | collective-permute-start | bytes 1572872 | tf_op jit(solution)/shard_map/ppermute | solution.py:52
  50.7 20.3 %collective-permute-start.1 = (bf16[1024,512]{1,0:T(8,128)(2,1)S(1)}, bf16[1024,512]{1,0:T(8,128)(2,1)}, u32[]{:S(2)}, u32[]{:S(2)}) collective-permute-start(bf16[1024,512]{1,0:T(8,128)(2,1)S(1)} %pad_maximum_fusion.refs_0_), channel_id=1, source_target_pairs={{0,1},{1,2},{2,3},{3,0},{4,7},{5,4},{6,5},{7,6},{8,9},{9,10},{10,1... | collective-permute-start | bytes 3145736 | tf_op jit(solution)/shard_map/ppermute | solution.py:52
  55.0 25.8 %collective-permute-start.19 = (bf16[1024,512]{1,0:T(8,128)(2,1)S(1)}, bf16[1024,512]{1,0:T(8,128)(2,1)}, u32[]{:S(2)}, u32[]{:S(2)}) collective-permute-start(bf16[1024,512]{1,0:T(8,128)(2,1)S(1)} %collective-permute-done.18.refs_1_), channel_id=1, source_target_pairs={{0,1},{1,2},{2,3},{3,0},{4,7},{5,4},{6,5},{7,6},{8,9},{9,10},{10,1... | collective-permute-start | bytes 3145736 | tf_op jit(solution)/shard_map/ppermute | solution.py:52
  57.9 23.5 %collective-permute-start.4 = (bf16[1024,512]{1,0:T(8,128)(2,1)S(1)}, bf16[1024,512]{1,0:T(8,128)(2,1)S(1)}, u32[]{:S(2)}, u32[]{:S(2)}) collective-permute-start(bf16[1024,512]{1,0:T(8,128)(2,1)S(1)} %pad_maximum_fusion.refs_0_), channel_id=1, source_target_pairs={{0,4},{1,5},{2,6},{3,7},{4,0},{5,1},{6,2},{7,3},{8,12},{9,13},{10,... | collective-permute-start | bytes 3145736 | tf_op jit(solution)/shard_map/ppermute | solution.py:52
  60.4 8.4 %collective-permute-start.27 = (bf16[512,512]{1,0:T(8,128)(2,1)S(1)}, bf16[512,512]{1,0:T(8,128)(2,1)S(1)}, u32[]{:S(2)}, u32[]{:S(2)}) collective-permute-start(bf16[512,512]{1,0:T(8,128)(2,1)S(1)} %collective-permute-done.26.refs_9_), channel_id=1, source_target_pairs={{0,16},{1,17},{2,18},{3,19},{4,52},{5,53},{6,54},{7,55},{8,24},{9,... | collective-permute-start | bytes 1572872 | tf_op jit(solution)/shard_map/ppermute | solution.py:52
  60.4 1.0 copy-start.2
  61.4 14.0 %collective-permute-start.13 = (bf16[512,512]{1,0:T(8,128)(2,1)S(1)}, bf16[512,512]{1,0:T(8,128)(2,1)S(1)}, u32[]{:S(2)}, u32[]{:S(2)}) collective-permute-start(bf16[512,512]{1,0:T(8,128)(2,1)S(1)} %collective-permute-done.12), channel_id=1, source_target_pairs={{0,8},{1,9},{2,10},{3,11},{4,76},{5,77},{6,78},{7,79},{8,64},{9,65... | collective-permute-start | bytes 1572872 | tf_op jit(solution)/shard_map/ppermute | solution.py:52
  68.9 13.5 %collective-permute-start.10 = (bf16[512,512]{1,0:T(8,128)(2,1)S(1)}, bf16[512,512]{1,0:T(8,128)(2,1)S(1)}, u32[]{:S(2)}, u32[]{:S(2)}) collective-permute-start(bf16[512,512]{1,0:T(8,128)(2,1)S(1)} %collective-permute-done.9.refs_9_), channel_id=1, source_target_pairs={{0,16},{1,17},{2,18},{3,19},{4,52},{5,53},{6,54},{7,55},{8,24},{9,... | collective-permute-start | bytes 1572872 | tf_op jit(solution)/shard_map/ppermute | solution.py:52
  70.1 0.8 copy-start.10
  70.9 25.6 %collective-permute-start.2 = (bf16[1024,512]{1,0:T(8,128)(2,1)}, bf16[1024,512]{1,0:T(8,128)(2,1)}, u32[]{:S(2)}, u32[]{:S(2)}) collective-permute-start(bf16[1024,512]{1,0:T(8,128)(2,1)} %collective-permute-done.1.refs_1_), channel_id=1, source_target_pairs={{0,1},{1,2},{2,3},{3,0},{4,7},{5,4},{6,5},{7,6},{8,9},{9,10},{10,1... | collective-permute-start | bytes 3145736 | tf_op jit(solution)/shard_map/ppermute | solution.py:52
  75.4 10.6 %collective-permute-start.31 = (bf16[512,512]{1,0:T(8,128)(2,1)S(1)}, bf16[512,512]{1,0:T(8,128)(2,1)S(1)}, u32[]{:S(2)}, u32[]{:S(2)}) collective-permute-start(bf16[512,512]{1,0:T(8,128)(2,1)S(1)} %collective-permute-done.30.refs_12_), channel_id=1, source_target_pairs={{0,16},{1,17},{2,18},{3,19},{4,52},{5,53},{6,54},{7,55},{8,24},{9,... | collective-permute-start | bytes 1572872 | tf_op jit(solution)/shard_map/ppermute | solution.py:52
  80.8 22.5 %collective-permute-start.20 = (bf16[1024,512]{1,0:T(8,128)(2,1)}, bf16[1024,512]{1,0:T(8,128)(2,1)}, u32[]{:S(2)}, u32[]{:S(2)}) collective-permute-start(bf16[1024,512]{1,0:T(8,128)(2,1)} %collective-permute-done.19.refs_2_), channel_id=1, source_target_pairs={{0,1},{1,2},{2,3},{3,0},{4,7},{5,4},{6,5},{7,6},{8,9},{9,10},{10,1... | collective-permute-start | bytes 3145736 | tf_op jit(solution)/shard_map/ppermute | solution.py:52
  81.4 1.0 copy-start.4
  82.4 21.1 %collective-permute-start.22 = (bf16[1024,512]{1,0:T(8,128)(2,1)S(1)}, bf16[1024,512]{1,0:T(8,128)(2,1)S(1)}, u32[]{:S(2)}, u32[]{:S(2)}) collective-permute-start(bf16[1024,512]{1,0:T(8,128)(2,1)S(1)} %collective-permute-done.18.refs_1_), channel_id=1, source_target_pairs={{0,4},{1,5},{2,6},{3,7},{4,0},{5,1},{6,2},{7,3},{8,12},{9,13},{10,... | collective-permute-start | bytes 3145736 | tf_op jit(solution)/shard_map/ppermute | solution.py:52
  82.4 24.9 %copy-start.18 = (bf16[512,512]{1,0:T(8,128)(2,1)}, bf16[512,512]{1,0:T(8,128)(2,1)S(1)}, u32[]{:S(2)}) copy-start(bf16[512,512]{1,0:T(8,128)(2,1)S(1)} %collective-permute-done.10.refs_10_) | copy-start | bytes 1572868
  82.4 9.0 %collective-permute-start.28 = (bf16[512,512]{1,0:T(8,128)(2,1)S(1)}, bf16[512,512]{1,0:T(8,128)(2,1)S(1)}, u32[]{:S(2)}, u32[]{:S(2)}) collective-permute-start(bf16[512,512]{1,0:T(8,128)(2,1)S(1)} %collective-permute-done.27.refs_10_), channel_id=1, source_target_pairs={{0,16},{1,17},{2,18},{3,19},{4,52},{5,53},{6,54},{7,55},{8,24},{9,... | collective-permute-start | bytes 1572872 | tf_op jit(solution)/shard_map/ppermute | solution.py:52
  85.3 0.8 copy-start.20
  86.1 12.5 %collective-permute-start.14 = (bf16[512,512]{1,0:T(8,128)(2,1)S(1)}, bf16[512,512]{1,0:T(8,128)(2,1)S(1)}, u32[]{:S(2)}, u32[]{:S(2)}) collective-permute-start(bf16[512,512]{1,0:T(8,128)(2,1)S(1)} %collective-permute-done.13.refs_12_), channel_id=1, source_target_pairs={{0,16},{1,17},{2,18},{3,19},{4,52},{5,53},{6,54},{7,55},{8,24},{9,... | collective-permute-start | bytes 1572872 | tf_op jit(solution)/shard_map/ppermute | solution.py:52
  91.4 0.8 copy-start.26
  92.2 15.9 %collective-permute-start.32 = (bf16[512,512]{1,0:T(8,128)(2,1)S(1)}, bf16[512,512]{1,0:T(8,128)(2,1)S(1)}, u32[]{:S(2)}, u32[]{:S(2)}) collective-permute-start(bf16[512,512]{1,0:T(8,128)(2,1)S(1)} %collective-permute-done.31.refs_13_), channel_id=1, source_target_pairs={{0,16},{1,17},{2,18},{3,19},{4,52},{5,53},{6,54},{7,55},{8,24},{9,... | collective-permute-start | bytes 1572872 | tf_op jit(solution)/shard_map/ppermute | solution.py:52
  96.5 25.1 %collective-permute-start.3 = (bf16[1024,512]{1,0:T(8,128)(2,1)}, bf16[1024,512]{1,0:T(8,128)(2,1)}, u32[]{:S(2)}, u32[]{:S(2)}) collective-permute-start(bf16[1024,512]{1,0:T(8,128)(2,1)} %collective-permute-done.2.refs_2_), channel_id=1, source_target_pairs={{0,1},{1,2},{2,3},{3,0},{4,7},{5,4},{6,5},{7,6},{8,9},{9,10},{10,1... | collective-permute-start | bytes 3145736 | tf_op jit(solution)/shard_map/ppermute | solution.py:52
  98.6 23.1 %collective-permute-start.23 = (bf16[1024,512]{1,0:T(8,128)(2,1)}, bf16[1024,512]{1,0:T(8,128)(2,1)}, u32[]{:S(2)}, u32[]{:S(2)}) collective-permute-start(bf16[1024,512]{1,0:T(8,128)(2,1)} %collective-permute-done.19.refs_2_), channel_id=1, source_target_pairs={{0,4},{1,5},{2,6},{3,7},{4,0},{5,1},{6,2},{7,3},{8,12},{9,13},{10,... | collective-permute-start | bytes 3145736 | tf_op jit(solution)/shard_map/ppermute | solution.py:52
  103.3 20.3 %collective-permute-start.24 = (bf16[1024,512]{1,0:T(8,128)(2,1)}, bf16[1024,512]{1,0:T(8,128)(2,1)}, u32[]{:S(2)}, u32[]{:S(2)}) collective-permute-start(bf16[1024,512]{1,0:T(8,128)(2,1)} %collective-permute-done.20.refs_3_), channel_id=1, source_target_pairs={{0,4},{1,5},{2,6},{3,7},{4,0},{5,1},{6,2},{7,3},{8,12},{9,13},{10,... | collective-permute-start | bytes 3145736 | tf_op jit(solution)/shard_map/ppermute | solution.py:52
  103.4 1.0 copy-start.6
  104.4 9.0 %collective-permute-start.15 = (bf16[512,512]{1,0:T(8,128)(2,1)S(1)}, bf16[512,512]{1,0:T(8,128)(2,1)S(1)}, u32[]{:S(2)}, u32[]{:S(2)}) collective-permute-start(bf16[512,512]{1,0:T(8,128)(2,1)S(1)} %collective-permute-done.14.refs_13_), channel_id=1, source_target_pairs={{0,16},{1,17},{2,18},{3,19},{4,52},{5,53},{6,54},{7,55},{8,24},{9,... | collective-permute-start | bytes 1572872 | tf_op jit(solution)/shard_map/ppermute | solution.py:52
  108.1 10.9 %collective-permute-start.33 = (bf16[512,512]{1,0:T(8,128)(2,1)S(1)}, bf16[512,512]{1,0:T(8,128)(2,1)S(1)}, u32[]{:S(2)}, u32[]{:S(2)}) collective-permute-start(bf16[512,512]{1,0:T(8,128)(2,1)S(1)} %collective-permute-done.32.refs_14_), channel_id=1, source_target_pairs={{0,16},{1,17},{2,18},{3,19},{4,52},{5,53},{6,54},{7,55},{8,24},{9,... | collective-permute-start | bytes 1572872 | tf_op jit(solution)/shard_map/ppermute | solution.py:52
  113.4 0.8 copy-start.28
  114.2 38.3 %collective-permute-start.5 = (bf16[1024,512]{1,0:T(8,128)(2,1)}, bf16[1024,512]{1,0:T(8,128)(2,1)}, u32[]{:S(2)}, u32[]{:S(2)}) collective-permute-start(bf16[1024,512]{1,0:T(8,128)(2,1)} %collective-permute-done.1.refs_1_), channel_id=1, source_target_pairs={{0,4},{1,5},{2,6},{3,7},{4,0},{5,1},{6,2},{7,3},{8,12},{9,13},{10,... | collective-permute-start | bytes 3145736 | tf_op jit(solution)/shard_map/ppermute | solution.py:52
  119.0 0.8 copy-start.32
  119.8 32.7 %collective-permute-start.6 = (bf16[1024,512]{1,0:T(8,128)(2,1)}, bf16[1024,512]{1,0:T(8,128)(2,1)}, u32[]{:S(2)}, u32[]{:S(2)}) collective-permute-start(bf16[1024,512]{1,0:T(8,128)(2,1)} %collective-permute-done.2.refs_2_), channel_id=1, source_target_pairs={{0,4},{1,5},{2,6},{3,7},{4,0},{5,1},{6,2},{7,3},{8,12},{9,13},{10,... | collective-permute-start | bytes 3145736 | tf_op jit(solution)/shard_map/ppermute | solution.py:52
  121.6 30.9 %collective-permute-start.7 = (bf16[1024,512]{1,0:T(8,128)(2,1)}, bf16[1024,512]{1,0:T(8,128)(2,1)}, u32[]{:S(2)}, u32[]{:S(2)}) collective-permute-start(bf16[1024,512]{1,0:T(8,128)(2,1)} %collective-permute-done.3.refs_3_), channel_id=1, source_target_pairs={{0,4},{1,5},{2,6},{3,7},{4,0},{5,1},{6,2},{7,3},{8,12},{9,13},{10,... | collective-permute-start | bytes 3145736 | tf_op jit(solution)/shard_map/ppermute | solution.py:52
  121.7 30.8 %collective-permute-start.11 = (bf16[512,512]{1,0:T(8,128)(2,1)}, bf16[512,512]{1,0:T(8,128)(2,1)S(1)}, u32[]{:S(2)}, u32[]{:S(2)}) collective-permute-start(bf16[512,512]{1,0:T(8,128)(2,1)} %copy-done.18), channel_id=1, source_target_pairs={{0,16},{1,17},{2,18},{3,19},{4,52},{5,53},{6,54},{7,55},{8,24},{9,... | collective-permute-start | bytes 1572872 | tf_op jit(solution)/shard_map/ppermute | solution.py:52
  123.6 29.0 %collective-permute-start.16 = (bf16[512,512]{1,0:T(8,128)(2,1)}, bf16[512,512]{1,0:T(8,128)(2,1)S(1)}, u32[]{:S(2)}, u32[]{:S(2)}) collective-permute-start(bf16[512,512]{1,0:T(8,128)(2,1)} %copy-done.28), channel_id=1, source_target_pairs={{0,16},{1,17},{2,18},{3,19},{4,52},{5,53},{6,54},{7,55},{8,24},{9,... | collective-permute-start | bytes 1572872 | tf_op jit(solution)/shard_map/ppermute | solution.py:52
  123.8 2.2 %copy-start = (bf16[2048,1024]{1,0:T(8,128)(2,1)S(1)}, bf16[2048,1024]{1,0:T(8,128)(2,1)}, u32[]{:S(2)}) copy-start(bf16[2048,1024]{1,0:T(8,128)(2,1)} %refs_16_.3) | copy-start | bytes 12582916
  126.0 1.2 copy-start.3
  127.3 1.2 copy-start.7
  128.5 1.0 copy-start.9
  129.5 1.0 copy-start.13
  130.6 1.0 copy-start.15
  131.6 1.0 copy-start.21
  132.6 1.0 copy-start.25
  133.7 1.0 copy-start.27
  134.7 1.0 copy-start.31
  135.8 1.0 copy-start.33
  136.8 15.7 %copy-start.1 = (bf16[2048,1024]{1,0:T(8,128)(2,1)S(1)}, bf16[2048,1024]{1,0:T(8,128)(2,1)}, u32[]{:S(2)}) copy-start(bf16[2048,1024]{1,0:T(8,128)(2,1)} %refs_16_.2) | copy-start | bytes 12582916
  136.8 15.7 %copy-start.5 = (bf16[1024,512]{1,0:T(8,128)(2,1)S(1)}, bf16[1024,512]{1,0:T(8,128)(2,1)}, u32[]{:S(2)}) copy-start(bf16[1024,512]{1,0:T(8,128)(2,1)} %copy-done.4) | copy-start | bytes 3145732
  136.8 15.8 %copy-start.11 = (bf16[512,512]{1,0:T(8,128)(2,1)S(1)}, bf16[512,512]{1,0:T(8,128)(2,1)}, u32[]{:S(2)}) copy-start(bf16[512,512]{1,0:T(8,128)(2,1)} %copy-done.10) | copy-start | bytes 1572868
  136.8 15.8 %copy-start.17 = (bf16[512,512]{1,0:T(8,128)(2,1)S(1)}, bf16[512,512]{1,0:T(8,128)(2,1)}, u32[]{:S(2)}) copy-start(bf16[512,512]{1,0:T(8,128)(2,1)} %copy-done.16) | copy-start | bytes 1572868
  136.8 15.8 %copy-start.19 = (bf16[512,512]{1,0:T(8,128)(2,1)S(1)}, bf16[512,512]{1,0:T(8,128)(2,1)}, u32[]{:S(2)}) copy-start(bf16[512,512]{1,0:T(8,128)(2,1)} %copy-done.18) | copy-start | bytes 1572868
  136.8 15.8 %copy-start.23 = (bf16[512,512]{1,0:T(8,128)(2,1)S(1)}, bf16[512,512]{1,0:T(8,128)(2,1)}, u32[]{:S(2)}) copy-start(bf16[512,512]{1,0:T(8,128)(2,1)} %copy-done.22) | copy-start | bytes 1572868
  136.8 15.8 %copy-start.29 = (bf16[512,512]{1,0:T(8,128)(2,1)S(1)}, bf16[512,512]{1,0:T(8,128)(2,1)}, u32[]{:S(2)}) copy-start(bf16[512,512]{1,0:T(8,128)(2,1)} %copy-done.28) | copy-start | bytes 1572868
  (5 other events, 4.0 us)

commit v2 on v1

v2 whole, which is shorter than its diff:
```python
import functools

import jax
import jax.numpy as jnp
from jax import lax
from jax.experimental import pallas as pl
from jax.experimental.pallas import tpu as pltpu
from jax.sharding import Mesh, PartitionSpec as P

decay_rate = 0.5
AXES = ("yh", "x", "yl", "core", "z")
SIZES = (2, 4, 2, 2, 4)
PIECE = 512


AT = (0, -1, -2, -3)


def index(yh, x, yl, core, z):
    return (((yh % 2 * 4 + x % 4) * 2 + yl % 2) * 2 + core % 2) * 4 + z % 4


def permutation(move):
    every = [
        (yh, x, yl, core, z)
        for yh in range(2)
        for x in range(4)
        for yl in range(2)
        for core in range(2)
        for z in range(4)
    ]
    return [(index(*place), index(*move(*place))) for place in every]


def along_x(yh, x, yl, core, z):
    return x + z - 2 * (x % 2) - yl + 2 + 2 * core


def scatter_move(yh, x, yl, core, z):
    return core, along_x(yh, x, yl, core, z), yh, x // 2, 2 * (x % 2) + yl


SCATTER = permutation(scatter_move)
BACK_X = permutation(lambda yh, x, yl, core, z: (yh, x - 1 + 2 * core, yl, core, z))
BACK_Z = permutation(lambda yh, x, yl, core, z: (yh, x, yl, core, z - 1 + 2 * core))
RING_X = permutation(lambda yh, x, yl, core, z: (yh, x + 1 - 2 * core, yl, core, z))
RING_Z = permutation(lambda yh, x, yl, core, z: (yh, x, yl, core, z + 1 - 2 * core))
ACROSS_Y = permutation(lambda yh, x, yl, core, z: (1 - yh, x, yl, core, z))
SWAP_YL = permutation(lambda yh, x, yl, core, z: (yh, x, 1 - yl, core, z))
SWAP_CORE = permutation(lambda yh, x, yl, core, z: (yh, x, yl, 1 - core, z))


def send(block, moves):
    return lax.ppermute(block, AXES, moves)


def update_kernel(tokens, factor_at, groups, halves, place, *refs):
    n_left, n_right = 4 * len(groups), 4 * len(halves)
    left_refs, right_refs = refs[:n_left], refs[n_left : n_left + n_right]
    factor_ref, out_ref, left, right, left_sems, right_sems = refs[-6:]
    yh, x, yl, core, z = (place[i] for i in range(5))
    step = pl.program_id(0)
    toward = 1 - 2 * core

    def right_copy(j, s):
        half = lax.rem(yh + halves[j], 2)
        source = x + AT[s] * toward
        token = source - 2 * core - z // 2 + z + 2 + 2 * half
        column = 0 if len(halves) == 1 else pl.multiple_of(half * PIECE, PIECE)
        row = pl.multiple_of(lax.rem(token + 8, 4) * PIECE, PIECE)
        return pltpu.make_async_copy(
            right_refs[4 * j + s],
            right.at[pl.ds(row, PIECE), pl.ds(column, PIECE)],
            right_sems.at[4 * j + s],
        )

    def left_copy(g, s):
        held_by = lax.rem(core + groups[g] // 2, 2)
        token = lax.rem(z + AT[s] * (1 - 2 * held_by) + 4, 4)
        return pltpu.make_async_copy(
            left_refs[4 * g + s].at[groups[g] % 2],
            left.at[g, pl.ds(pl.multiple_of(token * PIECE, PIECE), PIECE), :],
            left_sems.at[4 * g + s],
        )

    @pl.when(step == 0)
    def _():
        for s in range(4):
            for j in range(len(halves)):
                right_copy(j, s).start()
            left_copy(0, s).start()
        for s in range(4):
            for j in range(len(halves)):
                right_copy(j, s).wait()

    for g in range(len(groups)):

        @pl.when(step == g)
        def _():
            for s in range(4):
                left_copy(g, s).wait()
            if g + 1 < len(groups):
                for s in range(4):
                    left_copy(g + 1, s).start()

    product = lax.dot_general(
        left[step], right[...], (((0,), (0,)), ((), ())), preferred_element_type=jnp.float32
    )
    out_ref[...] = (
        decay_rate * factor_ref[...].astype(jnp.float32)
        + (1.0 - decay_rate) * (product / tokens)
    ).astype(out_ref.dtype)


def update(place, factor_at, groups, halves, lefts, rights, factor, out):
    rows, columns = factor.shape
    tokens = 4 * PIECE
    width = PIECE * len(halves)

    def block(step, place):
        group = groups[0] + step * (groups[1] - groups[0])
        row = 2 * lax.rem(place[2] + group % 2, 2) + lax.rem(place[3] + group // 2, 2)
        return row, 0 if len(halves) == 2 else lax.rem(place[0] + halves[0], 2)

    tile = pl.BlockSpec((PIECE, width), block)
    elsewhere = pl.BlockSpec(memory_space=pltpu.HBM)
    before = [] if out is None else [out]
    return pl.pallas_call(
        functools.partial(update_kernel, tokens, factor_at, groups, halves),
        out_shape=jax.ShapeDtypeStruct((rows, columns), factor.dtype),
        grid_spec=pltpu.PrefetchScalarGridSpec(
            num_scalar_prefetch=1,
            grid=(len(groups),),
            in_specs=[elsewhere] * (len(lefts) + len(rights) + len(before)) + [tile],
            out_specs=tile,
            scratch_shapes=[
                pltpu.VMEM((len(groups), tokens, PIECE), jnp.bfloat16),
                pltpu.VMEM((tokens, width), jnp.bfloat16),
                pltpu.SemaphoreType.DMA((len(lefts),)),
                pltpu.SemaphoreType.DMA((len(rights),)),
            ],
        ),
        input_output_aliases={1 + len(lefts) + len(rights): 0} if before else {},
        compiler_params=pltpu.CompilerParams(vmem_limit_bytes=60 * 2**20),
        cost_estimate=pl.CostEstimate(
            flops=1000,
            bytes_accessed=1000,
            transcendentals=0,
        ),
    )(place, *lefts, *rights, *before, factor)


def shards(activations, gradients, act_factor, grad_factor):
    place = jnp.stack([lax.axis_index(axis) for axis in AXES]).astype(jnp.int32)
    held = {"a": activations, "b": gradients, "fa": act_factor, "fb": grad_factor}

    def gated(name, gates):
        if not gates:
            return held[name]
        names = (name, *gates)
        held.update(zip(names, lax.optimization_barrier(tuple(held[n] for n in names))))
        return held[name]

    for name, source, how, gates in ORDER:
        if how == "join":
            held[name] = jnp.stack([held[source], gated(gates[0], ())])
        elif how in PARTS:
            f, groups, halves, before = PARTS[how]
            kinds = ["m", "m", "M", "M"]
            lefts = [held[f + kinds[g] + str(s)] for g in groups for s in range(4)]
            rights = [held[f + "rq"[j] + str(s)] for j in halves for s in range(4)]
            out = held["o" + f] if before else None
            held["o" + f] = update(place, f, groups, halves, lefts, rights, gated("f" + f, gates), out)
        else:
            held[name] = send(gated(source, gates), MOVES[how])
    return held["oa"], held["ob"]


PARTS = {
    "KA": ("a", (0, 1, 2, 3), (0, 1), False),
    "KB": ("b", (0, 1, 2, 3), (0, 1), False),
}
MOVES = {
    "z": RING_Z,
    "x": RING_X,
    "-z": BACK_Z,
    "-x": BACK_X,
    "y": ACROSS_Y,
    "l": SWAP_YL,
    "c": SWAP_CORE,
    "s": SCATTER,
}
ORDER = (
    ("ar0", "a", "s", ()),
    ("ar1", "ar0", "x", ()),
    ("aq0", "ar0", "y", ("ar1",)),
    ("ar2", "ar1", "x", ()),
    ("ar3", "ar2", "x", ()),
    ("aq1", "aq0", "x", ()),
    ("aq2", "aq1", "x", ()),
    ("aq3", "aq2", "x", ()),
    ("br0", "b", "s", ()),
    ("aY", "a", "l", ("br0",)),
    ("am0", "a", "join", ("aY",)),
    ("aM0", "am0", "c", ()),
    ("am1", "am0", "z", ()),
    ("am2", "am1", "z", ()),
    ("am3", "am2", "z", ()),
    ("aM1", "am1", "c", ()),
    ("aM2", "am2", "c", ()),
    ("aM3", "am3", "c", ()),
    ("bY", "b", "l", ()),
    ("bm0", "b", "join", ("bY",)),
    ("bM0", "bm0", "c", ()),
    ("bm1", "bm0", "z", ()),
    ("bm2", "bm1", "z", ()),
    ("bm3", "bm2", "z", ()),
    ("br1", "br0", "x", ()),
    ("bq0", "br0", "y", ("br1",)),
    ("br2", "br1", "x", ()),
    ("br3", "br2", "x", ()),
    ("bq1", "bq0", "x", ()),
    ("bq2", "bq1", "x", ()),
    ("bq3", "bq2", "x", ()),
    ("bM1", "bm1", "c", ()),
    ("bM2", "bm2", "c", ()),
    ("bM3", "bm3", "c", ()),
    ("KA", "x", "KA", ()),
    ("KB", "x", "KB", ()),
)


def solution(mesh):
    fine = Mesh(mesh.devices.reshape(SIZES), AXES)
    row, col, depth = ("yh", "x"), ("yl", "core"), "z"
    samples = P(depth, row + col)
    factor = P(row, col + (depth,))
    return jax.shard_map(
        shards,
        mesh=fine,
        in_specs=(samples, samples, factor, factor),
        out_specs=(factor, factor),
        check_vma=False,
    )
```

time: 169 us -> 149 us (0.88)
  local copies, waits for them, and re-layouts: 27.4 us -> 1.32 us
  starting transfers between devices: 52.9 us -> 67.2 us
  waiting for transfers between devices: 54.6 us -> 45.2 us
    unnamed x72 -> x46, local copies, waits for them, and re-layouts: 27.3 us -> 0.72 us
    ppermute x34 -> x32, starting transfers between devices: 52.9 us -> 67.2 us  [send(): return lax.ppermute(block, AXES, moves)]
    ppermute x34 -> x32, waiting for transfers between devices: 54.6 us -> 45.2 us  [send(): return lax.ppermute(block, AXES, moves)]
    another operation x0 -> x2, other arithmetic: none -> 2.28 us  [shards(): held[name] = jnp.stack([held[source], gated(gates[0], ())])]
  transfers between devices with their start and end apart: 34 -> 32, of which waited for: 11 -> 9; matrix products, arithmetic and copies ran while one was open for 2% -> 2% of each run, Pallas kernels for 9% -> 11%
where the time goes in v2:
time: 149 us
  starting transfers between devices  67.2 us (45%)
  waiting for transfers between devices  45.2 us (30%)
  Pallas kernels  31.6 us (21%)
  other arithmetic  2.28 us (2%)
    ppermute x32, starting transfers between devices, send(): return lax.ppermute(block, AXES, moves)  67.2 us
    ppermute x32, waiting for transfers between devices, send(): return lax.ppermute(block, AXES, moves)  45.2 us
    pallas_call x2, Pallas kernels, update(): pl.pallas_call(functools.partial(update_kernel, tokens, factor_at, groups...  31.6 us
  transfers between devices with their start and end apart: 32, of which 9 were waited for; matrix products, arithmetic and copies ran while one was open for 2% of the time, Pallas kernels for 11%

profile of v2, /device:TPU:1, one launch (start us, length us, event | category | flops | bytes accessed | tf_op | source)
XLA Modules:
  0.0 148.6 jit_solution(16435691721784612798)
XLA Ops:
  0.6 6.2 %collective-permute-start = (bf16[512,512]{1,0:T(8,128)(2,1)}, bf16[512,512]{1,0:T(8,128)(2,1)S(1)}, u32[]{:S(2)}, u32[]{:S(2)}) collective-permute-start(bf16[512,512]{1,0:T(8,128)(2,1)} %param.5), channel_id=1, source_target_pairs={{0,32},{1,48},{2,0},{3,16},{4,64},{5,80},{6,96},{7,112},{8,17},{9,... | collective-permute-start | bytes 1572872 | tf_op jit(solution)/shard_map/ppermute | solution.py:54
  6.8 3.3 %collective-permute-start.17 = (bf16[512,512]{1,0:T(8,128)(2,1)}, bf16[512,512]{1,0:T(8,128)(2,1)S(1)}, u32[]{:S(2)}, u32[]{:S(2)}) collective-permute-start(bf16[512,512]{1,0:T(8,128)(2,1)} %param.5), channel_id=1, source_target_pairs={{0,8},{1,9},{2,10},{3,11},{4,12},{5,13},{6,14},{7,15},{8,0},{9,1},... | collective-permute-start | bytes 1572872 | tf_op jit(solution)/shard_map/ppermute | solution.py:54
  10.2 3.5 %collective-permute-start.9 = (bf16[512,512]{1,0:T(8,128)(2,1)}, bf16[512,512]{1,0:T(8,128)(2,1)S(1)}, u32[]{:S(2)}, u32[]{:S(2)}) collective-permute-start(bf16[512,512]{1,0:T(8,128)(2,1)} %param.4), channel_id=1, source_target_pairs={{0,32},{1,48},{2,0},{3,16},{4,64},{5,80},{6,96},{7,112},{8,17},{9,... | collective-permute-start | bytes 1572872 | tf_op jit(solution)/shard_map/ppermute | solution.py:54
  13.6 3.8 %collective-permute-done.refs_16_ = bf16[512,512]{1,0:T(8,128)(2,1)S(1)} collective-permute-done((bf16[512,512]{1,0:T(8,128)(2,1)}, bf16[512,512]{1,0:T(8,128)(2,1)S(1)}, u32[]{:S(2)}, u32[]{:S(2)}) %collective-permute-start) | collective-permute-done | bytes 524320 | tf_op jit(solution)/shard_map/ppermute | solution.py:54
  17.4 2.6 %collective-permute-start.25 = (bf16[512,512]{1,0:T(8,128)(2,1)S(1)}, bf16[512,512]{1,0:T(8,128)(2,1)S(1)}, u32[]{:S(2)}, u32[]{:S(2)}) collective-permute-start(bf16[512,512]{1,0:T(8,128)(2,1)S(1)} %collective-permute-done.refs_16_), channel_id=1, source_target_pairs={{0,16},{1,17},{2,18},{3,19},{4,52},{5,53},{6,54},{7,55},{8,24},{9,... | collective-permute-start | bytes 1572872 | tf_op jit(solution)/shard_map/ppermute | solution.py:54
  20.0 1.4 collective-permute-start.1
  21.5 12.6 %collective-permute-done.17 = bf16[512,512]{1,0:T(8,128)(2,1)S(1)} collective-permute-done((bf16[512,512]{1,0:T(8,128)(2,1)}, bf16[512,512]{1,0:T(8,128)(2,1)S(1)}, u32[]{:S(2)}, u32[]{:S(2)}) %collective-permute-start.17) | collective-permute-done | bytes 524320 | tf_op jit(solution)/shard_map/ppermute | solution.py:54
  34.1 1.1 pad_maximum_fusion.1.refs_0_.refs_4_
  35.2 0.0 copy-start.1
  35.2 0.1 collective-permute-start.18
  35.3 0.3 collective-permute-start.21
  35.7 0.0 collective-permute-done.9.refs_16_
  35.7 3.4 %collective-permute-start.10 = (bf16[512,512]{1,0:T(8,128)(2,1)S(1)}, bf16[512,512]{1,0:T(8,128)(2,1)S(1)}, u32[]{:S(2)}, u32[]{:S(2)}) collective-permute-start(bf16[512,512]{1,0:T(8,128)(2,1)S(1)} %collective-permute-done.9.refs_16_), channel_id=1, source_target_pairs={{0,16},{1,17},{2,18},{3,19},{4,52},{5,53},{6,54},{7,55},{8,24},{9,... | collective-permute-start | bytes 1572872 | tf_op jit(solution)/shard_map/ppermute | solution.py:54
  39.1 0.0 collective-permute-done.25.refs_17_
  39.1 1.4 collective-permute-start.28
  40.5 4.9 %collective-permute-done.1 = bf16[512,512]{1,0:T(8,128)(2,1)S(1)} collective-permute-done((bf16[512,512]{1,0:T(8,128)(2,1)}, bf16[512,512]{1,0:T(8,128)(2,1)S(1)}, u32[]{:S(2)}, u32[]{:S(2)}) %collective-permute-start.1) | collective-permute-done | bytes 524320 | tf_op jit(solution)/shard_map/ppermute | solution.py:54
  45.3 1.1 pad_maximum_fusion.refs_0_.refs_4_
  46.5 0.7 collective-permute-start.2
  47.2 0.0 collective-permute-done.10.refs_17_
  47.2 2.7 %collective-permute-start.26 = (bf16[512,512]{1,0:T(8,128)(2,1)S(1)}, bf16[512,512]{1,0:T(8,128)(2,1)S(1)}, u32[]{:S(2)}, u32[]{:S(2)}) collective-permute-start(bf16[512,512]{1,0:T(8,128)(2,1)S(1)} %collective-permute-done.25.refs_17_), channel_id=1, source_target_pairs={{0,16},{1,17},{2,18},{3,19},{4,52},{5,53},{6,54},{7,55},{8,24},{9,... | collective-permute-start | bytes 1572872 | tf_op jit(solution)/shard_map/ppermute | solution.py:54
  49.9 4.4 %collective-permute-done.28.refs_20_ = bf16[512,512]{1,0:T(8,128)(2,1)S(1)} collective-permute-done((bf16[512,512]{1,0:T(8,128)(2,1)S(1)}, bf16[512,512]{1,0:T(8,128)(2,1)S(1)}, u32[]{:S(2)}, u32[]{:S(2)}) %collective-permute-start.28) | collective-permute-done | bytes 524320 | tf_op jit(solution)/shard_map/ppermute | solution.py:54
  54.3 2.6 %collective-permute-start.13 = (bf16[512,512]{1,0:T(8,128)(2,1)S(1)}, bf16[512,512]{1,0:T(8,128)(2,1)S(1)}, u32[]{:S(2)}, u32[]{:S(2)}) collective-permute-start(bf16[512,512]{1,0:T(8,128)(2,1)S(1)} %collective-permute-done.9.refs_16_), channel_id=1, source_target_pairs={{0,64},{1,65},{2,66},{3,67},{4,68},{5,69},{6,70},{7,71},{8,72},{9,... | collective-permute-start | bytes 1572872 | tf_op jit(solution)/shard_map/ppermute | solution.py:54
  57.0 0.0 collective-permute-done.18.refs_1_.refs_5_
  57.0 3.1 %collective-permute-start.19 = (bf16[2,512,512]{2,1,0:T(8,128)(2,1)S(1)}, bf16[2,512,512]{2,1,0:T(8,128)(2,1)S(1)}, u32[]{:S(2)}, u32[]{:S(2)}) collective-permute-start(bf16[2,512,512]{2,1,0:T(8,128)(2,1)S(1)} %collective-permute-done.18.refs_1_.refs_5_), channel_id=1, source_target_pairs={{0,1},{1,2},{2,3},{3,0},{4,7},{5,4},{6,5},{7,6},{8,9},{9,10},{10,1... | collective-permute-start | bytes 3145736 | tf_op jit(solution)/shard_map/ppermute | solution.py:54
  60.1 0.0 collective-permute-done.26.refs_18_
  60.1 1.4 collective-permute-start.11
  61.5 0.0 collective-permute-done.21.refs_8_.refs_12_
  61.5 0.5 collective-permute-start.29
  62.0 6.8 %collective-permute-done.13.refs_20_ = bf16[512,512]{1,0:T(8,128)(2,1)S(1)} collective-permute-done((bf16[512,512]{1,0:T(8,128)(2,1)S(1)}, bf16[512,512]{1,0:T(8,128)(2,1)S(1)}, u32[]{:S(2)}, u32[]{:S(2)}) %collective-permute-start.13) | collective-permute-done | bytes 524320 | tf_op jit(solution)/shard_map/ppermute | solution.py:54
  68.8 4.2 %collective-permute-start.27 = (bf16[512,512]{1,0:T(8,128)(2,1)S(1)}, bf16[512,512]{1,0:T(8,128)(2,1)S(1)}, u32[]{:S(2)}, u32[]{:S(2)}) collective-permute-start(bf16[512,512]{1,0:T(8,128)(2,1)S(1)} %collective-permute-done.26.refs_18_), channel_id=1, source_target_pairs={{0,16},{1,17},{2,18},{3,19},{4,52},{5,53},{6,54},{7,55},{8,24},{9,... | collective-permute-start | bytes 1572872 | tf_op jit(solution)/shard_map/ppermute | solution.py:54
  73.0 0.0 collective-permute-done.2.refs_1_.refs_5_
  73.0 2.3 %collective-permute-start.3 = (bf16[2,512,512]{2,1,0:T(8,128)(2,1)S(1)}, bf16[2,512,512]{2,1,0:T(8,128)(2,1)}, u32[]{:S(2)}, u32[]{:S(2)}) collective-permute-start(bf16[2,512,512]{2,1,0:T(8,128)(2,1)S(1)} %collective-permute-done.2.refs_1_.refs_5_), channel_id=1, source_target_pairs={{0,1},{1,2},{2,3},{3,0},{4,7},{5,4},{6,5},{7,6},{8,9},{9,10},{10,1... | collective-permute-start | bytes 3145736 | tf_op jit(solution)/shard_map/ppermute | solution.py:54
  75.3 0.0 collective-permute-done.11.refs_18_
  75.3 1.1 collective-permute-start.5
  76.4 0.0 collective-permute-done.29.refs_21_
  76.4 0.2 collective-permute-start.14
  76.6 4.8 %collective-permute-done.27.refs_19_ = bf16[512,512]{1,0:T(8,128)(2,1)S(1)} collective-permute-done((bf16[512,512]{1,0:T(8,128)(2,1)S(1)}, bf16[512,512]{1,0:T(8,128)(2,1)S(1)}, u32[]{:S(2)}, u32[]{:S(2)}) %collective-permute-start.27) | collective-permute-done | bytes 524320 | tf_op jit(solution)/shard_map/ppermute | solution.py:54
  81.4 3.7 %collective-permute-start.22 = (bf16[2,512,512]{2,1,0:T(8,128)(2,1)S(1)}, bf16[2,512,512]{2,1,0:T(8,128)(2,1)S(1)}, u32[]{:S(2)}, u32[]{:S(2)}) collective-permute-start(bf16[2,512,512]{2,1,0:T(8,128)(2,1)S(1)} %collective-permute-done.18.refs_1_.refs_5_), channel_id=1, source_target_pairs={{0,4},{1,5},{2,6},{3,7},{4,0},{5,1},{6,2},{7,3},{8,12},{9,13},{10,... | collective-permute-start | bytes 3145736 | tf_op jit(solution)/shard_map/ppermute | solution.py:54
  85.1 0.0 collective-permute-done.19.refs_2_.refs_6_
  85.1 1.1 collective-permute-start.20
  86.2 0.8 collective-permute-done.14.refs_21_
  87.0 1.2 collective-permute-start.30
  88.2 0.0 collective-permute-done.3.refs_2_.refs_6_
  88.2 2.7 %collective-permute-start.4 = (bf16[2,512,512]{2,1,0:T(8,128)(2,1)}, bf16[2,512,512]{2,1,0:T(8,128)(2,1)}, u32[]{:S(2)}, u32[]{:S(2)}) collective-permute-start(bf16[2,512,512]{2,1,0:T(8,128)(2,1)} %collective-permute-done.3.refs_2_.refs_6_), channel_id=1, source_target_pairs={{0,1},{1,2},{2,3},{3,0},{4,7},{5,4},{6,5},{7,6},{8,9},{9,10},{10,1... | collective-permute-start | bytes 3145736 | tf_op jit(solution)/shard_map/ppermute | solution.py:54
  91.0 0.1 collective-permute-start.15
  91.0 4.3 %collective-permute-done.30.refs_22_ = bf16[512,512]{1,0:T(8,128)(2,1)S(1)} collective-permute-done((bf16[512,512]{1,0:T(8,128)(2,1)S(1)}, bf16[512,512]{1,0:T(8,128)(2,1)S(1)}, u32[]{:S(2)}, u32[]{:S(2)}) %collective-permute-start.30) | collective-permute-done | bytes 524320 | tf_op jit(solution)/shard_map/ppermute | solution.py:54
  95.4 5.7 %collective-permute-start.23 = (bf16[2,512,512]{2,1,0:T(8,128)(2,1)S(1)}, bf16[2,512,512]{2,1,0:T(8,128)(2,1)S(1)}, u32[]{:S(2)}, u32[]{:S(2)}) collective-permute-start(bf16[2,512,512]{2,1,0:T(8,128)(2,1)S(1)} %collective-permute-done.19.refs_2_.refs_6_), channel_id=1, source_target_pairs={{0,4},{1,5},{2,6},{3,7},{4,0},{5,1},{6,2},{7,3},{8,12},{9,13},{10,... | collective-permute-start | bytes 3145736 | tf_op jit(solution)/shard_map/ppermute | solution.py:54
  101.1 0.0 collective-permute-start.31
  101.1 2.4 %collective-permute-start.24 = (bf16[2,512,512]{2,1,0:T(8,128)(2,1)S(1)}, bf16[2,512,512]{2,1,0:T(8,128)(2,1)S(1)}, u32[]{:S(2)}, u32[]{:S(2)}) collective-permute-start(bf16[2,512,512]{2,1,0:T(8,128)(2,1)S(1)} %collective-permute-done.20.refs_3_.refs_7_), channel_id=1, source_target_pairs={{0,4},{1,5},{2,6},{3,7},{4,0},{5,1},{6,2},{7,3},{8,12},{9,13},{10,... | collective-permute-start | bytes 3145736 | tf_op jit(solution)/shard_map/ppermute | solution.py:54
  103.5 0.0 collective-permute-done.15.refs_22_
  103.5 3.3 %collective-permute-start.6 = (bf16[2,512,512]{2,1,0:T(8,128)(2,1)S(1)}, bf16[2,512,512]{2,1,0:T(8,128)(2,1)}, u32[]{:S(2)}, u32[]{:S(2)}) collective-permute-start(bf16[2,512,512]{2,1,0:T(8,128)(2,1)S(1)} %collective-permute-done.2.refs_1_.refs_5_), channel_id=1, source_target_pairs={{0,4},{1,5},{2,6},{3,7},{4,0},{5,1},{6,2},{7,3},{8,12},{9,13},{10,... | collective-permute-start | bytes 3145736 | tf_op jit(solution)/shard_map/ppermute | solution.py:54
  106.8 2.7 %collective-permute-done.31.refs_23_ = bf16[512,512]{1,0:T(8,128)(2,1)S(1)} collective-permute-done((bf16[512,512]{1,0:T(8,128)(2,1)S(1)}, bf16[512,512]{1,0:T(8,128)(2,1)S(1)}, u32[]{:S(2)}, u32[]{:S(2)}) %collective-permute-start.31) | collective-permute-done | bytes 524320 | tf_op jit(solution)/shard_map/ppermute | solution.py:54
  109.5 2.8 %collective-permute-start.7 = (bf16[2,512,512]{2,1,0:T(8,128)(2,1)}, bf16[2,512,512]{2,1,0:T(8,128)(2,1)}, u32[]{:S(2)}, u32[]{:S(2)}) collective-permute-start(bf16[2,512,512]{2,1,0:T(8,128)(2,1)} %collective-permute-done.3.refs_2_.refs_6_), channel_id=1, source_target_pairs={{0,4},{1,5},{2,6},{3,7},{4,0},{5,1},{6,2},{7,3},{8,12},{9,13},{10,... | collective-permute-start | bytes 3145736 | tf_op jit(solution)/shard_map/ppermute | solution.py:54
  112.3 0.0 collective-permute-done.4.refs_3_.refs_7_
  112.3 2.5 %collective-permute-start.8 = (bf16[2,512,512]{2,1,0:T(8,128)(2,1)}, bf16[2,512,512]{2,1,0:T(8,128)(2,1)}, u32[]{:S(2)}, u32[]{:S(2)}) collective-permute-start(bf16[2,512,512]{2,1,0:T(8,128)(2,1)} %collective-permute-done.4.refs_3_.refs_7_), channel_id=1, source_target_pairs={{0,4},{1,5},{2,6},{3,7},{4,0},{5,1},{6,2},{7,3},{8,12},{9,13},{10,... | collective-permute-start | bytes 3145736 | tf_op jit(solution)/shard_map/ppermute | solution.py:54
  114.9 0.1 collective-permute-start.12
  115.0 0.5 collective-permute-start.16
  115.5 0.3 copy-done.9
  115.8 0.3 copy-done.10
  116.2 0.6 stack.41.place
  116.8 15.8 %shard_map.60 = bf16[2048,1024]{1,0:T(8,128)(2,1)} custom-call(s32[5]{0:T(128)} %stack.41.place, bf16[2,512,512]{2,1,0:T(8,128)(2,1)} %copy-done.1, bf16[2,512,512]{2,1,0:T(8,128)(2,1)} %copy-done.3, bf16[2,512,512]{2,1,0:T(8,128)(2,1)} %copy-done.5, bf16[2,512,512]{2,1,0:T(8,128)(2,1)} %copy-done.8, bf16[2,512,512]{2,1,0:T(8,128)(2,1)} %copy-done.1, ...), custom_call_target="tpu_custom_call" | custom-call | flops 1000 | bytes 1000 | tf_op jit(solution)/shard_map/pallas_call | solution.py:128
  132.6 0.0 collective-permute-done.12.refs_19_
  132.6 0.0 collective-permute-done.7.refs_10_.refs_14_
  132.6 15.8 %shard_map.59 = bf16[2048,1024]{1,0:T(8,128)(2,1)} custom-call(s32[5]{0:T(128)} %stack.41.place, bf16[2,512,512]{2,1,0:T(8,128)(2,1)} %copy-done, bf16[2,512,512]{2,1,0:T(8,128)(2,1)} %copy-done.2, bf16[2,512,512]{2,1,0:T(8,128)(2,1)} %collective-permute-done.3.refs_2_.refs_6_, bf16[2,512,512]{2,1,0:T(8,128)(2,1)} %collective-permute-done.4.refs_3_.refs_7_, ...), custom_call_target="tpu_custom_call" | custom-call | flops 1000 | bytes 1000 | tf_op jit(solution)/shard_map/pallas_call | solution.py:128
  (51 shorter events, 0.1 us)
Async XLA Ops:
  0.6 16.8 %collective-permute-start = (bf16[512,512]{1,0:T(8,128)(2,1)}, bf16[512,512]{1,0:T(8,128)(2,1)S(1)}, u32[]{:S(2)}, u32[]{:S(2)}) collective-permute-start(bf16[512,512]{1,0:T(8,128)(2,1)} %param.5), channel_id=1, source_target_pairs={{0,32},{1,48},{2,0},{3,16},{4,64},{5,80},{6,96},{7,112},{8,17},{9,... | collective-permute-start | bytes 1572872 | tf_op jit(solution)/shard_map/ppermute | solution.py:54
  6.8 27.2 %collective-permute-start.17 = (bf16[512,512]{1,0:T(8,128)(2,1)}, bf16[512,512]{1,0:T(8,128)(2,1)S(1)}, u32[]{:S(2)}, u32[]{:S(2)}) collective-permute-start(bf16[512,512]{1,0:T(8,128)(2,1)} %param.5), channel_id=1, source_target_pairs={{0,8},{1,9},{2,10},{3,11},{4,12},{5,13},{6,14},{7,15},{8,0},{9,1},... | collective-permute-start | bytes 1572872 | tf_op jit(solution)/shard_map/ppermute | solution.py:54
  10.2 25.5 %collective-permute-start.9 = (bf16[512,512]{1,0:T(8,128)(2,1)}, bf16[512,512]{1,0:T(8,128)(2,1)S(1)}, u32[]{:S(2)}, u32[]{:S(2)}) collective-permute-start(bf16[512,512]{1,0:T(8,128)(2,1)} %param.4), channel_id=1, source_target_pairs={{0,32},{1,48},{2,0},{3,16},{4,64},{5,80},{6,96},{7,112},{8,17},{9,... | collective-permute-start | bytes 1572872 | tf_op jit(solution)/shard_map/ppermute | solution.py:54
  17.4 98.0 %copy-start.12 = (bf16[512,512]{1,0:T(8,128)(2,1)}, bf16[512,512]{1,0:T(8,128)(2,1)S(1)}, u32[]{:S(2)}) copy-start(bf16[512,512]{1,0:T(8,128)(2,1)S(1)} %collective-permute-done.refs_16_) | copy-start | bytes 1572868
  17.4 21.6 %collective-permute-start.25 = (bf16[512,512]{1,0:T(8,128)(2,1)S(1)}, bf16[512,512]{1,0:T(8,128)(2,1)S(1)}, u32[]{:S(2)}, u32[]{:S(2)}) collective-permute-start(bf16[512,512]{1,0:T(8,128)(2,1)S(1)} %collective-permute-done.refs_16_), channel_id=1, source_target_pairs={{0,16},{1,17},{2,18},{3,19},{4,52},{5,53},{6,54},{7,55},{8,24},{9,... | collective-permute-start | bytes 1572872 | tf_op jit(solution)/shard_map/ppermute | solution.py:54
  20.0 25.3 %collective-permute-start.1 = (bf16[512,512]{1,0:T(8,128)(2,1)}, bf16[512,512]{1,0:T(8,128)(2,1)S(1)}, u32[]{:S(2)}, u32[]{:S(2)}) collective-permute-start(bf16[512,512]{1,0:T(8,128)(2,1)} %param.4), channel_id=1, source_target_pairs={{0,8},{1,9},{2,10},{3,11},{4,12},{5,13},{6,14},{7,15},{8,0},{9,1},... | collective-permute-start | bytes 1572872 | tf_op jit(solution)/shard_map/ppermute | solution.py:54
  35.2 81.5 %copy-start.1 = (bf16[2,512,512]{2,1,0:T(8,128)(2,1)}, bf16[2,512,512]{2,1,0:T(8,128)(2,1)S(1)}, u32[]{:S(2)}) copy-start(bf16[2,512,512]{2,1,0:T(8,128)(2,1)S(1)} %pad_maximum_fusion.1.refs_0_.refs_4_) | copy-start | bytes 3145732
  35.2 21.7 %collective-permute-start.18 = (bf16[2,512,512]{2,1,0:T(8,128)(2,1)S(1)}, bf16[2,512,512]{2,1,0:T(8,128)(2,1)S(1)}, u32[]{:S(2)}, u32[]{:S(2)}) collective-permute-start(bf16[2,512,512]{2,1,0:T(8,128)(2,1)S(1)} %pad_maximum_fusion.1.refs_0_.refs_4_), channel_id=1, source_target_pairs={{0,1},{1,2},{2,3},{3,0},{4,7},{5,4},{6,5},{7,6},{8,9},{9,10},{10,1... | collective-permute-start | bytes 3145736 | tf_op jit(solution)/shard_map/ppermute | solution.py:54
  35.3 26.1 %collective-permute-start.21 = (bf16[2,512,512]{2,1,0:T(8,128)(2,1)S(1)}, bf16[2,512,512]{2,1,0:T(8,128)(2,1)S(1)}, u32[]{:S(2)}, u32[]{:S(2)}) collective-permute-start(bf16[2,512,512]{2,1,0:T(8,128)(2,1)S(1)} %pad_maximum_fusion.1.refs_0_.refs_4_), channel_id=1, source_target_pairs={{0,4},{1,5},{2,6},{3,7},{4,0},{5,1},{6,2},{7,3},{8,12},{9,13},{10,... | collective-permute-start | bytes 3145736 | tf_op jit(solution)/shard_map/ppermute | solution.py:54
  35.7 79.8 %copy-start.11 = (bf16[512,512]{1,0:T(8,128)(2,1)}, bf16[512,512]{1,0:T(8,128)(2,1)S(1)}, u32[]{:S(2)}) copy-start(bf16[512,512]{1,0:T(8,128)(2,1)S(1)} %collective-permute-done.9.refs_16_) | copy-start | bytes 1572868
  35.7 11.5 %collective-permute-start.10 = (bf16[512,512]{1,0:T(8,128)(2,1)S(1)}, bf16[512,512]{1,0:T(8,128)(2,1)S(1)}, u32[]{:S(2)}, u32[]{:S(2)}) collective-permute-start(bf16[512,512]{1,0:T(8,128)(2,1)S(1)} %collective-permute-done.9.refs_16_), channel_id=1, source_target_pairs={{0,16},{1,17},{2,18},{3,19},{4,52},{5,53},{6,54},{7,55},{8,24},{9,... | collective-permute-start | bytes 1572872 | tf_op jit(solution)/shard_map/ppermute | solution.py:54
  39.1 76.4 %copy-start.14 = (bf16[512,512]{1,0:T(8,128)(2,1)}, bf16[512,512]{1,0:T(8,128)(2,1)S(1)}, u32[]{:S(2)}) copy-start(bf16[512,512]{1,0:T(8,128)(2,1)S(1)} %collective-permute-done.25.refs_17_) | copy-start | bytes 1572868
  39.1 15.3 %collective-permute-start.28 = (bf16[512,512]{1,0:T(8,128)(2,1)S(1)}, bf16[512,512]{1,0:T(8,128)(2,1)S(1)}, u32[]{:S(2)}, u32[]{:S(2)}) collective-permute-start(bf16[512,512]{1,0:T(8,128)(2,1)S(1)} %collective-permute-done.refs_16_), channel_id=1, source_target_pairs={{0,64},{1,65},{2,66},{3,67},{4,68},{5,69},{6,70},{7,71},{8,72},{9,... | collective-permute-start | bytes 1572872 | tf_op jit(solution)/shard_map/ppermute | solution.py:54
  46.5 86.1 %copy-start = (bf16[2,512,512]{2,1,0:T(8,128)(2,1)}, bf16[2,512,512]{2,1,0:T(8,128)(2,1)S(1)}, u32[]{:S(2)}) copy-start(bf16[2,512,512]{2,1,0:T(8,128)(2,1)S(1)} %pad_maximum_fusion.refs_0_.refs_4_) | copy-start | bytes 3145732
  46.5 26.5 %collective-permute-start.2 = (bf16[2,512,512]{2,1,0:T(8,128)(2,1)S(1)}, bf16[2,512,512]{2,1,0:T(8,128)(2,1)S(1)}, u32[]{:S(2)}, u32[]{:S(2)}) collective-permute-start(bf16[2,512,512]{2,1,0:T(8,128)(2,1)S(1)} %pad_maximum_fusion.refs_0_.refs_4_), channel_id=1, source_target_pairs={{0,1},{1,2},{2,3},{3,0},{4,7},{5,4},{6,5},{7,6},{8,9},{9,10},{10,1... | collective-permute-start | bytes 3145736 | tf_op jit(solution)/shard_map/ppermute | solution.py:54
  47.2 68.3 %copy-start.13 = (bf16[512,512]{1,0:T(8,128)(2,1)}, bf16[512,512]{1,0:T(8,128)(2,1)S(1)}, u32[]{:S(2)}) copy-start(bf16[512,512]{1,0:T(8,128)(2,1)S(1)} %collective-permute-done.10.refs_17_) | copy-start | bytes 1572868
  47.2 12.9 %collective-permute-start.26 = (bf16[512,512]{1,0:T(8,128)(2,1)S(1)}, bf16[512,512]{1,0:T(8,128)(2,1)S(1)}, u32[]{:S(2)}, u32[]{:S(2)}) collective-permute-start(bf16[512,512]{1,0:T(8,128)(2,1)S(1)} %collective-permute-done.25.refs_17_), channel_id=1, source_target_pairs={{0,16},{1,17},{2,18},{3,19},{4,52},{5,53},{6,54},{7,55},{8,24},{9,... | collective-permute-start | bytes 1572872 | tf_op jit(solution)/shard_map/ppermute | solution.py:54
  54.3 61.2 %copy-start.16 = (bf16[512,512]{1,0:T(8,128)(2,1)}, bf16[512,512]{1,0:T(8,128)(2,1)S(1)}, u32[]{:S(2)}) copy-start(bf16[512,512]{1,0:T(8,128)(2,1)S(1)} %collective-permute-done.28.refs_20_) | copy-start | bytes 1572868
  54.3 14.4 %collective-permute-start.13 = (bf16[512,512]{1,0:T(8,128)(2,1)S(1)}, bf16[512,512]{1,0:T(8,128)(2,1)S(1)}, u32[]{:S(2)}, u32[]{:S(2)}) collective-permute-start(bf16[512,512]{1,0:T(8,128)(2,1)S(1)} %collective-permute-done.9.refs_16_), channel_id=1, source_target_pairs={{0,64},{1,65},{2,66},{3,67},{4,68},{5,69},{6,70},{7,71},{8,72},{9,... | collective-permute-start | bytes 1572872 | tf_op jit(solution)/shard_map/ppermute | solution.py:54
  57.0 46.6 %copy-start.3 = (bf16[2,512,512]{2,1,0:T(8,128)(2,1)}, bf16[2,512,512]{2,1,0:T(8,128)(2,1)S(1)}, u32[]{:S(2)}) copy-start(bf16[2,512,512]{2,1,0:T(8,128)(2,1)S(1)} %collective-permute-done.18.refs_1_.refs_5_) | copy-start | bytes 3145732
  57.0 28.1 %collective-permute-start.19 = (bf16[2,512,512]{2,1,0:T(8,128)(2,1)S(1)}, bf16[2,512,512]{2,1,0:T(8,128)(2,1)S(1)}, u32[]{:S(2)}, u32[]{:S(2)}) collective-permute-start(bf16[2,512,512]{2,1,0:T(8,128)(2,1)S(1)} %collective-permute-done.18.refs_1_.refs_5_), channel_id=1, source_target_pairs={{0,1},{1,2},{2,3},{3,0},{4,7},{5,4},{6,5},{7,6},{8,9},{9,10},{10,1... | collective-permute-start | bytes 3145736 | tf_op jit(solution)/shard_map/ppermute | solution.py:54
  60.1 16.5 %copy-start.17 = (bf16[512,512]{1,0:T(8,128)(2,1)}, bf16[512,512]{1,0:T(8,128)(2,1)S(1)}, u32[]{:S(2)}) copy-start(bf16[512,512]{1,0:T(8,128)(2,1)S(1)} %collective-permute-done.26.refs_18_) | copy-start | bytes 1572868
  60.1 15.2 %collective-permute-start.11 = (bf16[512,512]{1,0:T(8,128)(2,1)S(1)}, bf16[512,512]{1,0:T(8,128)(2,1)}, u32[]{:S(2)}, u32[]{:S(2)}) collective-permute-start(bf16[512,512]{1,0:T(8,128)(2,1)S(1)} %collective-permute-done.10.refs_17_), channel_id=1, source_target_pairs={{0,16},{1,17},{2,18},{3,19},{4,52},{5,53},{6,54},{7,55},{8,24},{9,... | collective-permute-start | bytes 1572872 | tf_op jit(solution)/shard_map/ppermute | solution.py:54
  61.5 42.1 %copy-start.4 = (bf16[2,512,512]{2,1,0:T(8,128)(2,1)}, bf16[2,512,512]{2,1,0:T(8,128)(2,1)S(1)}, u32[]{:S(2)}) copy-start(bf16[2,512,512]{2,1,0:T(8,128)(2,1)S(1)} %collective-permute-done.21.refs_8_.refs_12_) | copy-start | bytes 3145732
  61.5 14.9 %collective-permute-start.29 = (bf16[512,512]{1,0:T(8,128)(2,1)S(1)}, bf16[512,512]{1,0:T(8,128)(2,1)S(1)}, u32[]{:S(2)}, u32[]{:S(2)}) collective-permute-start(bf16[512,512]{1,0:T(8,128)(2,1)S(1)} %collective-permute-done.28.refs_20_), channel_id=1, source_target_pairs={{0,16},{1,17},{2,18},{3,19},{4,52},{5,53},{6,54},{7,55},{8,24},{9,... | collective-permute-start | bytes 1572872 | tf_op jit(solution)/shard_map/ppermute | solution.py:54
  68.7 22.3 %copy-start.15 = (bf16[512,512]{1,0:T(8,128)(2,1)}, bf16[512,512]{1,0:T(8,128)(2,1)S(1)}, u32[]{:S(2)}) copy-start(bf16[512,512]{1,0:T(8,128)(2,1)S(1)} %collective-permute-done.13.refs_20_) | copy-start | bytes 1572868
  68.8 12.7 %collective-permute-start.27 = (bf16[512,512]{1,0:T(8,128)(2,1)S(1)}, bf16[512,512]{1,0:T(8,128)(2,1)S(1)}, u32[]{:S(2)}, u32[]{:S(2)}) collective-permute-start(bf16[512,512]{1,0:T(8,128)(2,1)S(1)} %collective-permute-done.26.refs_18_), channel_id=1, source_target_pairs={{0,16},{1,17},{2,18},{3,19},{4,52},{5,53},{6,54},{7,55},{8,24},{9,... | collective-permute-start | bytes 1572872 | tf_op jit(solution)/shard_map/ppermute | solution.py:54
  73.0 59.6 %copy-start.2 = (bf16[2,512,512]{2,1,0:T(8,128)(2,1)}, bf16[2,512,512]{2,1,0:T(8,128)(2,1)S(1)}, u32[]{:S(2)}) copy-start(bf16[2,512,512]{2,1,0:T(8,128)(2,1)S(1)} %collective-permute-done.2.refs_1_.refs_5_) | copy-start | bytes 3145732
  73.0 15.3 %collective-permute-start.3 = (bf16[2,512,512]{2,1,0:T(8,128)(2,1)S(1)}, bf16[2,512,512]{2,1,0:T(8,128)(2,1)}, u32[]{:S(2)}, u32[]{:S(2)}) collective-permute-start(bf16[2,512,512]{2,1,0:T(8,128)(2,1)S(1)} %collective-permute-done.2.refs_1_.refs_5_), channel_id=1, source_target_pairs={{0,1},{1,2},{2,3},{3,0},{4,7},{5,4},{6,5},{7,6},{8,9},{9,10},{10,1... | collective-permute-start | bytes 3145736 | tf_op jit(solution)/shard_map/ppermute | solution.py:54
  75.3 15.6 %collective-permute-start.5 = (bf16[2,512,512]{2,1,0:T(8,128)(2,1)S(1)}, bf16[2,512,512]{2,1,0:T(8,128)(2,1)S(1)}, u32[]{:S(2)}, u32[]{:S(2)}) collective-permute-start(bf16[2,512,512]{2,1,0:T(8,128)(2,1)S(1)} %pad_maximum_fusion.refs_0_.refs_4_), channel_id=1, source_target_pairs={{0,4},{1,5},{2,6},{3,7},{4,0},{5,1},{6,2},{7,3},{8,12},{9,13},{10,... | collective-permute-start | bytes 3145736 | tf_op jit(solution)/shard_map/ppermute | solution.py:54
  76.4 14.7 %copy-start.19 = (bf16[512,512]{1,0:T(8,128)(2,1)}, bf16[512,512]{1,0:T(8,128)(2,1)S(1)}, u32[]{:S(2)}) copy-start(bf16[512,512]{1,0:T(8,128)(2,1)S(1)} %collective-permute-done.29.refs_21_) | copy-start | bytes 1572868
  76.4 10.7 %collective-permute-start.14 = (bf16[512,512]{1,0:T(8,128)(2,1)S(1)}, bf16[512,512]{1,0:T(8,128)(2,1)S(1)}, u32[]{:S(2)}, u32[]{:S(2)}) collective-permute-start(bf16[512,512]{1,0:T(8,128)(2,1)S(1)} %collective-permute-done.13.refs_20_), channel_id=1, source_target_pairs={{0,16},{1,17},{2,18},{3,19},{4,52},{5,53},{6,54},{7,55},{8,24},{9,... | collective-permute-start | bytes 1572872 | tf_op jit(solution)/shard_map/ppermute | solution.py:54
  81.4 19.7 %copy-start.20 = (bf16[512,512]{1,0:T(8,128)(2,1)}, bf16[512,512]{1,0:T(8,128)(2,1)S(1)}, u32[]{:S(2)}) copy-start(bf16[512,512]{1,0:T(8,128)(2,1)S(1)} %collective-permute-done.27.refs_19_) | copy-start | bytes 1572868
  81.4 19.7 %collective-permute-start.22 = (bf16[2,512,512]{2,1,0:T(8,128)(2,1)S(1)}, bf16[2,512,512]{2,1,0:T(8,128)(2,1)S(1)}, u32[]{:S(2)}, u32[]{:S(2)}) collective-permute-start(bf16[2,512,512]{2,1,0:T(8,128)(2,1)S(1)} %collective-permute-done.18.refs_1_.refs_5_), channel_id=1, source_target_pairs={{0,4},{1,5},{2,6},{3,7},{4,0},{5,1},{6,2},{7,3},{8,12},{9,13},{10,... | collective-permute-start | bytes 3145736 | tf_op jit(solution)/shard_map/ppermute | solution.py:54
  85.1 21.7 %copy-start.5 = (bf16[2,512,512]{2,1,0:T(8,128)(2,1)}, bf16[2,512,512]{2,1,0:T(8,128)(2,1)S(1)}, u32[]{:S(2)}) copy-start(bf16[2,512,512]{2,1,0:T(8,128)(2,1)S(1)} %collective-permute-done.19.refs_2_.refs_6_) | copy-start | bytes 3145732
  85.1 16.0 %collective-permute-start.20 = (bf16[2,512,512]{2,1,0:T(8,128)(2,1)S(1)}, bf16[2,512,512]{2,1,0:T(8,128)(2,1)S(1)}, u32[]{:S(2)}, u32[]{:S(2)}) collective-permute-start(bf16[2,512,512]{2,1,0:T(8,128)(2,1)S(1)} %collective-permute-done.19.refs_2_.refs_6_), channel_id=1, source_target_pairs={{0,1},{1,2},{2,3},{3,0},{4,7},{5,4},{6,5},{7,6},{8,9},{9,10},{10,1... | collective-permute-start | bytes 3145736 | tf_op jit(solution)/shard_map/ppermute | solution.py:54
  87.0 28.5 %copy-start.18 = (bf16[512,512]{1,0:T(8,128)(2,1)}, bf16[512,512]{1,0:T(8,128)(2,1)S(1)}, u32[]{:S(2)}) copy-start(bf16[512,512]{1,0:T(8,128)(2,1)S(1)} %collective-permute-done.14.refs_21_) | copy-start | bytes 1572868
  87.0 8.3 %collective-permute-start.30 = (bf16[512,512]{1,0:T(8,128)(2,1)S(1)}, bf16[512,512]{1,0:T(8,128)(2,1)S(1)}, u32[]{:S(2)}, u32[]{:S(2)}) collective-permute-start(bf16[512,512]{1,0:T(8,128)(2,1)S(1)} %collective-permute-done.29.refs_21_), channel_id=1, source_target_pairs={{0,16},{1,17},{2,18},{3,19},{4,52},{5,53},{6,54},{7,55},{8,24},{9,... | collective-permute-start | bytes 1572872 | tf_op jit(solution)/shard_map/ppermute | solution.py:54
  88.2 24.1 %collective-permute-start.4 = (bf16[2,512,512]{2,1,0:T(8,128)(2,1)}, bf16[2,512,512]{2,1,0:T(8,128)(2,1)}, u32[]{:S(2)}, u32[]{:S(2)}) collective-permute-start(bf16[2,512,512]{2,1,0:T(8,128)(2,1)} %collective-permute-done.3.refs_2_.refs_6_), channel_id=1, source_target_pairs={{0,1},{1,2},{2,3},{3,0},{4,7},{5,4},{6,5},{7,6},{8,9},{9,10},{10,1... | collective-permute-start | bytes 3145736 | tf_op jit(solution)/shard_map/ppermute | solution.py:54
  91.0 23.9 %copy-start.6 = (bf16[2,512,512]{2,1,0:T(8,128)(2,1)}, bf16[2,512,512]{2,1,0:T(8,128)(2,1)S(1)}, u32[]{:S(2)}) copy-start(bf16[2,512,512]{2,1,0:T(8,128)(2,1)S(1)} %collective-permute-done.5.refs_8_.refs_12_) | copy-start | bytes 3145732
  91.0 12.6 %collective-permute-start.15 = (bf16[512,512]{1,0:T(8,128)(2,1)S(1)}, bf16[512,512]{1,0:T(8,128)(2,1)}, u32[]{:S(2)}, u32[]{:S(2)}) collective-permute-start(bf16[512,512]{1,0:T(8,128)(2,1)S(1)} %collective-permute-done.14.refs_21_), channel_id=1, source_target_pairs={{0,16},{1,17},{2,18},{3,19},{4,52},{5,53},{6,54},{7,55},{8,24},{9,... | collective-permute-start | bytes 1572872 | tf_op jit(solution)/shard_map/ppermute | solution.py:54
  95.4 20.2 %copy-start.21 = (bf16[512,512]{1,0:T(8,128)(2,1)}, bf16[512,512]{1,0:T(8,128)(2,1)S(1)}, u32[]{:S(2)}) copy-start(bf16[512,512]{1,0:T(8,128)(2,1)S(1)} %collective-permute-done.30.refs_22_) | copy-start | bytes 1572868
  95.4 19.5 %collective-permute-start.23 = (bf16[2,512,512]{2,1,0:T(8,128)(2,1)S(1)}, bf16[2,512,512]{2,1,0:T(8,128)(2,1)S(1)}, u32[]{:S(2)}, u32[]{:S(2)}) collective-permute-start(bf16[2,512,512]{2,1,0:T(8,128)(2,1)S(1)} %collective-permute-done.19.refs_2_.refs_6_), channel_id=1, source_target_pairs={{0,4},{1,5},{2,6},{3,7},{4,0},{5,1},{6,2},{7,3},{8,12},{9,13},{10,... | collective-permute-start | bytes 3145736 | tf_op jit(solution)/shard_map/ppermute | solution.py:54
  101.1 13.9 %copy-start.7 = (bf16[2,512,512]{2,1,0:T(8,128)(2,1)}, bf16[2,512,512]{2,1,0:T(8,128)(2,1)S(1)}, u32[]{:S(2)}) copy-start(bf16[2,512,512]{2,1,0:T(8,128)(2,1)S(1)} %collective-permute-done.22.refs_9_.refs_13_) | copy-start | bytes 3145732
  101.1 8.4 %collective-permute-start.31 = (bf16[512,512]{1,0:T(8,128)(2,1)S(1)}, bf16[512,512]{1,0:T(8,128)(2,1)S(1)}, u32[]{:S(2)}, u32[]{:S(2)}) collective-permute-start(bf16[512,512]{1,0:T(8,128)(2,1)S(1)} %collective-permute-done.30.refs_22_), channel_id=1, source_target_pairs={{0,16},{1,17},{2,18},{3,19},{4,52},{5,53},{6,54},{7,55},{8,24},{9,... | collective-permute-start | bytes 1572872 | tf_op jit(solution)/shard_map/ppermute | solution.py:54
  101.1 13.8 %copy-start.8 = (bf16[2,512,512]{2,1,0:T(8,128)(2,1)}, bf16[2,512,512]{2,1,0:T(8,128)(2,1)S(1)}, u32[]{:S(2)}) copy-start(bf16[2,512,512]{2,1,0:T(8,128)(2,1)S(1)} %collective-permute-done.20.refs_3_.refs_7_) | copy-start | bytes 3145732
  101.1 13.8 %collective-permute-start.24 = (bf16[2,512,512]{2,1,0:T(8,128)(2,1)S(1)}, bf16[2,512,512]{2,1,0:T(8,128)(2,1)S(1)}, u32[]{:S(2)}, u32[]{:S(2)}) collective-permute-start(bf16[2,512,512]{2,1,0:T(8,128)(2,1)S(1)} %collective-permute-done.20.refs_3_.refs_7_), channel_id=1, source_target_pairs={{0,4},{1,5},{2,6},{3,7},{4,0},{5,1},{6,2},{7,3},{8,12},{9,13},{10,... | collective-permute-start | bytes 3145736 | tf_op jit(solution)/shard_map/ppermute | solution.py:54
  103.5 29.1 %collective-permute-start.6 = (bf16[2,512,512]{2,1,0:T(8,128)(2,1)S(1)}, bf16[2,512,512]{2,1,0:T(8,128)(2,1)}, u32[]{:S(2)}, u32[]{:S(2)}) collective-permute-start(bf16[2,512,512]{2,1,0:T(8,128)(2,1)S(1)} %collective-permute-done.2.refs_1_.refs_5_), channel_id=1, source_target_pairs={{0,4},{1,5},{2,6},{3,7},{4,0},{5,1},{6,2},{7,3},{8,12},{9,13},{10,... | collective-permute-start | bytes 3145736 | tf_op jit(solution)/shard_map/ppermute | solution.py:54
  109.5 6.0 %copy-start.22 = (bf16[512,512]{1,0:T(8,128)(2,1)}, bf16[512,512]{1,0:T(8,128)(2,1)S(1)}, u32[]{:S(2)}) copy-start(bf16[512,512]{1,0:T(8,128)(2,1)S(1)} %collective-permute-done.31.refs_23_) | copy-start | bytes 1572868
  109.5 23.1 %collective-permute-start.7 = (bf16[2,512,512]{2,1,0:T(8,128)(2,1)}, bf16[2,512,512]{2,1,0:T(8,128)(2,1)}, u32[]{:S(2)}, u32[]{:S(2)}) collective-permute-start(bf16[2,512,512]{2,1,0:T(8,128)(2,1)} %collective-permute-done.3.refs_2_.refs_6_), channel_id=1, source_target_pairs={{0,4},{1,5},{2,6},{3,7},{4,0},{5,1},{6,2},{7,3},{8,12},{9,13},{10,... | collective-permute-start | bytes 3145736 | tf_op jit(solution)/shard_map/ppermute | solution.py:54
  112.3 20.3 %collective-permute-start.8 = (bf16[2,512,512]{2,1,0:T(8,128)(2,1)}, bf16[2,512,512]{2,1,0:T(8,128)(2,1)}, u32[]{:S(2)}, u32[]{:S(2)}) collective-permute-start(bf16[2,512,512]{2,1,0:T(8,128)(2,1)} %collective-permute-done.4.refs_3_.refs_7_), channel_id=1, source_target_pairs={{0,4},{1,5},{2,6},{3,7},{4,0},{5,1},{6,2},{7,3},{8,12},{9,13},{10,... | collective-permute-start | bytes 3145736 | tf_op jit(solution)/shard_map/ppermute | solution.py:54
  114.9 1.0 copy-start.9
  114.9 17.7 %collective-permute-start.12 = (bf16[512,512]{1,0:T(8,128)(2,1)}, bf16[512,512]{1,0:T(8,128)(2,1)}, u32[]{:S(2)}, u32[]{:S(2)}) collective-permute-start(bf16[512,512]{1,0:T(8,128)(2,1)} %collective-permute-done.11.refs_18_), channel_id=1, source_target_pairs={{0,16},{1,17},{2,18},{3,19},{4,52},{5,53},{6,54},{7,55},{8,24},{9,... | collective-permute-start | bytes 1572872 | tf_op jit(solution)/shard_map/ppermute | solution.py:54
  115.0 1.2 copy-start.10
  115.0 17.6 %collective-permute-start.16 = (bf16[512,512]{1,0:T(8,128)(2,1)}, bf16[512,512]{1,0:T(8,128)(2,1)}, u32[]{:S(2)}, u32[]{:S(2)}) collective-permute-start(bf16[512,512]{1,0:T(8,128)(2,1)} %collective-permute-done.15.refs_22_), channel_id=1, source_target_pairs={{0,16},{1,17},{2,18},{3,19},{4,52},{5,53},{6,54},{7,55},{8,24},{9,... | collective-permute-start | bytes 1572872 | tf_op jit(solution)/shard_map/ppermute | solution.py:54

commit v3 on v2

--- a/solution.py
+++ b/solution.py
@@ -216,12 +216,12 @@
     ("bm2", "bm1", "z", ()),
     ("bm3", "bm2", "z", ()),
     ("br1", "br0", "x", ()),
-    ("bq0", "br0", "y", ("br1",)),
     ("br2", "br1", "x", ()),
+    ("bq0", "br0", "y", ("br2",)),
     ("br3", "br2", "x", ()),
     ("bq1", "bq0", "x", ()),
     ("bq2", "bq1", "x", ()),
-    ("bq3", "bq2", "x", ()),
+    ("bq3", "br3", "y", ()),
     ("bM1", "bm1", "c", ()),
     ("bM2", "bm2", "c", ()),
     ("bM3", "bm3", "c", ()),

time: 149 us -> 146 us (0.980)
  starting transfers between devices: 67.2 us -> 64.4 us
    ppermute x32, starting transfers between devices: 67.2 us -> 64.4 us  [send(): return lax.ppermute(block, AXES, moves)]
  transfers between devices with their start and end apart: 32 -> 32, of which waited for: 9 -> 10; matrix products, arithmetic and copies ran while one was open for 2% -> 2% of each run, Pallas kernels for 11% -> 11%
where the time goes in v3:
time: 146 us
  starting transfers between devices  64.4 us (44%)
  waiting for transfers between devices  44 us (30%)
  Pallas kernels  31.6 us (22%)
  local copies, waits for them, and re-layouts  2.46 us (2%)
  other arithmetic  2.28 us (2%)
    ppermute x32, starting transfers between devices, send(): return lax.ppermute(block, AXES, moves)  64.4 us
    ppermute x32, waiting for transfers between devices, send(): return lax.ppermute(block, AXES, moves)  44 us
    pallas_call x2, Pallas kernels, update(): pl.pallas_call(functools.partial(update_kernel, tokens, factor_at, groups...  31.6 us
  transfers between devices with their start and end apart: 32, of which 10 were waited for; matrix products, arithmetic and copies ran while one was open for 2% of the time, Pallas kernels for 11%

profile of v3, /device:TPU:1, one launch (start us, length us, event | category | flops | bytes accessed | tf_op | source)
XLA Modules:
  0.0 145.8 jit_solution(7554568503841426174)
XLA Ops:
  0.6 6.2 %collective-permute-start = (bf16[512,512]{1,0:T(8,128)(2,1)}, bf16[512,512]{1,0:T(8,128)(2,1)S(1)}, u32[]{:S(2)}, u32[]{:S(2)}) collective-permute-start(bf16[512,512]{1,0:T(8,128)(2,1)} %param.5), channel_id=1, source_target_pairs={{0,32},{1,48},{2,0},{3,16},{4,64},{5,80},{6,96},{7,112},{8,17},{9,... | collective-permute-start | bytes 1572872 | tf_op jit(solution)/shard_map/ppermute | solution.py:54
  6.8 3.3 %collective-permute-start.17 = (bf16[512,512]{1,0:T(8,128)(2,1)}, bf16[512,512]{1,0:T(8,128)(2,1)S(1)}, u32[]{:S(2)}, u32[]{:S(2)}) collective-permute-start(bf16[512,512]{1,0:T(8,128)(2,1)} %param.5), channel_id=1, source_target_pairs={{0,8},{1,9},{2,10},{3,11},{4,12},{5,13},{6,14},{7,15},{8,0},{9,1},... | collective-permute-start | bytes 1572872 | tf_op jit(solution)/shard_map/ppermute | solution.py:54
  10.2 3.5 %collective-permute-start.9 = (bf16[512,512]{1,0:T(8,128)(2,1)}, bf16[512,512]{1,0:T(8,128)(2,1)S(1)}, u32[]{:S(2)}, u32[]{:S(2)}) collective-permute-start(bf16[512,512]{1,0:T(8,128)(2,1)} %param.4), channel_id=1, source_target_pairs={{0,32},{1,48},{2,0},{3,16},{4,64},{5,80},{6,96},{7,112},{8,17},{9,... | collective-permute-start | bytes 1572872 | tf_op jit(solution)/shard_map/ppermute | solution.py:54
  13.6 3.8 %collective-permute-done.refs_16_ = bf16[512,512]{1,0:T(8,128)(2,1)S(1)} collective-permute-done((bf16[512,512]{1,0:T(8,128)(2,1)}, bf16[512,512]{1,0:T(8,128)(2,1)S(1)}, u32[]{:S(2)}, u32[]{:S(2)}) %collective-permute-start) | collective-permute-done | bytes 524320 | tf_op jit(solution)/shard_map/ppermute | solution.py:54
  17.4 2.6 %collective-permute-start.25 = (bf16[512,512]{1,0:T(8,128)(2,1)S(1)}, bf16[512,512]{1,0:T(8,128)(2,1)S(1)}, u32[]{:S(2)}, u32[]{:S(2)}) collective-permute-start(bf16[512,512]{1,0:T(8,128)(2,1)S(1)} %collective-permute-done.refs_16_), channel_id=1, source_target_pairs={{0,16},{1,17},{2,18},{3,19},{4,52},{5,53},{6,54},{7,55},{8,24},{9,... | collective-permute-start | bytes 1572872 | tf_op jit(solution)/shard_map/ppermute | solution.py:54
  20.0 1.4 collective-permute-start.1
  21.5 12.6 %collective-permute-done.17 = bf16[512,512]{1,0:T(8,128)(2,1)S(1)} collective-permute-done((bf16[512,512]{1,0:T(8,128)(2,1)}, bf16[512,512]{1,0:T(8,128)(2,1)S(1)}, u32[]{:S(2)}, u32[]{:S(2)}) %collective-permute-start.17) | collective-permute-done | bytes 524320 | tf_op jit(solution)/shard_map/ppermute | solution.py:54
  34.1 1.1 pad_maximum_fusion.1.refs_0_.refs_4_
  35.2 0.0 copy-start.1
  35.2 0.1 collective-permute-start.18
  35.3 0.3 collective-permute-start.21
  35.7 0.0 collective-permute-done.9.refs_16_
  35.7 3.4 %collective-permute-start.10 = (bf16[512,512]{1,0:T(8,128)(2,1)S(1)}, bf16[512,512]{1,0:T(8,128)(2,1)S(1)}, u32[]{:S(2)}, u32[]{:S(2)}) collective-permute-start(bf16[512,512]{1,0:T(8,128)(2,1)S(1)} %collective-permute-done.9.refs_16_), channel_id=1, source_target_pairs={{0,16},{1,17},{2,18},{3,19},{4,52},{5,53},{6,54},{7,55},{8,24},{9,... | collective-permute-start | bytes 1572872 | tf_op jit(solution)/shard_map/ppermute | solution.py:54
  39.1 0.0 collective-permute-done.25.refs_17_
  39.1 0.1 collective-permute-start.26
  39.2 5.1 %collective-permute-done.1 = bf16[512,512]{1,0:T(8,128)(2,1)S(1)} collective-permute-done((bf16[512,512]{1,0:T(8,128)(2,1)}, bf16[512,512]{1,0:T(8,128)(2,1)S(1)}, u32[]{:S(2)}, u32[]{:S(2)}) %collective-permute-start.1) | collective-permute-done | bytes 524320 | tf_op jit(solution)/shard_map/ppermute | solution.py:54
  44.2 1.1 pad_maximum_fusion.refs_0_.refs_4_
  45.4 1.8 %collective-permute-start.2 = (bf16[2,512,512]{2,1,0:T(8,128)(2,1)S(1)}, bf16[2,512,512]{2,1,0:T(8,128)(2,1)S(1)}, u32[]{:S(2)}, u32[]{:S(2)}) collective-permute-start(bf16[2,512,512]{2,1,0:T(8,128)(2,1)S(1)} %pad_maximum_fusion.refs_0_.refs_4_), channel_id=1, source_target_pairs={{0,1},{1,2},{2,3},{3,0},{4,7},{5,4},{6,5},{7,6},{8,9},{9,10},{10,1... | collective-permute-start | bytes 3145736 | tf_op jit(solution)/shard_map/ppermute | solution.py:54
  47.2 0.0 collective-permute-done.10.refs_17_
  47.2 1.5 %collective-permute-start.13 = (bf16[512,512]{1,0:T(8,128)(2,1)S(1)}, bf16[512,512]{1,0:T(8,128)(2,1)S(1)}, u32[]{:S(2)}, u32[]{:S(2)}) collective-permute-start(bf16[512,512]{1,0:T(8,128)(2,1)S(1)} %collective-permute-done.9.refs_16_), channel_id=1, source_target_pairs={{0,64},{1,65},{2,66},{3,67},{4,68},{5,69},{6,70},{7,71},{8,72},{9,... | collective-permute-start | bytes 1572872 | tf_op jit(solution)/shard_map/ppermute | solution.py:54
  48.7 2.1 %collective-permute-done.26.refs_18_ = bf16[512,512]{1,0:T(8,128)(2,1)S(1)} collective-permute-done((bf16[512,512]{1,0:T(8,128)(2,1)S(1)}, bf16[512,512]{1,0:T(8,128)(2,1)S(1)}, u32[]{:S(2)}, u32[]{:S(2)}) %collective-permute-start.26) | collective-permute-done | bytes 524320 | tf_op jit(solution)/shard_map/ppermute | solution.py:54
  50.8 3.4 %collective-permute-start.11 = (bf16[512,512]{1,0:T(8,128)(2,1)S(1)}, bf16[512,512]{1,0:T(8,128)(2,1)}, u32[]{:S(2)}, u32[]{:S(2)}) collective-permute-start(bf16[512,512]{1,0:T(8,128)(2,1)S(1)} %collective-permute-done.10.refs_17_), channel_id=1, source_target_pairs={{0,16},{1,17},{2,18},{3,19},{4,52},{5,53},{6,54},{7,55},{8,24},{9,... | collective-permute-start | bytes 1572872 | tf_op jit(solution)/shard_map/ppermute | solution.py:54
  54.2 0.0 collective-permute-done.18.refs_1_.refs_5_
  54.2 6.7 %collective-permute-start.19 = (bf16[2,512,512]{2,1,0:T(8,128)(2,1)S(1)}, bf16[2,512,512]{2,1,0:T(8,128)(2,1)S(1)}, u32[]{:S(2)}, u32[]{:S(2)}) collective-permute-start(bf16[2,512,512]{2,1,0:T(8,128)(2,1)S(1)} %collective-permute-done.18.refs_1_.refs_5_), channel_id=1, source_target_pairs={{0,1},{1,2},{2,3},{3,0},{4,7},{5,4},{6,5},{7,6},{8,9},{9,10},{10,1... | collective-permute-start | bytes 3145736 | tf_op jit(solution)/shard_map/ppermute | solution.py:54
  60.9 0.0 collective-permute-start.28
  60.9 1.5 %collective-permute-done.13.refs_20_ = bf16[512,512]{1,0:T(8,128)(2,1)S(1)} collective-permute-done((bf16[512,512]{1,0:T(8,128)(2,1)S(1)}, bf16[512,512]{1,0:T(8,128)(2,1)S(1)}, u32[]{:S(2)}, u32[]{:S(2)}) %collective-permute-start.13) | collective-permute-done | bytes 524320 | tf_op jit(solution)/shard_map/ppermute | solution.py:54
  62.4 0.6 collective-permute-start.5
  63.0 0.0 collective-permute-done.11.refs_18_
  63.1 1.8 %collective-permute-start.27 = (bf16[512,512]{1,0:T(8,128)(2,1)S(1)}, bf16[512,512]{1,0:T(8,128)(2,1)S(1)}, u32[]{:S(2)}, u32[]{:S(2)}) collective-permute-start(bf16[512,512]{1,0:T(8,128)(2,1)S(1)} %collective-permute-done.26.refs_18_), channel_id=1, source_target_pairs={{0,16},{1,17},{2,18},{3,19},{4,52},{5,53},{6,54},{7,55},{8,24},{9,... | collective-permute-start | bytes 1572872 | tf_op jit(solution)/shard_map/ppermute | solution.py:54
  64.8 5.7 %collective-permute-start.3 = (bf16[2,512,512]{2,1,0:T(8,128)(2,1)S(1)}, bf16[2,512,512]{2,1,0:T(8,128)(2,1)}, u32[]{:S(2)}, u32[]{:S(2)}) collective-permute-start(bf16[2,512,512]{2,1,0:T(8,128)(2,1)S(1)} %collective-permute-done.2.refs_1_.refs_5_), channel_id=1, source_target_pairs={{0,1},{1,2},{2,3},{3,0},{4,7},{5,4},{6,5},{7,6},{8,9},{9,10},{10,1... | collective-permute-start | bytes 3145736 | tf_op jit(solution)/shard_map/ppermute | solution.py:54
  70.5 3.1 %collective-permute-done.28.refs_20_ = bf16[512,512]{1,0:T(8,128)(2,1)S(1)} collective-permute-done((bf16[512,512]{1,0:T(8,128)(2,1)S(1)}, bf16[512,512]{1,0:T(8,128)(2,1)S(1)}, u32[]{:S(2)}, u32[]{:S(2)}) %collective-permute-start.28) | collective-permute-done | bytes 524320 | tf_op jit(solution)/shard_map/ppermute | solution.py:54
  73.6 1.8 %collective-permute-start.14 = (bf16[512,512]{1,0:T(8,128)(2,1)S(1)}, bf16[512,512]{1,0:T(8,128)(2,1)S(1)}, u32[]{:S(2)}, u32[]{:S(2)}) collective-permute-start(bf16[512,512]{1,0:T(8,128)(2,1)S(1)} %collective-permute-done.13.refs_20_), channel_id=1, source_target_pairs={{0,16},{1,17},{2,18},{3,19},{4,52},{5,53},{6,54},{7,55},{8,24},{9,... | collective-permute-start | bytes 1572872 | tf_op jit(solution)/shard_map/ppermute | solution.py:54
  75.4 1.0 collective-permute-start.22
  76.3 0.0 collective-permute-done.19.refs_2_.refs_6_
  76.3 2.1 %collective-permute-start.20 = (bf16[2,512,512]{2,1,0:T(8,128)(2,1)S(1)}, bf16[2,512,512]{2,1,0:T(8,128)(2,1)S(1)}, u32[]{:S(2)}, u32[]{:S(2)}) collective-permute-start(bf16[2,512,512]{2,1,0:T(8,128)(2,1)S(1)} %collective-permute-done.19.refs_2_.refs_6_), channel_id=1, source_target_pairs={{0,1},{1,2},{2,3},{3,0},{4,7},{5,4},{6,5},{7,6},{8,9},{9,10},{10,1... | collective-permute-start | bytes 3145736 | tf_op jit(solution)/shard_map/ppermute | solution.py:54
  78.4 3.9 %collective-permute-done.14.refs_21_ = bf16[512,512]{1,0:T(8,128)(2,1)S(1)} collective-permute-done((bf16[512,512]{1,0:T(8,128)(2,1)S(1)}, bf16[512,512]{1,0:T(8,128)(2,1)S(1)}, u32[]{:S(2)}, u32[]{:S(2)}) %collective-permute-start.14) | collective-permute-done | bytes 524320 | tf_op jit(solution)/shard_map/ppermute | solution.py:54
  82.3 2.7 %collective-permute-start.29 = (bf16[512,512]{1,0:T(8,128)(2,1)S(1)}, bf16[512,512]{1,0:T(8,128)(2,1)S(1)}, u32[]{:S(2)}, u32[]{:S(2)}) collective-permute-start(bf16[512,512]{1,0:T(8,128)(2,1)S(1)} %collective-permute-done.28.refs_20_), channel_id=1, source_target_pairs={{0,16},{1,17},{2,18},{3,19},{4,52},{5,53},{6,54},{7,55},{8,24},{9,... | collective-permute-start | bytes 1572872 | tf_op jit(solution)/shard_map/ppermute | solution.py:54
  85.0 1.2 collective-permute-start.31
  86.2 3.2 %collective-permute-start.4 = (bf16[2,512,512]{2,1,0:T(8,128)(2,1)}, bf16[2,512,512]{2,1,0:T(8,128)(2,1)}, u32[]{:S(2)}, u32[]{:S(2)}) collective-permute-start(bf16[2,512,512]{2,1,0:T(8,128)(2,1)} %collective-permute-done.3.refs_2_.refs_6_), channel_id=1, source_target_pairs={{0,1},{1,2},{2,3},{3,0},{4,7},{5,4},{6,5},{7,6},{8,9},{9,10},{10,1... | collective-permute-start | bytes 3145736 | tf_op jit(solution)/shard_map/ppermute | solution.py:54
  89.4 1.7 %collective-permute-done.29.refs_21_ = bf16[512,512]{1,0:T(8,128)(2,1)S(1)} collective-permute-done((bf16[512,512]{1,0:T(8,128)(2,1)S(1)}, bf16[512,512]{1,0:T(8,128)(2,1)S(1)}, u32[]{:S(2)}, u32[]{:S(2)}) %collective-permute-start.29) | collective-permute-done | bytes 524320 | tf_op jit(solution)/shard_map/ppermute | solution.py:54
  91.1 3.4 %collective-permute-start.15 = (bf16[512,512]{1,0:T(8,128)(2,1)S(1)}, bf16[512,512]{1,0:T(8,128)(2,1)}, u32[]{:S(2)}, u32[]{:S(2)}) collective-permute-start(bf16[512,512]{1,0:T(8,128)(2,1)S(1)} %collective-permute-done.14.refs_21_), channel_id=1, source_target_pairs={{0,16},{1,17},{2,18},{3,19},{4,52},{5,53},{6,54},{7,55},{8,24},{9,... | collective-permute-start | bytes 1572872 | tf_op jit(solution)/shard_map/ppermute | solution.py:54
  94.5 4.9 %collective-permute-done.31.refs_23_ = bf16[512,512]{1,0:T(8,128)(2,1)S(1)} collective-permute-done((bf16[512,512]{1,0:T(8,128)(2,1)S(1)}, bf16[512,512]{1,0:T(8,128)(2,1)S(1)}, u32[]{:S(2)}, u32[]{:S(2)}) %collective-permute-start.31) | collective-permute-done | bytes 524320 | tf_op jit(solution)/shard_map/ppermute | solution.py:54
  99.5 1.4 collective-permute-start.23
  100.9 0.1 collective-permute-start.30
  101.0 0.0 collective-permute-done.20.refs_3_.refs_7_
  101.0 0.7 collective-permute-start.24
  101.7 2.3 %collective-permute-start.6 = (bf16[2,512,512]{2,1,0:T(8,128)(2,1)S(1)}, bf16[2,512,512]{2,1,0:T(8,128)(2,1)}, u32[]{:S(2)}, u32[]{:S(2)}) collective-permute-start(bf16[2,512,512]{2,1,0:T(8,128)(2,1)S(1)} %collective-permute-done.2.refs_1_.refs_5_), channel_id=1, source_target_pairs={{0,4},{1,5},{2,6},{3,7},{4,0},{5,1},{6,2},{7,3},{8,12},{9,13},{10,... | collective-permute-start | bytes 3145736 | tf_op jit(solution)/shard_map/ppermute | solution.py:54
  103.9 5.2 %collective-permute-done.30.refs_22_ = bf16[512,512]{1,0:T(8,128)(2,1)S(1)} collective-permute-done((bf16[512,512]{1,0:T(8,128)(2,1)S(1)}, bf16[512,512]{1,0:T(8,128)(2,1)S(1)}, u32[]{:S(2)}, u32[]{:S(2)}) %collective-permute-start.30) | collective-permute-done | bytes 524320 | tf_op jit(solution)/shard_map/ppermute | solution.py:54
  109.2 2.1 %collective-permute-start.7 = (bf16[2,512,512]{2,1,0:T(8,128)(2,1)}, bf16[2,512,512]{2,1,0:T(8,128)(2,1)}, u32[]{:S(2)}, u32[]{:S(2)}) collective-permute-start(bf16[2,512,512]{2,1,0:T(8,128)(2,1)} %collective-permute-done.3.refs_2_.refs_6_), channel_id=1, source_target_pairs={{0,4},{1,5},{2,6},{3,7},{4,0},{5,1},{6,2},{7,3},{8,12},{9,13},{10,... | collective-permute-start | bytes 3145736 | tf_op jit(solution)/shard_map/ppermute | solution.py:54
  111.3 0.0 collective-permute-done.4.refs_3_.refs_7_
  111.3 0.1 collective-permute-start.8
  111.4 0.0 collective-permute-done.23.refs_10_.refs_14_
  111.4 0.1 collective-permute-start.12
  111.5 0.0 collective-permute-done.24.refs_11_.refs_15_
  111.5 0.9 copy-done.9
  112.4 0.0 collective-permute-start.16
  112.5 0.9 copy-done.10
  113.4 0.6 stack.41.place
  114.0 15.8 %shard_map.60 = bf16[2048,1024]{1,0:T(8,128)(2,1)} custom-call(s32[5]{0:T(128)} %stack.41.place, bf16[2,512,512]{2,1,0:T(8,128)(2,1)} %copy-done.1, bf16[2,512,512]{2,1,0:T(8,128)(2,1)} %copy-done.3, bf16[2,512,512]{2,1,0:T(8,128)(2,1)} %copy-done.6, bf16[2,512,512]{2,1,0:T(8,128)(2,1)} %copy-done.8, bf16[2,512,512]{2,1,0:T(8,128)(2,1)} %copy-done.1, ...), custom_call_target="tpu_custom_call" | custom-call | flops 1000 | bytes 1000 | tf_op jit(solution)/shard_map/pallas_call | solution.py:128
  129.8 0.0 collective-permute-done.12.refs_19_
  129.8 0.0 collective-permute-done.6.refs_9_.refs_13_
  129.8 0.0 collective-permute-done.7.refs_10_.refs_14_
  129.8 0.0 collective-permute-done.8.refs_11_.refs_15_
  129.9 15.8 %shard_map.59 = bf16[2048,1024]{1,0:T(8,128)(2,1)} custom-call(s32[5]{0:T(128)} %stack.41.place, bf16[2,512,512]{2,1,0:T(8,128)(2,1)} %copy-done, bf16[2,512,512]{2,1,0:T(8,128)(2,1)} %copy-done.2, bf16[2,512,512]{2,1,0:T(8,128)(2,1)} %collective-permute-done.3.refs_2_.refs_6_, bf16[2,512,512]{2,1,0:T(8,128)(2,1)} %collective-permute-done.4.refs_3_.refs_7_, ...), custom_call_target="tpu_custom_call" | custom-call | flops 1000 | bytes 1000 | tf_op jit(solution)/shard_map/pallas_call | solution.py:128
  (51 shorter events, 0.1 us)
Async XLA Ops:
  0.6 16.8 %collective-permute-start = (bf16[512,512]{1,0:T(8,128)(2,1)}, bf16[512,512]{1,0:T(8,128)(2,1)S(1)}, u32[]{:S(2)}, u32[]{:S(2)}) collective-permute-start(bf16[512,512]{1,0:T(8,128)(2,1)} %param.5), channel_id=1, source_target_pairs={{0,32},{1,48},{2,0},{3,16},{4,64},{5,80},{6,96},{7,112},{8,17},{9,... | collective-permute-start | bytes 1572872 | tf_op jit(solution)/shard_map/ppermute | solution.py:54
  6.8 27.2 %collective-permute-start.17 = (bf16[512,512]{1,0:T(8,128)(2,1)}, bf16[512,512]{1,0:T(8,128)(2,1)S(1)}, u32[]{:S(2)}, u32[]{:S(2)}) collective-permute-start(bf16[512,512]{1,0:T(8,128)(2,1)} %param.5), channel_id=1, source_target_pairs={{0,8},{1,9},{2,10},{3,11},{4,12},{5,13},{6,14},{7,15},{8,0},{9,1},... | collective-permute-start | bytes 1572872 | tf_op jit(solution)/shard_map/ppermute | solution.py:54
  10.2 25.5 %collective-permute-start.9 = (bf16[512,512]{1,0:T(8,128)(2,1)}, bf16[512,512]{1,0:T(8,128)(2,1)S(1)}, u32[]{:S(2)}, u32[]{:S(2)}) collective-permute-start(bf16[512,512]{1,0:T(8,128)(2,1)} %param.4), channel_id=1, source_target_pairs={{0,32},{1,48},{2,0},{3,16},{4,64},{5,80},{6,96},{7,112},{8,17},{9,... | collective-permute-start | bytes 1572872 | tf_op jit(solution)/shard_map/ppermute | solution.py:54
  17.4 95.0 %copy-start.12 = (bf16[512,512]{1,0:T(8,128)(2,1)}, bf16[512,512]{1,0:T(8,128)(2,1)S(1)}, u32[]{:S(2)}) copy-start(bf16[512,512]{1,0:T(8,128)(2,1)S(1)} %collective-permute-done.refs_16_) | copy-start | bytes 1572868
  17.4 21.6 %collective-permute-start.25 = (bf16[512,512]{1,0:T(8,128)(2,1)S(1)}, bf16[512,512]{1,0:T(8,128)(2,1)S(1)}, u32[]{:S(2)}, u32[]{:S(2)}) collective-permute-start(bf16[512,512]{1,0:T(8,128)(2,1)S(1)} %collective-permute-done.refs_16_), channel_id=1, source_target_pairs={{0,16},{1,17},{2,18},{3,19},{4,52},{5,53},{6,54},{7,55},{8,24},{9,... | collective-permute-start | bytes 1572872 | tf_op jit(solution)/shard_map/ppermute | solution.py:54
  20.0 24.2 %collective-permute-start.1 = (bf16[512,512]{1,0:T(8,128)(2,1)}, bf16[512,512]{1,0:T(8,128)(2,1)S(1)}, u32[]{:S(2)}, u32[]{:S(2)}) collective-permute-start(bf16[512,512]{1,0:T(8,128)(2,1)} %param.4), channel_id=1, source_target_pairs={{0,8},{1,9},{2,10},{3,11},{4,12},{5,13},{6,14},{7,15},{8,0},{9,1},... | collective-permute-start | bytes 1572872 | tf_op jit(solution)/shard_map/ppermute | solution.py:54
  35.2 78.8 %copy-start.1 = (bf16[2,512,512]{2,1,0:T(8,128)(2,1)}, bf16[2,512,512]{2,1,0:T(8,128)(2,1)S(1)}, u32[]{:S(2)}) copy-start(bf16[2,512,512]{2,1,0:T(8,128)(2,1)S(1)} %pad_maximum_fusion.1.refs_0_.refs_4_) | copy-start | bytes 3145732
  35.2 19.0 %collective-permute-start.18 = (bf16[2,512,512]{2,1,0:T(8,128)(2,1)S(1)}, bf16[2,512,512]{2,1,0:T(8,128)(2,1)S(1)}, u32[]{:S(2)}, u32[]{:S(2)}) collective-permute-start(bf16[2,512,512]{2,1,0:T(8,128)(2,1)S(1)} %pad_maximum_fusion.1.refs_0_.refs_4_), channel_id=1, source_target_pairs={{0,1},{1,2},{2,3},{3,0},{4,7},{5,4},{6,5},{7,6},{8,9},{9,10},{10,1... | collective-permute-start | bytes 3145736 | tf_op jit(solution)/shard_map/ppermute | solution.py:54
  35.3 25.6 %collective-permute-start.21 = (bf16[2,512,512]{2,1,0:T(8,128)(2,1)S(1)}, bf16[2,512,512]{2,1,0:T(8,128)(2,1)S(1)}, u32[]{:S(2)}, u32[]{:S(2)}) collective-permute-start(bf16[2,512,512]{2,1,0:T(8,128)(2,1)S(1)} %pad_maximum_fusion.1.refs_0_.refs_4_), channel_id=1, source_target_pairs={{0,4},{1,5},{2,6},{3,7},{4,0},{5,1},{6,2},{7,3},{8,12},{9,13},{10,... | collective-permute-start | bytes 3145736 | tf_op jit(solution)/shard_map/ppermute | solution.py:54
  35.7 76.7 %copy-start.11 = (bf16[512,512]{1,0:T(8,128)(2,1)}, bf16[512,512]{1,0:T(8,128)(2,1)S(1)}, u32[]{:S(2)}) copy-start(bf16[512,512]{1,0:T(8,128)(2,1)S(1)} %collective-permute-done.9.refs_16_) | copy-start | bytes 1572868
  35.7 11.5 %collective-permute-start.10 = (bf16[512,512]{1,0:T(8,128)(2,1)S(1)}, bf16[512,512]{1,0:T(8,128)(2,1)S(1)}, u32[]{:S(2)}, u32[]{:S(2)}) collective-permute-start(bf16[512,512]{1,0:T(8,128)(2,1)S(1)} %collective-permute-done.9.refs_16_), channel_id=1, source_target_pairs={{0,16},{1,17},{2,18},{3,19},{4,52},{5,53},{6,54},{7,55},{8,24},{9,... | collective-permute-start | bytes 1572872 | tf_op jit(solution)/shard_map/ppermute | solution.py:54
  39.1 73.3 %copy-start.14 = (bf16[512,512]{1,0:T(8,128)(2,1)}, bf16[512,512]{1,0:T(8,128)(2,1)S(1)}, u32[]{:S(2)}) copy-start(bf16[512,512]{1,0:T(8,128)(2,1)S(1)} %collective-permute-done.25.refs_17_) | copy-start | bytes 1572868
  39.1 11.7 %collective-permute-start.26 = (bf16[512,512]{1,0:T(8,128)(2,1)S(1)}, bf16[512,512]{1,0:T(8,128)(2,1)S(1)}, u32[]{:S(2)}, u32[]{:S(2)}) collective-permute-start(bf16[512,512]{1,0:T(8,128)(2,1)S(1)} %collective-permute-done.25.refs_17_), channel_id=1, source_target_pairs={{0,16},{1,17},{2,18},{3,19},{4,52},{5,53},{6,54},{7,55},{8,24},{9,... | collective-permute-start | bytes 1572872 | tf_op jit(solution)/shard_map/ppermute | solution.py:54
  45.4 84.4 %copy-start = (bf16[2,512,512]{2,1,0:T(8,128)(2,1)}, bf16[2,512,512]{2,1,0:T(8,128)(2,1)S(1)}, u32[]{:S(2)}) copy-start(bf16[2,512,512]{2,1,0:T(8,128)(2,1)S(1)} %pad_maximum_fusion.refs_0_.refs_4_) | copy-start | bytes 3145732
  45.4 19.4 %collective-permute-start.2 = (bf16[2,512,512]{2,1,0:T(8,128)(2,1)S(1)}, bf16[2,512,512]{2,1,0:T(8,128)(2,1)S(1)}, u32[]{:S(2)}, u32[]{:S(2)}) collective-permute-start(bf16[2,512,512]{2,1,0:T(8,128)(2,1)S(1)} %pad_maximum_fusion.refs_0_.refs_4_), channel_id=1, source_target_pairs={{0,1},{1,2},{2,3},{3,0},{4,7},{5,4},{6,5},{7,6},{8,9},{9,10},{10,1... | collective-permute-start | bytes 3145736 | tf_op jit(solution)/shard_map/ppermute | solution.py:54
  47.2 65.2 %copy-start.13 = (bf16[512,512]{1,0:T(8,128)(2,1)}, bf16[512,512]{1,0:T(8,128)(2,1)S(1)}, u32[]{:S(2)}) copy-start(bf16[512,512]{1,0:T(8,128)(2,1)S(1)} %collective-permute-done.10.refs_17_) | copy-start | bytes 1572868
  47.2 15.2 %collective-permute-start.13 = (bf16[512,512]{1,0:T(8,128)(2,1)S(1)}, bf16[512,512]{1,0:T(8,128)(2,1)S(1)}, u32[]{:S(2)}, u32[]{:S(2)}) collective-permute-start(bf16[512,512]{1,0:T(8,128)(2,1)S(1)} %collective-permute-done.9.refs_16_), channel_id=1, source_target_pairs={{0,64},{1,65},{2,66},{3,67},{4,68},{5,69},{6,70},{7,71},{8,72},{9,... | collective-permute-start | bytes 1572872 | tf_op jit(solution)/shard_map/ppermute | solution.py:54
  50.8 61.6 %copy-start.16 = (bf16[512,512]{1,0:T(8,128)(2,1)}, bf16[512,512]{1,0:T(8,128)(2,1)S(1)}, u32[]{:S(2)}) copy-start(bf16[512,512]{1,0:T(8,128)(2,1)S(1)} %collective-permute-done.26.refs_18_) | copy-start | bytes 1572868
  50.8 12.2 %collective-permute-start.11 = (bf16[512,512]{1,0:T(8,128)(2,1)S(1)}, bf16[512,512]{1,0:T(8,128)(2,1)}, u32[]{:S(2)}, u32[]{:S(2)}) collective-permute-start(bf16[512,512]{1,0:T(8,128)(2,1)S(1)} %collective-permute-done.10.refs_17_), channel_id=1, source_target_pairs={{0,16},{1,17},{2,18},{3,19},{4,52},{5,53},{6,54},{7,55},{8,24},{9,... | collective-permute-start | bytes 1572872 | tf_op jit(solution)/shard_map/ppermute | solution.py:54
  54.2 47.4 %copy-start.3 = (bf16[2,512,512]{2,1,0:T(8,128)(2,1)}, bf16[2,512,512]{2,1,0:T(8,128)(2,1)S(1)}, u32[]{:S(2)}) copy-start(bf16[2,512,512]{2,1,0:T(8,128)(2,1)S(1)} %collective-permute-done.18.refs_1_.refs_5_) | copy-start | bytes 3145732
  54.2 22.1 %collective-permute-start.19 = (bf16[2,512,512]{2,1,0:T(8,128)(2,1)S(1)}, bf16[2,512,512]{2,1,0:T(8,128)(2,1)S(1)}, u32[]{:S(2)}, u32[]{:S(2)}) collective-permute-start(bf16[2,512,512]{2,1,0:T(8,128)(2,1)S(1)} %collective-permute-done.18.refs_1_.refs_5_), channel_id=1, source_target_pairs={{0,1},{1,2},{2,3},{3,0},{4,7},{5,4},{6,5},{7,6},{8,9},{9,10},{10,1... | collective-permute-start | bytes 3145736 | tf_op jit(solution)/shard_map/ppermute | solution.py:54
  60.9 40.7 %copy-start.4 = (bf16[2,512,512]{2,1,0:T(8,128)(2,1)}, bf16[2,512,512]{2,1,0:T(8,128)(2,1)S(1)}, u32[]{:S(2)}) copy-start(bf16[2,512,512]{2,1,0:T(8,128)(2,1)S(1)} %collective-permute-done.21.refs_8_.refs_12_) | copy-start | bytes 3145732
  60.9 12.7 %collective-permute-start.28 = (bf16[512,512]{1,0:T(8,128)(2,1)S(1)}, bf16[512,512]{1,0:T(8,128)(2,1)S(1)}, u32[]{:S(2)}, u32[]{:S(2)}) collective-permute-start(bf16[512,512]{1,0:T(8,128)(2,1)S(1)} %collective-permute-done.refs_16_), channel_id=1, source_target_pairs={{0,64},{1,65},{2,66},{3,67},{4,68},{5,69},{6,70},{7,71},{8,72},{9,... | collective-permute-start | bytes 1572872 | tf_op jit(solution)/shard_map/ppermute | solution.py:54
  62.4 32.1 %copy-start.15 = (bf16[512,512]{1,0:T(8,128)(2,1)}, bf16[512,512]{1,0:T(8,128)(2,1)S(1)}, u32[]{:S(2)}) copy-start(bf16[512,512]{1,0:T(8,128)(2,1)S(1)} %collective-permute-done.13.refs_20_) | copy-start | bytes 1572868
  62.4 22.6 %collective-permute-start.5 = (bf16[2,512,512]{2,1,0:T(8,128)(2,1)S(1)}, bf16[2,512,512]{2,1,0:T(8,128)(2,1)S(1)}, u32[]{:S(2)}, u32[]{:S(2)}) collective-permute-start(bf16[2,512,512]{2,1,0:T(8,128)(2,1)S(1)} %pad_maximum_fusion.refs_0_.refs_4_), channel_id=1, source_target_pairs={{0,4},{1,5},{2,6},{3,7},{4,0},{5,1},{6,2},{7,3},{8,12},{9,13},{10,... | collective-permute-start | bytes 3145736 | tf_op jit(solution)/shard_map/ppermute | solution.py:54
  63.1 12.3 %collective-permute-start.27 = (bf16[512,512]{1,0:T(8,128)(2,1)S(1)}, bf16[512,512]{1,0:T(8,128)(2,1)S(1)}, u32[]{:S(2)}, u32[]{:S(2)}) collective-permute-start(bf16[512,512]{1,0:T(8,128)(2,1)S(1)} %collective-permute-done.26.refs_18_), channel_id=1, source_target_pairs={{0,16},{1,17},{2,18},{3,19},{4,52},{5,53},{6,54},{7,55},{8,24},{9,... | collective-permute-start | bytes 1572872 | tf_op jit(solution)/shard_map/ppermute | solution.py:54
  64.8 65.0 %copy-start.2 = (bf16[2,512,512]{2,1,0:T(8,128)(2,1)}, bf16[2,512,512]{2,1,0:T(8,128)(2,1)S(1)}, u32[]{:S(2)}) copy-start(bf16[2,512,512]{2,1,0:T(8,128)(2,1)S(1)} %collective-permute-done.2.refs_1_.refs_5_) | copy-start | bytes 3145732
  64.8 21.4 %collective-permute-start.3 = (bf16[2,512,512]{2,1,0:T(8,128)(2,1)S(1)}, bf16[2,512,512]{2,1,0:T(8,128)(2,1)}, u32[]{:S(2)}, u32[]{:S(2)}) collective-permute-start(bf16[2,512,512]{2,1,0:T(8,128)(2,1)S(1)} %collective-permute-done.2.refs_1_.refs_5_), channel_id=1, source_target_pairs={{0,1},{1,2},{2,3},{3,0},{4,7},{5,4},{6,5},{7,6},{8,9},{9,10},{10,1... | collective-permute-start | bytes 3145736 | tf_op jit(solution)/shard_map/ppermute | solution.py:54
  73.6 21.0 %copy-start.18 = (bf16[512,512]{1,0:T(8,128)(2,1)}, bf16[512,512]{1,0:T(8,128)(2,1)S(1)}, u32[]{:S(2)}) copy-start(bf16[512,512]{1,0:T(8,128)(2,1)S(1)} %collective-permute-done.28.refs_20_) | copy-start | bytes 1572868
  73.6 8.7 %collective-permute-start.14 = (bf16[512,512]{1,0:T(8,128)(2,1)S(1)}, bf16[512,512]{1,0:T(8,128)(2,1)S(1)}, u32[]{:S(2)}, u32[]{:S(2)}) collective-permute-start(bf16[512,512]{1,0:T(8,128)(2,1)S(1)} %collective-permute-done.13.refs_20_), channel_id=1, source_target_pairs={{0,16},{1,17},{2,18},{3,19},{4,52},{5,53},{6,54},{7,55},{8,24},{9,... | collective-permute-start | bytes 1572872 | tf_op jit(solution)/shard_map/ppermute | solution.py:54
  75.4 25.6 %copy-start.19 = (bf16[512,512]{1,0:T(8,128)(2,1)}, bf16[512,512]{1,0:T(8,128)(2,1)S(1)}, u32[]{:S(2)}) copy-start(bf16[512,512]{1,0:T(8,128)(2,1)S(1)} %collective-permute-done.27.refs_19_) | copy-start | bytes 1572868
  75.4 25.5 %collective-permute-start.22 = (bf16[2,512,512]{2,1,0:T(8,128)(2,1)S(1)}, bf16[2,512,512]{2,1,0:T(8,128)(2,1)S(1)}, u32[]{:S(2)}, u32[]{:S(2)}) collective-permute-start(bf16[2,512,512]{2,1,0:T(8,128)(2,1)S(1)} %collective-permute-done.18.refs_1_.refs_5_), channel_id=1, source_target_pairs={{0,4},{1,5},{2,6},{3,7},{4,0},{5,1},{6,2},{7,3},{8,12},{9,13},{10,... | collective-permute-start | bytes 3145736 | tf_op jit(solution)/shard_map/ppermute | solution.py:54
  76.3 32.8 %copy-start.6 = (bf16[2,512,512]{2,1,0:T(8,128)(2,1)}, bf16[2,512,512]{2,1,0:T(8,128)(2,1)S(1)}, u32[]{:S(2)}) copy-start(bf16[2,512,512]{2,1,0:T(8,128)(2,1)S(1)} %collective-permute-done.19.refs_2_.refs_6_) | copy-start | bytes 3145732
  76.3 24.6 %collective-permute-start.20 = (bf16[2,512,512]{2,1,0:T(8,128)(2,1)S(1)}, bf16[2,512,512]{2,1,0:T(8,128)(2,1)S(1)}, u32[]{:S(2)}, u32[]{:S(2)}) collective-permute-start(bf16[2,512,512]{2,1,0:T(8,128)(2,1)S(1)} %collective-permute-done.19.refs_2_.refs_6_), channel_id=1, source_target_pairs={{0,1},{1,2},{2,3},{3,0},{4,7},{5,4},{6,5},{7,6},{8,9},{9,10},{10,1... | collective-permute-start | bytes 3145736 | tf_op jit(solution)/shard_map/ppermute | solution.py:54
  82.3 30.2 %copy-start.17 = (bf16[512,512]{1,0:T(8,128)(2,1)}, bf16[512,512]{1,0:T(8,128)(2,1)S(1)}, u32[]{:S(2)}) copy-start(bf16[512,512]{1,0:T(8,128)(2,1)S(1)} %collective-permute-done.14.refs_21_) | copy-start | bytes 1572868
  82.3 8.8 %collective-permute-start.29 = (bf16[512,512]{1,0:T(8,128)(2,1)S(1)}, bf16[512,512]{1,0:T(8,128)(2,1)S(1)}, u32[]{:S(2)}, u32[]{:S(2)}) collective-permute-start(bf16[512,512]{1,0:T(8,128)(2,1)S(1)} %collective-permute-done.28.refs_20_), channel_id=1, source_target_pairs={{0,16},{1,17},{2,18},{3,19},{4,52},{5,53},{6,54},{7,55},{8,24},{9,... | collective-permute-start | bytes 1572872 | tf_op jit(solution)/shard_map/ppermute | solution.py:54
  85.0 18.9 %copy-start.5 = (bf16[2,512,512]{2,1,0:T(8,128)(2,1)}, bf16[2,512,512]{2,1,0:T(8,128)(2,1)S(1)}, u32[]{:S(2)}) copy-start(bf16[2,512,512]{2,1,0:T(8,128)(2,1)S(1)} %collective-permute-done.5.refs_8_.refs_12_) | copy-start | bytes 3145732
  85.0 14.5 %collective-permute-start.31 = (bf16[512,512]{1,0:T(8,128)(2,1)S(1)}, bf16[512,512]{1,0:T(8,128)(2,1)S(1)}, u32[]{:S(2)}, u32[]{:S(2)}) collective-permute-start(bf16[512,512]{1,0:T(8,128)(2,1)S(1)} %collective-permute-done.27.refs_19_), channel_id=1, source_target_pairs={{0,64},{1,65},{2,66},{3,67},{4,68},{5,69},{6,70},{7,71},{8,72},{9,... | collective-permute-start | bytes 1572872 | tf_op jit(solution)/shard_map/ppermute | solution.py:54
  86.2 25.1 %collective-permute-start.4 = (bf16[2,512,512]{2,1,0:T(8,128)(2,1)}, bf16[2,512,512]{2,1,0:T(8,128)(2,1)}, u32[]{:S(2)}, u32[]{:S(2)}) collective-permute-start(bf16[2,512,512]{2,1,0:T(8,128)(2,1)} %collective-permute-done.3.refs_2_.refs_6_), channel_id=1, source_target_pairs={{0,1},{1,2},{2,3},{3,0},{4,7},{5,4},{6,5},{7,6},{8,9},{9,10},{10,1... | collective-permute-start | bytes 3145736 | tf_op jit(solution)/shard_map/ppermute | solution.py:54
  91.1 21.3 %copy-start.20 = (bf16[512,512]{1,0:T(8,128)(2,1)}, bf16[512,512]{1,0:T(8,128)(2,1)S(1)}, u32[]{:S(2)}) copy-start(bf16[512,512]{1,0:T(8,128)(2,1)S(1)} %collective-permute-done.29.refs_21_) | copy-start | bytes 1572868
  91.1 10.5 %collective-permute-start.15 = (bf16[512,512]{1,0:T(8,128)(2,1)S(1)}, bf16[512,512]{1,0:T(8,128)(2,1)}, u32[]{:S(2)}, u32[]{:S(2)}) collective-permute-start(bf16[512,512]{1,0:T(8,128)(2,1)S(1)} %collective-permute-done.14.refs_21_), channel_id=1, source_target_pairs={{0,16},{1,17},{2,18},{3,19},{4,52},{5,53},{6,54},{7,55},{8,24},{9,... | collective-permute-start | bytes 1572872 | tf_op jit(solution)/shard_map/ppermute | solution.py:54
  99.5 1.5 %copy-start.21 = (bf16[512,512]{1,0:T(8,128)(2,1)}, bf16[512,512]{1,0:T(8,128)(2,1)S(1)}, u32[]{:S(2)}) copy-start(bf16[512,512]{1,0:T(8,128)(2,1)S(1)} %collective-permute-done.31.refs_23_) | copy-start | bytes 1572868
  99.5 12.0 %collective-permute-start.23 = (bf16[2,512,512]{2,1,0:T(8,128)(2,1)S(1)}, bf16[2,512,512]{2,1,0:T(8,128)(2,1)S(1)}, u32[]{:S(2)}, u32[]{:S(2)}) collective-permute-start(bf16[2,512,512]{2,1,0:T(8,128)(2,1)S(1)} %collective-permute-done.19.refs_2_.refs_6_), channel_id=1, source_target_pairs={{0,4},{1,5},{2,6},{3,7},{4,0},{5,1},{6,2},{7,3},{8,12},{9,13},{10,... | collective-permute-start | bytes 3145736 | tf_op jit(solution)/shard_map/ppermute | solution.py:54
  100.9 10.6 %copy-start.7 = (bf16[2,512,512]{2,1,0:T(8,128)(2,1)}, bf16[2,512,512]{2,1,0:T(8,128)(2,1)S(1)}, u32[]{:S(2)}) copy-start(bf16[2,512,512]{2,1,0:T(8,128)(2,1)S(1)} %collective-permute-done.22.refs_9_.refs_13_) | copy-start | bytes 3145732
  100.9 8.3 %collective-permute-start.30 = (bf16[512,512]{1,0:T(8,128)(2,1)S(1)}, bf16[512,512]{1,0:T(8,128)(2,1)S(1)}, u32[]{:S(2)}, u32[]{:S(2)}) collective-permute-start(bf16[512,512]{1,0:T(8,128)(2,1)S(1)} %collective-permute-done.29.refs_21_), channel_id=1, source_target_pairs={{0,16},{1,17},{2,18},{3,19},{4,52},{5,53},{6,54},{7,55},{8,24},{9,... | collective-permute-start | bytes 1572872 | tf_op jit(solution)/shard_map/ppermute | solution.py:54
  101.0 10.6 %copy-start.8 = (bf16[2,512,512]{2,1,0:T(8,128)(2,1)}, bf16[2,512,512]{2,1,0:T(8,128)(2,1)S(1)}, u32[]{:S(2)}) copy-start(bf16[2,512,512]{2,1,0:T(8,128)(2,1)S(1)} %collective-permute-done.20.refs_3_.refs_7_) | copy-start | bytes 3145732
  101.0 10.6 %collective-permute-start.24 = (bf16[2,512,512]{2,1,0:T(8,128)(2,1)S(1)}, bf16[2,512,512]{2,1,0:T(8,128)(2,1)S(1)}, u32[]{:S(2)}, u32[]{:S(2)}) collective-permute-start(bf16[2,512,512]{2,1,0:T(8,128)(2,1)S(1)} %collective-permute-done.20.refs_3_.refs_7_), channel_id=1, source_target_pairs={{0,4},{1,5},{2,6},{3,7},{4,0},{5,1},{6,2},{7,3},{8,12},{9,13},{10,... | collective-permute-start | bytes 3145736 | tf_op jit(solution)/shard_map/ppermute | solution.py:54
  101.7 28.2 %collective-permute-start.6 = (bf16[2,512,512]{2,1,0:T(8,128)(2,1)S(1)}, bf16[2,512,512]{2,1,0:T(8,128)(2,1)}, u32[]{:S(2)}, u32[]{:S(2)}) collective-permute-start(bf16[2,512,512]{2,1,0:T(8,128)(2,1)S(1)} %collective-permute-done.2.refs_1_.refs_5_), channel_id=1, source_target_pairs={{0,4},{1,5},{2,6},{3,7},{4,0},{5,1},{6,2},{7,3},{8,12},{9,13},{10,... | collective-permute-start | bytes 3145736 | tf_op jit(solution)/shard_map/ppermute | solution.py:54
  109.2 3.3 %copy-start.22 = (bf16[512,512]{1,0:T(8,128)(2,1)}, bf16[512,512]{1,0:T(8,128)(2,1)S(1)}, u32[]{:S(2)}) copy-start(bf16[512,512]{1,0:T(8,128)(2,1)S(1)} %collective-permute-done.30.refs_22_) | copy-start | bytes 1572868
  109.2 20.6 %collective-permute-start.7 = (bf16[2,512,512]{2,1,0:T(8,128)(2,1)}, bf16[2,512,512]{2,1,0:T(8,128)(2,1)}, u32[]{:S(2)}, u32[]{:S(2)}) collective-permute-start(bf16[2,512,512]{2,1,0:T(8,128)(2,1)} %collective-permute-done.3.refs_2_.refs_6_), channel_id=1, source_target_pairs={{0,4},{1,5},{2,6},{3,7},{4,0},{5,1},{6,2},{7,3},{8,12},{9,13},{10,... | collective-permute-start | bytes 3145736 | tf_op jit(solution)/shard_map/ppermute | solution.py:54
  111.3 18.5 %collective-permute-start.8 = (bf16[2,512,512]{2,1,0:T(8,128)(2,1)}, bf16[2,512,512]{2,1,0:T(8,128)(2,1)}, u32[]{:S(2)}, u32[]{:S(2)}) collective-permute-start(bf16[2,512,512]{2,1,0:T(8,128)(2,1)} %collective-permute-done.4.refs_3_.refs_7_), channel_id=1, source_target_pairs={{0,4},{1,5},{2,6},{3,7},{4,0},{5,1},{6,2},{7,3},{8,12},{9,13},{10,... | collective-permute-start | bytes 3145736 | tf_op jit(solution)/shard_map/ppermute | solution.py:54
  111.4 1.0 copy-start.9
  111.4 18.4 %collective-permute-start.12 = (bf16[512,512]{1,0:T(8,128)(2,1)}, bf16[512,512]{1,0:T(8,128)(2,1)}, u32[]{:S(2)}, u32[]{:S(2)}) collective-permute-start(bf16[512,512]{1,0:T(8,128)(2,1)} %collective-permute-done.11.refs_18_), channel_id=1, source_target_pairs={{0,16},{1,17},{2,18},{3,19},{4,52},{5,53},{6,54},{7,55},{8,24},{9,... | collective-permute-start | bytes 1572872 | tf_op jit(solution)/shard_map/ppermute | solution.py:54
  112.4 1.0 copy-start.10
  112.4 17.4 %collective-permute-start.16 = (bf16[512,512]{1,0:T(8,128)(2,1)}, bf16[512,512]{1,0:T(8,128)(2,1)}, u32[]{:S(2)}, u32[]{:S(2)}) collective-permute-start(bf16[512,512]{1,0:T(8,128)(2,1)} %collective-permute-done.15.refs_22_), channel_id=1, source_target_pairs={{0,16},{1,17},{2,18},{3,19},{4,52},{5,53},{6,54},{7,55},{8,24},{9,... | collective-permute-start | bytes 1572872 | tf_op jit(solution)/shard_map/ppermute | solution.py:54

commit v4 on v3

--- a/solution.py
+++ b/solution.py
@@ -33,11 +33,11 @@
 
 
 def along_x(yh, x, yl, core, z):
-    return x + z - 2 * (x % 2) - yl + 2 + 2 * core
+    return x + z - 2 * (x % 2) - yl + 2
 
 
 def scatter_move(yh, x, yl, core, z):
-    return core, along_x(yh, x, yl, core, z), yh, x // 2, 2 * (x % 2) + yl
+    return core + yl, along_x(yh, x, yl, core, z), yh, x // 2, 2 * (x % 2) + yl
 
 
 SCATTER = permutation(scatter_move)
@@ -63,9 +63,9 @@
     toward = 1 - 2 * core
 
     def right_copy(j, s):
-        half = lax.rem(yh + halves[j], 2)
+        half = lax.rem(yh + halves[j] + z, 2)
         source = x + AT[s] * toward
-        token = source - 2 * core - z // 2 + z + 2 + 2 * half
+        token = source - 2 * core - z // 2 + z + 2
         column = 0 if len(halves) == 1 else pl.multiple_of(half * PIECE, PIECE)
         row = pl.multiple_of(lax.rem(token + 8, 4) * PIECE, PIECE)
         return pltpu.make_async_copy(
@@ -120,7 +120,7 @@
     def block(step, place):
         group = groups[0] + step * (groups[1] - groups[0])
         row = 2 * lax.rem(place[2] + group % 2, 2) + lax.rem(place[3] + group // 2, 2)
-        return row, 0 if len(halves) == 2 else lax.rem(place[0] + halves[0], 2)
+        return row, 0 if len(halves) == 2 else lax.rem(place[0] + halves[0] + place[4], 2)
 
     tile = pl.BlockSpec((PIECE, width), block)
     elsewhere = pl.BlockSpec(memory_space=pltpu.HBM)

time: 146 us -> 143 us (0.979)
  starting transfers between devices: 64.4 us -> 59 us
  waiting for transfers between devices: 44 us -> 47.6 us
    ppermute x32, starting transfers between devices: 64.4 us -> 59 us  [send(): return lax.ppermute(block, AXES, moves)]
    ppermute x32, waiting for transfers between devices: 44 us -> 47.6 us  [send(): return lax.ppermute(block, AXES, moves)]
  transfers between devices with their start and end apart: 32 -> 32, of which waited for: 10 -> 11; matrix products, arithmetic and copies ran while one was open for 2% -> 2% of each run, Pallas kernels for 11% -> 11%
where the time goes in v4:
time: 143 us
  starting transfers between devices  59 us (41%)
  waiting for transfers between devices  47.6 us (33%)
  Pallas kernels  31.6 us (22%)
  other arithmetic  2.28 us (2%)
  local copies, waits for them, and re-layouts  1.73 us (1%)
    ppermute x32, starting transfers between devices, send(): return lax.ppermute(block, AXES, moves)  59 us
    ppermute x32, waiting for transfers between devices, send(): return lax.ppermute(block, AXES, moves)  47.6 us
    pallas_call x2, Pallas kernels, update(): pl.pallas_call(functools.partial(update_kernel, tokens, factor_at, groups...  31.6 us
  transfers between devices with their start and end apart: 32, of which 11 were waited for; matrix products, arithmetic and copies ran while one was open for 2% of the time, Pallas kernels for 11%

profile of v4, /device:TPU:1, one launch (start us, length us, event | category | flops | bytes accessed | tf_op | source)
XLA Modules:
  0.0 143.2 jit_solution(12805537980138841534)
XLA Ops:
  0.6 6.8 %collective-permute-start = (bf16[512,512]{1,0:T(8,128)(2,1)}, bf16[512,512]{1,0:T(8,128)(2,1)S(1)}, u32[]{:S(2)}, u32[]{:S(2)}) collective-permute-start(bf16[512,512]{1,0:T(8,128)(2,1)} %param.5), channel_id=1, source_target_pairs={{0,32},{1,48},{2,0},{3,16},{4,96},{5,112},{6,64},{7,80},{8,81},{9,... | collective-permute-start | bytes 1572872 | tf_op jit(solution)/shard_map/ppermute | solution.py:54
  7.5 0.0 collective-permute-start.17
  7.5 3.3 %collective-permute-start.9 = (bf16[512,512]{1,0:T(8,128)(2,1)}, bf16[512,512]{1,0:T(8,128)(2,1)S(1)}, u32[]{:S(2)}, u32[]{:S(2)}) collective-permute-start(bf16[512,512]{1,0:T(8,128)(2,1)} %param.4), channel_id=1, source_target_pairs={{0,32},{1,48},{2,0},{3,16},{4,96},{5,112},{6,64},{7,80},{8,81},{9,... | collective-permute-start | bytes 1572872 | tf_op jit(solution)/shard_map/ppermute | solution.py:54
  10.7 8.9 %collective-permute-done.refs_16_ = bf16[512,512]{1,0:T(8,128)(2,1)S(1)} collective-permute-done((bf16[512,512]{1,0:T(8,128)(2,1)}, bf16[512,512]{1,0:T(8,128)(2,1)S(1)}, u32[]{:S(2)}, u32[]{:S(2)}) %collective-permute-start) | collective-permute-done | bytes 524320 | tf_op jit(solution)/shard_map/ppermute | solution.py:54
  19.6 1.7 %collective-permute-start.25 = (bf16[512,512]{1,0:T(8,128)(2,1)S(1)}, bf16[512,512]{1,0:T(8,128)(2,1)S(1)}, u32[]{:S(2)}, u32[]{:S(2)}) collective-permute-start(bf16[512,512]{1,0:T(8,128)(2,1)S(1)} %collective-permute-done.refs_16_), channel_id=1, source_target_pairs={{0,16},{1,17},{2,18},{3,19},{4,52},{5,53},{6,54},{7,55},{8,24},{9,... | collective-permute-start | bytes 1572872 | tf_op jit(solution)/shard_map/ppermute | solution.py:54
  21.3 2.5 %collective-permute-start.1 = (bf16[512,512]{1,0:T(8,128)(2,1)}, bf16[512,512]{1,0:T(8,128)(2,1)S(1)}, u32[]{:S(2)}, u32[]{:S(2)}) collective-permute-start(bf16[512,512]{1,0:T(8,128)(2,1)} %param.4), channel_id=1, source_target_pairs={{0,8},{1,9},{2,10},{3,11},{4,12},{5,13},{6,14},{7,15},{8,0},{9,1},... | collective-permute-start | bytes 1572872 | tf_op jit(solution)/shard_map/ppermute | solution.py:54
  23.8 8.2 %collective-permute-done.17 = bf16[512,512]{1,0:T(8,128)(2,1)S(1)} collective-permute-done((bf16[512,512]{1,0:T(8,128)(2,1)}, bf16[512,512]{1,0:T(8,128)(2,1)S(1)}, u32[]{:S(2)}, u32[]{:S(2)}) %collective-permute-start.17) | collective-permute-done | bytes 524320 | tf_op jit(solution)/shard_map/ppermute | solution.py:54
  32.0 1.1 pad_maximum_fusion.1.refs_0_.refs_4_
  33.1 0.0 copy-start.1
  33.2 0.1 collective-permute-start.18
  33.2 1.1 collective-permute-start.21
  34.4 0.0 collective-permute-done.9.refs_16_
  34.4 4.8 %collective-permute-start.10 = (bf16[512,512]{1,0:T(8,128)(2,1)S(1)}, bf16[512,512]{1,0:T(8,128)(2,1)S(1)}, u32[]{:S(2)}, u32[]{:S(2)}) collective-permute-start(bf16[512,512]{1,0:T(8,128)(2,1)S(1)} %collective-permute-done.9.refs_16_), channel_id=1, source_target_pairs={{0,16},{1,17},{2,18},{3,19},{4,52},{5,53},{6,54},{7,55},{8,24},{9,... | collective-permute-start | bytes 1572872 | tf_op jit(solution)/shard_map/ppermute | solution.py:54
  39.2 0.0 collective-permute-done.25.refs_17_
  39.2 0.1 collective-permute-start.26
  39.2 3.5 %collective-permute-done.1 = bf16[512,512]{1,0:T(8,128)(2,1)S(1)} collective-permute-done((bf16[512,512]{1,0:T(8,128)(2,1)}, bf16[512,512]{1,0:T(8,128)(2,1)S(1)}, u32[]{:S(2)}, u32[]{:S(2)}) %collective-permute-start.1) | collective-permute-done | bytes 524320 | tf_op jit(solution)/shard_map/ppermute | solution.py:54
  42.7 1.1 pad_maximum_fusion.refs_0_.refs_4_
  43.9 0.6 collective-permute-start.2
  44.5 0.8 collective-permute-done.10.refs_17_
  45.3 2.2 %collective-permute-start.13 = (bf16[512,512]{1,0:T(8,128)(2,1)S(1)}, bf16[512,512]{1,0:T(8,128)(2,1)S(1)}, u32[]{:S(2)}, u32[]{:S(2)}) collective-permute-start(bf16[512,512]{1,0:T(8,128)(2,1)S(1)} %collective-permute-done.9.refs_16_), channel_id=1, source_target_pairs={{0,64},{1,65},{2,66},{3,67},{4,68},{5,69},{6,70},{7,71},{8,72},{9,... | collective-permute-start | bytes 1572872 | tf_op jit(solution)/shard_map/ppermute | solution.py:54
  47.5 3.4 %collective-permute-done.26.refs_18_ = bf16[512,512]{1,0:T(8,128)(2,1)S(1)} collective-permute-done((bf16[512,512]{1,0:T(8,128)(2,1)S(1)}, bf16[512,512]{1,0:T(8,128)(2,1)S(1)}, u32[]{:S(2)}, u32[]{:S(2)}) %collective-permute-start.26) | collective-permute-done | bytes 524320 | tf_op jit(solution)/shard_map/ppermute | solution.py:54
  50.9 3.4 %collective-permute-start.11 = (bf16[512,512]{1,0:T(8,128)(2,1)S(1)}, bf16[512,512]{1,0:T(8,128)(2,1)}, u32[]{:S(2)}, u32[]{:S(2)}) collective-permute-start(bf16[512,512]{1,0:T(8,128)(2,1)S(1)} %collective-permute-done.10.refs_17_), channel_id=1, source_target_pairs={{0,16},{1,17},{2,18},{3,19},{4,52},{5,53},{6,54},{7,55},{8,24},{9,... | collective-permute-start | bytes 1572872 | tf_op jit(solution)/shard_map/ppermute | solution.py:54
  54.3 2.9 %collective-permute-start.19 = (bf16[2,512,512]{2,1,0:T(8,128)(2,1)S(1)}, bf16[2,512,512]{2,1,0:T(8,128)(2,1)S(1)}, u32[]{:S(2)}, u32[]{:S(2)}) collective-permute-start(bf16[2,512,512]{2,1,0:T(8,128)(2,1)S(1)} %collective-permute-done.18.refs_1_.refs_5_), channel_id=1, source_target_pairs={{0,1},{1,2},{2,3},{3,0},{4,7},{5,4},{6,5},{7,6},{8,9},{9,10},{10,1... | collective-permute-start | bytes 3145736 | tf_op jit(solution)/shard_map/ppermute | solution.py:54
  57.2 1.8 %collective-permute-done.13.refs_20_ = bf16[512,512]{1,0:T(8,128)(2,1)S(1)} collective-permute-done((bf16[512,512]{1,0:T(8,128)(2,1)S(1)}, bf16[512,512]{1,0:T(8,128)(2,1)S(1)}, u32[]{:S(2)}, u32[]{:S(2)}) %collective-permute-start.13) | collective-permute-done | bytes 524320 | tf_op jit(solution)/shard_map/ppermute | solution.py:54
  59.0 2.1 %collective-permute-start.5 = (bf16[2,512,512]{2,1,0:T(8,128)(2,1)S(1)}, bf16[2,512,512]{2,1,0:T(8,128)(2,1)S(1)}, u32[]{:S(2)}, u32[]{:S(2)}) collective-permute-start(bf16[2,512,512]{2,1,0:T(8,128)(2,1)S(1)} %pad_maximum_fusion.refs_0_.refs_4_), channel_id=1, source_target_pairs={{0,4},{1,5},{2,6},{3,7},{4,0},{5,1},{6,2},{7,3},{8,12},{9,13},{10,... | collective-permute-start | bytes 3145736 | tf_op jit(solution)/shard_map/ppermute | solution.py:54
  61.2 0.0 collective-permute-done.11.refs_18_
  61.2 3.1 %collective-permute-start.27 = (bf16[512,512]{1,0:T(8,128)(2,1)S(1)}, bf16[512,512]{1,0:T(8,128)(2,1)S(1)}, u32[]{:S(2)}, u32[]{:S(2)}) collective-permute-start(bf16[512,512]{1,0:T(8,128)(2,1)S(1)} %collective-permute-done.26.refs_18_), channel_id=1, source_target_pairs={{0,16},{1,17},{2,18},{3,19},{4,52},{5,53},{6,54},{7,55},{8,24},{9,... | collective-permute-start | bytes 1572872 | tf_op jit(solution)/shard_map/ppermute | solution.py:54
  64.2 0.0 collective-permute-done.2.refs_1_.refs_5_
  64.3 2.5 %collective-permute-start.3 = (bf16[2,512,512]{2,1,0:T(8,128)(2,1)S(1)}, bf16[2,512,512]{2,1,0:T(8,128)(2,1)}, u32[]{:S(2)}, u32[]{:S(2)}) collective-permute-start(bf16[2,512,512]{2,1,0:T(8,128)(2,1)S(1)} %collective-permute-done.2.refs_1_.refs_5_), channel_id=1, source_target_pairs={{0,1},{1,2},{2,3},{3,0},{4,7},{5,4},{6,5},{7,6},{8,9},{9,10},{10,1... | collective-permute-start | bytes 3145736 | tf_op jit(solution)/shard_map/ppermute | solution.py:54
  66.7 5.0 %collective-permute-done.28.refs_20_ = bf16[512,512]{1,0:T(8,128)(2,1)S(1)} collective-permute-done((bf16[512,512]{1,0:T(8,128)(2,1)S(1)}, bf16[512,512]{1,0:T(8,128)(2,1)S(1)}, u32[]{:S(2)}, u32[]{:S(2)}) %collective-permute-start.28) | collective-permute-done | bytes 524320 | tf_op jit(solution)/shard_map/ppermute | solution.py:54
  71.7 2.2 %collective-permute-start.14 = (bf16[512,512]{1,0:T(8,128)(2,1)S(1)}, bf16[512,512]{1,0:T(8,128)(2,1)S(1)}, u32[]{:S(2)}, u32[]{:S(2)}) collective-permute-start(bf16[512,512]{1,0:T(8,128)(2,1)S(1)} %collective-permute-done.13.refs_20_), channel_id=1, source_target_pairs={{0,16},{1,17},{2,18},{3,19},{4,52},{5,53},{6,54},{7,55},{8,24},{9,... | collective-permute-start | bytes 1572872 | tf_op jit(solution)/shard_map/ppermute | solution.py:54
  73.9 0.0 collective-permute-done.27.refs_19_
  73.9 0.0 collective-permute-start.22
  73.9 0.0 collective-permute-done.19.refs_2_.refs_6_
  73.9 1.5 %collective-permute-start.20 = (bf16[2,512,512]{2,1,0:T(8,128)(2,1)S(1)}, bf16[2,512,512]{2,1,0:T(8,128)(2,1)S(1)}, u32[]{:S(2)}, u32[]{:S(2)}) collective-permute-start(bf16[2,512,512]{2,1,0:T(8,128)(2,1)S(1)} %collective-permute-done.19.refs_2_.refs_6_), channel_id=1, source_target_pairs={{0,1},{1,2},{2,3},{3,0},{4,7},{5,4},{6,5},{7,6},{8,9},{9,10},{10,1... | collective-permute-start | bytes 3145736 | tf_op jit(solution)/shard_map/ppermute | solution.py:54
  75.4 4.8 %collective-permute-done.14.refs_21_ = bf16[512,512]{1,0:T(8,128)(2,1)S(1)} collective-permute-done((bf16[512,512]{1,0:T(8,128)(2,1)S(1)}, bf16[512,512]{1,0:T(8,128)(2,1)S(1)}, u32[]{:S(2)}, u32[]{:S(2)}) %collective-permute-start.14) | collective-permute-done | bytes 524320 | tf_op jit(solution)/shard_map/ppermute | solution.py:54
  80.1 3.3 %collective-permute-start.29 = (bf16[512,512]{1,0:T(8,128)(2,1)S(1)}, bf16[512,512]{1,0:T(8,128)(2,1)S(1)}, u32[]{:S(2)}, u32[]{:S(2)}) collective-permute-start(bf16[512,512]{1,0:T(8,128)(2,1)S(1)} %collective-permute-done.28.refs_20_), channel_id=1, source_target_pairs={{0,16},{1,17},{2,18},{3,19},{4,52},{5,53},{6,54},{7,55},{8,24},{9,... | collective-permute-start | bytes 1572872 | tf_op jit(solution)/shard_map/ppermute | solution.py:54
  83.5 0.0 collective-permute-done.5.refs_8_.refs_12_
  83.5 2.5 %collective-permute-start.31 = (bf16[512,512]{1,0:T(8,128)(2,1)S(1)}, bf16[512,512]{1,0:T(8,128)(2,1)S(1)}, u32[]{:S(2)}, u32[]{:S(2)}) collective-permute-start(bf16[512,512]{1,0:T(8,128)(2,1)S(1)} %collective-permute-done.27.refs_19_), channel_id=1, source_target_pairs={{0,64},{1,65},{2,66},{3,67},{4,68},{5,69},{6,70},{7,71},{8,72},{9,... | collective-permute-start | bytes 1572872 | tf_op jit(solution)/shard_map/ppermute | solution.py:54
  86.0 0.0 collective-permute-done.3.refs_2_.refs_6_
  86.0 0.4 collective-permute-start.4
  86.4 3.2 %collective-permute-done.29.refs_21_ = bf16[512,512]{1,0:T(8,128)(2,1)S(1)} collective-permute-done((bf16[512,512]{1,0:T(8,128)(2,1)S(1)}, bf16[512,512]{1,0:T(8,128)(2,1)S(1)}, u32[]{:S(2)}, u32[]{:S(2)}) %collective-permute-start.29) | collective-permute-done | bytes 524320 | tf_op jit(solution)/shard_map/ppermute | solution.py:54
  89.6 3.4 %collective-permute-start.15 = (bf16[512,512]{1,0:T(8,128)(2,1)S(1)}, bf16[512,512]{1,0:T(8,128)(2,1)}, u32[]{:S(2)}, u32[]{:S(2)}) collective-permute-start(bf16[512,512]{1,0:T(8,128)(2,1)S(1)} %collective-permute-done.14.refs_21_), channel_id=1, source_target_pairs={{0,16},{1,17},{2,18},{3,19},{4,52},{5,53},{6,54},{7,55},{8,24},{9,... | collective-permute-start | bytes 1572872 | tf_op jit(solution)/shard_map/ppermute | solution.py:54
  93.0 4.8 %collective-permute-done.31.refs_23_ = bf16[512,512]{1,0:T(8,128)(2,1)S(1)} collective-permute-done((bf16[512,512]{1,0:T(8,128)(2,1)S(1)}, bf16[512,512]{1,0:T(8,128)(2,1)S(1)}, u32[]{:S(2)}, u32[]{:S(2)}) %collective-permute-start.31) | collective-permute-done | bytes 524320 | tf_op jit(solution)/shard_map/ppermute | solution.py:54
  97.8 1.6 %collective-permute-start.30 = (bf16[512,512]{1,0:T(8,128)(2,1)S(1)}, bf16[512,512]{1,0:T(8,128)(2,1)S(1)}, u32[]{:S(2)}, u32[]{:S(2)}) collective-permute-start(bf16[512,512]{1,0:T(8,128)(2,1)S(1)} %collective-permute-done.29.refs_21_), channel_id=1, source_target_pairs={{0,16},{1,17},{2,18},{3,19},{4,52},{5,53},{6,54},{7,55},{8,24},{9,... | collective-permute-start | bytes 1572872 | tf_op jit(solution)/shard_map/ppermute | solution.py:54
  99.5 0.1 collective-permute-start.24
  99.6 0.0 collective-permute-done.15.refs_22_
  99.6 3.4 %collective-permute-start.6 = (bf16[2,512,512]{2,1,0:T(8,128)(2,1)S(1)}, bf16[2,512,512]{2,1,0:T(8,128)(2,1)}, u32[]{:S(2)}, u32[]{:S(2)}) collective-permute-start(bf16[2,512,512]{2,1,0:T(8,128)(2,1)S(1)} %collective-permute-done.2.refs_1_.refs_5_), channel_id=1, source_target_pairs={{0,4},{1,5},{2,6},{3,7},{4,0},{5,1},{6,2},{7,3},{8,12},{9,13},{10,... | collective-permute-start | bytes 3145736 | tf_op jit(solution)/shard_map/ppermute | solution.py:54
  103.0 3.2 %collective-permute-done.30.refs_22_ = bf16[512,512]{1,0:T(8,128)(2,1)S(1)} collective-permute-done((bf16[512,512]{1,0:T(8,128)(2,1)S(1)}, bf16[512,512]{1,0:T(8,128)(2,1)S(1)}, u32[]{:S(2)}, u32[]{:S(2)}) %collective-permute-start.30) | collective-permute-done | bytes 524320 | tf_op jit(solution)/shard_map/ppermute | solution.py:54
  106.2 2.5 %collective-permute-start.7 = (bf16[2,512,512]{2,1,0:T(8,128)(2,1)}, bf16[2,512,512]{2,1,0:T(8,128)(2,1)}, u32[]{:S(2)}, u32[]{:S(2)}) collective-permute-start(bf16[2,512,512]{2,1,0:T(8,128)(2,1)} %collective-permute-done.3.refs_2_.refs_6_), channel_id=1, source_target_pairs={{0,4},{1,5},{2,6},{3,7},{4,0},{5,1},{6,2},{7,3},{8,12},{9,13},{10,... | collective-permute-start | bytes 3145736 | tf_op jit(solution)/shard_map/ppermute | solution.py:54
  108.7 0.0 collective-permute-done.4.refs_3_.refs_7_
  108.7 0.1 collective-permute-start.8
  108.8 0.0 collective-permute-done.23.refs_10_.refs_14_
  108.8 0.5 collective-permute-start.12
  109.3 0.0 collective-permute-done.24.refs_11_.refs_15_
  109.3 0.5 copy-done.9
  109.8 0.4 collective-permute-start.16
  110.2 0.5 copy-done.10
  110.8 0.6 stack.41.place
  111.4 15.8 %shard_map.60 = bf16[2048,1024]{1,0:T(8,128)(2,1)} custom-call(s32[5]{0:T(128)} %stack.41.place, bf16[2,512,512]{2,1,0:T(8,128)(2,1)} %copy-done.1, bf16[2,512,512]{2,1,0:T(8,128)(2,1)} %copy-done.3, bf16[2,512,512]{2,1,0:T(8,128)(2,1)} %copy-done.6, bf16[2,512,512]{2,1,0:T(8,128)(2,1)} %copy-done.8, bf16[2,512,512]{2,1,0:T(8,128)(2,1)} %copy-done.1, ...), custom_call_target="tpu_custom_call" | custom-call | flops 1000 | bytes 1000 | tf_op jit(solution)/shard_map/pallas_call | solution.py:128
  127.2 0.0 collective-permute-done.6.refs_9_.refs_13_
  127.2 0.0 collective-permute-done.16.refs_23_
  127.2 0.0 collective-permute-done.8.refs_11_.refs_15_
  127.2 15.8 %shard_map.59 = bf16[2048,1024]{1,0:T(8,128)(2,1)} custom-call(s32[5]{0:T(128)} %stack.41.place, bf16[2,512,512]{2,1,0:T(8,128)(2,1)} %copy-done, bf16[2,512,512]{2,1,0:T(8,128)(2,1)} %copy-done.2, bf16[2,512,512]{2,1,0:T(8,128)(2,1)} %collective-permute-done.3.refs_2_.refs_6_, bf16[2,512,512]{2,1,0:T(8,128)(2,1)} %collective-permute-done.4.refs_3_.refs_7_, ...), custom_call_target="tpu_custom_call" | custom-call | flops 1000 | bytes 1000 | tf_op jit(solution)/shard_map/pallas_call | solution.py:128
  (51 shorter events, 0.1 us)
Async XLA Ops:
  0.6 19.0 %collective-permute-start = (bf16[512,512]{1,0:T(8,128)(2,1)}, bf16[512,512]{1,0:T(8,128)(2,1)S(1)}, u32[]{:S(2)}, u32[]{:S(2)}) collective-permute-start(bf16[512,512]{1,0:T(8,128)(2,1)} %param.5), channel_id=1, source_target_pairs={{0,32},{1,48},{2,0},{3,16},{4,96},{5,112},{6,64},{7,80},{8,81},{9,... | collective-permute-start | bytes 1572872 | tf_op jit(solution)/shard_map/ppermute | solution.py:54
  7.5 24.5 %collective-permute-start.17 = (bf16[512,512]{1,0:T(8,128)(2,1)}, bf16[512,512]{1,0:T(8,128)(2,1)S(1)}, u32[]{:S(2)}, u32[]{:S(2)}) collective-permute-start(bf16[512,512]{1,0:T(8,128)(2,1)} %param.5), channel_id=1, source_target_pairs={{0,8},{1,9},{2,10},{3,11},{4,12},{5,13},{6,14},{7,15},{8,0},{9,1},... | collective-permute-start | bytes 1572872 | tf_op jit(solution)/shard_map/ppermute | solution.py:54
  7.5 26.9 %collective-permute-start.9 = (bf16[512,512]{1,0:T(8,128)(2,1)}, bf16[512,512]{1,0:T(8,128)(2,1)S(1)}, u32[]{:S(2)}, u32[]{:S(2)}) collective-permute-start(bf16[512,512]{1,0:T(8,128)(2,1)} %param.4), channel_id=1, source_target_pairs={{0,32},{1,48},{2,0},{3,16},{4,96},{5,112},{6,64},{7,80},{8,81},{9,... | collective-permute-start | bytes 1572872 | tf_op jit(solution)/shard_map/ppermute | solution.py:54
  19.6 90.6 %copy-start.12 = (bf16[512,512]{1,0:T(8,128)(2,1)}, bf16[512,512]{1,0:T(8,128)(2,1)S(1)}, u32[]{:S(2)}) copy-start(bf16[512,512]{1,0:T(8,128)(2,1)S(1)} %collective-permute-done.refs_16_) | copy-start | bytes 1572868
  19.6 19.6 %collective-permute-start.25 = (bf16[512,512]{1,0:T(8,128)(2,1)S(1)}, bf16[512,512]{1,0:T(8,128)(2,1)S(1)}, u32[]{:S(2)}, u32[]{:S(2)}) collective-permute-start(bf16[512,512]{1,0:T(8,128)(2,1)S(1)} %collective-permute-done.refs_16_), channel_id=1, source_target_pairs={{0,16},{1,17},{2,18},{3,19},{4,52},{5,53},{6,54},{7,55},{8,24},{9,... | collective-permute-start | bytes 1572872 | tf_op jit(solution)/shard_map/ppermute | solution.py:54
  21.3 21.4 %collective-permute-start.1 = (bf16[512,512]{1,0:T(8,128)(2,1)}, bf16[512,512]{1,0:T(8,128)(2,1)S(1)}, u32[]{:S(2)}, u32[]{:S(2)}) collective-permute-start(bf16[512,512]{1,0:T(8,128)(2,1)} %param.4), channel_id=1, source_target_pairs={{0,8},{1,9},{2,10},{3,11},{4,12},{5,13},{6,14},{7,15},{8,0},{9,1},... | collective-permute-start | bytes 1572872 | tf_op jit(solution)/shard_map/ppermute | solution.py:54
  33.1 78.2 %copy-start.1 = (bf16[2,512,512]{2,1,0:T(8,128)(2,1)}, bf16[2,512,512]{2,1,0:T(8,128)(2,1)S(1)}, u32[]{:S(2)}) copy-start(bf16[2,512,512]{2,1,0:T(8,128)(2,1)S(1)} %pad_maximum_fusion.1.refs_0_.refs_4_) | copy-start | bytes 3145732
  33.2 21.2 %collective-permute-start.18 = (bf16[2,512,512]{2,1,0:T(8,128)(2,1)S(1)}, bf16[2,512,512]{2,1,0:T(8,128)(2,1)S(1)}, u32[]{:S(2)}, u32[]{:S(2)}) collective-permute-start(bf16[2,512,512]{2,1,0:T(8,128)(2,1)S(1)} %pad_maximum_fusion.1.refs_0_.refs_4_), channel_id=1, source_target_pairs={{0,1},{1,2},{2,3},{3,0},{4,7},{5,4},{6,5},{7,6},{8,9},{9,10},{10,1... | collective-permute-start | bytes 3145736 | tf_op jit(solution)/shard_map/ppermute | solution.py:54
  33.2 23.9 %collective-permute-start.21 = (bf16[2,512,512]{2,1,0:T(8,128)(2,1)S(1)}, bf16[2,512,512]{2,1,0:T(8,128)(2,1)S(1)}, u32[]{:S(2)}, u32[]{:S(2)}) collective-permute-start(bf16[2,512,512]{2,1,0:T(8,128)(2,1)S(1)} %pad_maximum_fusion.1.refs_0_.refs_4_), channel_id=1, source_target_pairs={{0,4},{1,5},{2,6},{3,7},{4,0},{5,1},{6,2},{7,3},{8,12},{9,13},{10,... | collective-permute-start | bytes 3145736 | tf_op jit(solution)/shard_map/ppermute | solution.py:54
  34.4 75.8 %copy-start.11 = (bf16[512,512]{1,0:T(8,128)(2,1)}, bf16[512,512]{1,0:T(8,128)(2,1)S(1)}, u32[]{:S(2)}) copy-start(bf16[512,512]{1,0:T(8,128)(2,1)S(1)} %collective-permute-done.9.refs_16_) | copy-start | bytes 1572868
  34.4 10.9 %collective-permute-start.10 = (bf16[512,512]{1,0:T(8,128)(2,1)S(1)}, bf16[512,512]{1,0:T(8,128)(2,1)S(1)}, u32[]{:S(2)}, u32[]{:S(2)}) collective-permute-start(bf16[512,512]{1,0:T(8,128)(2,1)S(1)} %collective-permute-done.9.refs_16_), channel_id=1, source_target_pairs={{0,16},{1,17},{2,18},{3,19},{4,52},{5,53},{6,54},{7,55},{8,24},{9,... | collective-permute-start | bytes 1572872 | tf_op jit(solution)/shard_map/ppermute | solution.py:54
  39.2 71.0 %copy-start.14 = (bf16[512,512]{1,0:T(8,128)(2,1)}, bf16[512,512]{1,0:T(8,128)(2,1)S(1)}, u32[]{:S(2)}) copy-start(bf16[512,512]{1,0:T(8,128)(2,1)S(1)} %collective-permute-done.25.refs_17_) | copy-start | bytes 1572868
  39.2 11.8 %collective-permute-start.26 = (bf16[512,512]{1,0:T(8,128)(2,1)S(1)}, bf16[512,512]{1,0:T(8,128)(2,1)S(1)}, u32[]{:S(2)}, u32[]{:S(2)}) collective-permute-start(bf16[512,512]{1,0:T(8,128)(2,1)S(1)} %collective-permute-done.25.refs_17_), channel_id=1, source_target_pairs={{0,16},{1,17},{2,18},{3,19},{4,52},{5,53},{6,54},{7,55},{8,24},{9,... | collective-permute-start | bytes 1572872 | tf_op jit(solution)/shard_map/ppermute | solution.py:54
  43.9 83.3 %copy-start = (bf16[2,512,512]{2,1,0:T(8,128)(2,1)}, bf16[2,512,512]{2,1,0:T(8,128)(2,1)S(1)}, u32[]{:S(2)}) copy-start(bf16[2,512,512]{2,1,0:T(8,128)(2,1)S(1)} %pad_maximum_fusion.refs_0_.refs_4_) | copy-start | bytes 3145732
  43.9 20.4 %collective-permute-start.2 = (bf16[2,512,512]{2,1,0:T(8,128)(2,1)S(1)}, bf16[2,512,512]{2,1,0:T(8,128)(2,1)S(1)}, u32[]{:S(2)}, u32[]{:S(2)}) collective-permute-start(bf16[2,512,512]{2,1,0:T(8,128)(2,1)S(1)} %pad_maximum_fusion.refs_0_.refs_4_), channel_id=1, source_target_pairs={{0,1},{1,2},{2,3},{3,0},{4,7},{5,4},{6,5},{7,6},{8,9},{9,10},{10,1... | collective-permute-start | bytes 3145736 | tf_op jit(solution)/shard_map/ppermute | solution.py:54
  45.3 64.9 %copy-start.13 = (bf16[512,512]{1,0:T(8,128)(2,1)}, bf16[512,512]{1,0:T(8,128)(2,1)S(1)}, u32[]{:S(2)}) copy-start(bf16[512,512]{1,0:T(8,128)(2,1)S(1)} %collective-permute-done.10.refs_17_) | copy-start | bytes 1572868
  45.3 13.7 %collective-permute-start.13 = (bf16[512,512]{1,0:T(8,128)(2,1)S(1)}, bf16[512,512]{1,0:T(8,128)(2,1)S(1)}, u32[]{:S(2)}, u32[]{:S(2)}) collective-permute-start(bf16[512,512]{1,0:T(8,128)(2,1)S(1)} %collective-permute-done.9.refs_16_), channel_id=1, source_target_pairs={{0,64},{1,65},{2,66},{3,67},{4,68},{5,69},{6,70},{7,71},{8,72},{9,... | collective-permute-start | bytes 1572872 | tf_op jit(solution)/shard_map/ppermute | solution.py:54
  50.9 59.3 %copy-start.16 = (bf16[512,512]{1,0:T(8,128)(2,1)}, bf16[512,512]{1,0:T(8,128)(2,1)S(1)}, u32[]{:S(2)}) copy-start(bf16[512,512]{1,0:T(8,128)(2,1)S(1)} %collective-permute-done.26.refs_18_) | copy-start | bytes 1572868
  50.9 10.2 %collective-permute-start.11 = (bf16[512,512]{1,0:T(8,128)(2,1)S(1)}, bf16[512,512]{1,0:T(8,128)(2,1)}, u32[]{:S(2)}, u32[]{:S(2)}) collective-permute-start(bf16[512,512]{1,0:T(8,128)(2,1)S(1)} %collective-permute-done.10.refs_17_), channel_id=1, source_target_pairs={{0,16},{1,17},{2,18},{3,19},{4,52},{5,53},{6,54},{7,55},{8,24},{9,... | collective-permute-start | bytes 1572872 | tf_op jit(solution)/shard_map/ppermute | solution.py:54
  54.3 45.2 %copy-start.3 = (bf16[2,512,512]{2,1,0:T(8,128)(2,1)}, bf16[2,512,512]{2,1,0:T(8,128)(2,1)S(1)}, u32[]{:S(2)}) copy-start(bf16[2,512,512]{2,1,0:T(8,128)(2,1)S(1)} %collective-permute-done.18.refs_1_.refs_5_) | copy-start | bytes 3145732
  54.3 19.6 %collective-permute-start.19 = (bf16[2,512,512]{2,1,0:T(8,128)(2,1)S(1)}, bf16[2,512,512]{2,1,0:T(8,128)(2,1)S(1)}, u32[]{:S(2)}, u32[]{:S(2)}) collective-permute-start(bf16[2,512,512]{2,1,0:T(8,128)(2,1)S(1)} %collective-permute-done.18.refs_1_.refs_5_), channel_id=1, source_target_pairs={{0,1},{1,2},{2,3},{3,0},{4,7},{5,4},{6,5},{7,6},{8,9},{9,10},{10,1... | collective-permute-start | bytes 3145736 | tf_op jit(solution)/shard_map/ppermute | solution.py:54
  57.2 42.4 %copy-start.4 = (bf16[2,512,512]{2,1,0:T(8,128)(2,1)}, bf16[2,512,512]{2,1,0:T(8,128)(2,1)S(1)}, u32[]{:S(2)}) copy-start(bf16[2,512,512]{2,1,0:T(8,128)(2,1)S(1)} %collective-permute-done.21.refs_8_.refs_12_) | copy-start | bytes 3145732
  57.2 14.5 %collective-permute-start.28 = (bf16[512,512]{1,0:T(8,128)(2,1)S(1)}, bf16[512,512]{1,0:T(8,128)(2,1)S(1)}, u32[]{:S(2)}, u32[]{:S(2)}) collective-permute-start(bf16[512,512]{1,0:T(8,128)(2,1)S(1)} %collective-permute-done.refs_16_), channel_id=1, source_target_pairs={{0,64},{1,65},{2,66},{3,67},{4,68},{5,69},{6,70},{7,71},{8,72},{9,... | collective-permute-start | bytes 1572872 | tf_op jit(solution)/shard_map/ppermute | solution.py:54
  59.0 34.0 %copy-start.15 = (bf16[512,512]{1,0:T(8,128)(2,1)}, bf16[512,512]{1,0:T(8,128)(2,1)S(1)}, u32[]{:S(2)}) copy-start(bf16[512,512]{1,0:T(8,128)(2,1)S(1)} %collective-permute-done.13.refs_20_) | copy-start | bytes 1572868
  59.0 24.5 %collective-permute-start.5 = (bf16[2,512,512]{2,1,0:T(8,128)(2,1)S(1)}, bf16[2,512,512]{2,1,0:T(8,128)(2,1)S(1)}, u32[]{:S(2)}, u32[]{:S(2)}) collective-permute-start(bf16[2,512,512]{2,1,0:T(8,128)(2,1)S(1)} %pad_maximum_fusion.refs_0_.refs_4_), channel_id=1, source_target_pairs={{0,4},{1,5},{2,6},{3,7},{4,0},{5,1},{6,2},{7,3},{8,12},{9,13},{10,... | collective-permute-start | bytes 3145736 | tf_op jit(solution)/shard_map/ppermute | solution.py:54
  61.2 12.7 %collective-permute-start.27 = (bf16[512,512]{1,0:T(8,128)(2,1)S(1)}, bf16[512,512]{1,0:T(8,128)(2,1)S(1)}, u32[]{:S(2)}, u32[]{:S(2)}) collective-permute-start(bf16[512,512]{1,0:T(8,128)(2,1)S(1)} %collective-permute-done.26.refs_18_), channel_id=1, source_target_pairs={{0,16},{1,17},{2,18},{3,19},{4,52},{5,53},{6,54},{7,55},{8,24},{9,... | collective-permute-start | bytes 1572872 | tf_op jit(solution)/shard_map/ppermute | solution.py:54
  64.2 62.9 %copy-start.2 = (bf16[2,512,512]{2,1,0:T(8,128)(2,1)}, bf16[2,512,512]{2,1,0:T(8,128)(2,1)S(1)}, u32[]{:S(2)}) copy-start(bf16[2,512,512]{2,1,0:T(8,128)(2,1)S(1)} %collective-permute-done.2.refs_1_.refs_5_) | copy-start | bytes 3145732
  64.3 21.7 %collective-permute-start.3 = (bf16[2,512,512]{2,1,0:T(8,128)(2,1)S(1)}, bf16[2,512,512]{2,1,0:T(8,128)(2,1)}, u32[]{:S(2)}, u32[]{:S(2)}) collective-permute-start(bf16[2,512,512]{2,1,0:T(8,128)(2,1)S(1)} %collective-permute-done.2.refs_1_.refs_5_), channel_id=1, source_target_pairs={{0,1},{1,2},{2,3},{3,0},{4,7},{5,4},{6,5},{7,6},{8,9},{9,10},{10,1... | collective-permute-start | bytes 3145736 | tf_op jit(solution)/shard_map/ppermute | solution.py:54
  71.7 21.3 %copy-start.18 = (bf16[512,512]{1,0:T(8,128)(2,1)}, bf16[512,512]{1,0:T(8,128)(2,1)S(1)}, u32[]{:S(2)}) copy-start(bf16[512,512]{1,0:T(8,128)(2,1)S(1)} %collective-permute-done.28.refs_20_) | copy-start | bytes 1572868
  71.7 8.4 %collective-permute-start.14 = (bf16[512,512]{1,0:T(8,128)(2,1)S(1)}, bf16[512,512]{1,0:T(8,128)(2,1)S(1)}, u32[]{:S(2)}, u32[]{:S(2)}) collective-permute-start(bf16[512,512]{1,0:T(8,128)(2,1)S(1)} %collective-permute-done.13.refs_20_), channel_id=1, source_target_pairs={{0,16},{1,17},{2,18},{3,19},{4,52},{5,53},{6,54},{7,55},{8,24},{9,... | collective-permute-start | bytes 1572872 | tf_op jit(solution)/shard_map/ppermute | solution.py:54
  73.9 25.6 %copy-start.19 = (bf16[512,512]{1,0:T(8,128)(2,1)}, bf16[512,512]{1,0:T(8,128)(2,1)S(1)}, u32[]{:S(2)}) copy-start(bf16[512,512]{1,0:T(8,128)(2,1)S(1)} %collective-permute-done.27.refs_19_) | copy-start | bytes 1572868
  73.9 23.9 %collective-permute-start.22 = (bf16[2,512,512]{2,1,0:T(8,128)(2,1)S(1)}, bf16[2,512,512]{2,1,0:T(8,128)(2,1)S(1)}, u32[]{:S(2)}, u32[]{:S(2)}) collective-permute-start(bf16[2,512,512]{2,1,0:T(8,128)(2,1)S(1)} %collective-permute-done.18.refs_1_.refs_5_), channel_id=1, source_target_pairs={{0,4},{1,5},{2,6},{3,7},{4,0},{5,1},{6,2},{7,3},{8,12},{9,13},{10,... | collective-permute-start | bytes 3145736 | tf_op jit(solution)/shard_map/ppermute | solution.py:54
  73.9 32.3 %copy-start.6 = (bf16[2,512,512]{2,1,0:T(8,128)(2,1)}, bf16[2,512,512]{2,1,0:T(8,128)(2,1)S(1)}, u32[]{:S(2)}) copy-start(bf16[2,512,512]{2,1,0:T(8,128)(2,1)S(1)} %collective-permute-done.19.refs_2_.refs_6_) | copy-start | bytes 3145732
  73.9 25.6 %collective-permute-start.20 = (bf16[2,512,512]{2,1,0:T(8,128)(2,1)S(1)}, bf16[2,512,512]{2,1,0:T(8,128)(2,1)S(1)}, u32[]{:S(2)}, u32[]{:S(2)}) collective-permute-start(bf16[2,512,512]{2,1,0:T(8,128)(2,1)S(1)} %collective-permute-done.19.refs_2_.refs_6_), channel_id=1, source_target_pairs={{0,1},{1,2},{2,3},{3,0},{4,7},{5,4},{6,5},{7,6},{8,9},{9,10},{10,1... | collective-permute-start | bytes 3145736 | tf_op jit(solution)/shard_map/ppermute | solution.py:54
  80.1 30.1 %copy-start.17 = (bf16[512,512]{1,0:T(8,128)(2,1)}, bf16[512,512]{1,0:T(8,128)(2,1)S(1)}, u32[]{:S(2)}) copy-start(bf16[512,512]{1,0:T(8,128)(2,1)S(1)} %collective-permute-done.14.refs_21_) | copy-start | bytes 1572868
  80.1 9.5 %collective-permute-start.29 = (bf16[512,512]{1,0:T(8,128)(2,1)S(1)}, bf16[512,512]{1,0:T(8,128)(2,1)S(1)}, u32[]{:S(2)}, u32[]{:S(2)}) collective-permute-start(bf16[512,512]{1,0:T(8,128)(2,1)S(1)} %collective-permute-done.28.refs_20_), channel_id=1, source_target_pairs={{0,16},{1,17},{2,18},{3,19},{4,52},{5,53},{6,54},{7,55},{8,24},{9,... | collective-permute-start | bytes 1572872 | tf_op jit(solution)/shard_map/ppermute | solution.py:54
  83.5 19.5 %copy-start.5 = (bf16[2,512,512]{2,1,0:T(8,128)(2,1)}, bf16[2,512,512]{2,1,0:T(8,128)(2,1)S(1)}, u32[]{:S(2)}) copy-start(bf16[2,512,512]{2,1,0:T(8,128)(2,1)S(1)} %collective-permute-done.5.refs_8_.refs_12_) | copy-start | bytes 3145732
  83.5 14.3 %collective-permute-start.31 = (bf16[512,512]{1,0:T(8,128)(2,1)S(1)}, bf16[512,512]{1,0:T(8,128)(2,1)S(1)}, u32[]{:S(2)}, u32[]{:S(2)}) collective-permute-start(bf16[512,512]{1,0:T(8,128)(2,1)S(1)} %collective-permute-done.27.refs_19_), channel_id=1, source_target_pairs={{0,64},{1,65},{2,66},{3,67},{4,68},{5,69},{6,70},{7,71},{8,72},{9,... | collective-permute-start | bytes 1572872 | tf_op jit(solution)/shard_map/ppermute | solution.py:54
  86.0 22.8 %collective-permute-start.4 = (bf16[2,512,512]{2,1,0:T(8,128)(2,1)}, bf16[2,512,512]{2,1,0:T(8,128)(2,1)}, u32[]{:S(2)}, u32[]{:S(2)}) collective-permute-start(bf16[2,512,512]{2,1,0:T(8,128)(2,1)} %collective-permute-done.3.refs_2_.refs_6_), channel_id=1, source_target_pairs={{0,1},{1,2},{2,3},{3,0},{4,7},{5,4},{6,5},{7,6},{8,9},{9,10},{10,1... | collective-permute-start | bytes 3145736 | tf_op jit(solution)/shard_map/ppermute | solution.py:54
  89.6 20.6 %copy-start.20 = (bf16[512,512]{1,0:T(8,128)(2,1)}, bf16[512,512]{1,0:T(8,128)(2,1)S(1)}, u32[]{:S(2)}) copy-start(bf16[512,512]{1,0:T(8,128)(2,1)S(1)} %collective-permute-done.29.refs_21_) | copy-start | bytes 1572868
  89.6 9.9 %collective-permute-start.15 = (bf16[512,512]{1,0:T(8,128)(2,1)S(1)}, bf16[512,512]{1,0:T(8,128)(2,1)}, u32[]{:S(2)}, u32[]{:S(2)}) collective-permute-start(bf16[512,512]{1,0:T(8,128)(2,1)S(1)} %collective-permute-done.14.refs_21_), channel_id=1, source_target_pairs={{0,16},{1,17},{2,18},{3,19},{4,52},{5,53},{6,54},{7,55},{8,24},{9,... | collective-permute-start | bytes 1572872 | tf_op jit(solution)/shard_map/ppermute | solution.py:54
  97.8 1.6 %copy-start.21 = (bf16[512,512]{1,0:T(8,128)(2,1)}, bf16[512,512]{1,0:T(8,128)(2,1)S(1)}, u32[]{:S(2)}) copy-start(bf16[512,512]{1,0:T(8,128)(2,1)S(1)} %collective-permute-done.31.refs_23_) | copy-start | bytes 1572868
  97.8 11.0 %collective-permute-start.23 = (bf16[2,512,512]{2,1,0:T(8,128)(2,1)S(1)}, bf16[2,512,512]{2,1,0:T(8,128)(2,1)S(1)}, u32[]{:S(2)}, u32[]{:S(2)}) collective-permute-start(bf16[2,512,512]{2,1,0:T(8,128)(2,1)S(1)} %collective-permute-done.19.refs_2_.refs_6_), channel_id=1, source_target_pairs={{0,4},{1,5},{2,6},{3,7},{4,0},{5,1},{6,2},{7,3},{8,12},{9,13},{10,... | collective-permute-start | bytes 3145736 | tf_op jit(solution)/shard_map/ppermute | solution.py:54
  97.8 11.0 %copy-start.7 = (bf16[2,512,512]{2,1,0:T(8,128)(2,1)}, bf16[2,512,512]{2,1,0:T(8,128)(2,1)S(1)}, u32[]{:S(2)}) copy-start(bf16[2,512,512]{2,1,0:T(8,128)(2,1)S(1)} %collective-permute-done.22.refs_9_.refs_13_) | copy-start | bytes 3145732
  97.8 8.4 %collective-permute-start.30 = (bf16[512,512]{1,0:T(8,128)(2,1)S(1)}, bf16[512,512]{1,0:T(8,128)(2,1)S(1)}, u32[]{:S(2)}, u32[]{:S(2)}) collective-permute-start(bf16[512,512]{1,0:T(8,128)(2,1)S(1)} %collective-permute-done.29.refs_21_), channel_id=1, source_target_pairs={{0,16},{1,17},{2,18},{3,19},{4,52},{5,53},{6,54},{7,55},{8,24},{9,... | collective-permute-start | bytes 1572872 | tf_op jit(solution)/shard_map/ppermute | solution.py:54
  99.4 9.8 %copy-start.8 = (bf16[2,512,512]{2,1,0:T(8,128)(2,1)}, bf16[2,512,512]{2,1,0:T(8,128)(2,1)S(1)}, u32[]{:S(2)}) copy-start(bf16[2,512,512]{2,1,0:T(8,128)(2,1)S(1)} %collective-permute-done.20.refs_3_.refs_7_) | copy-start | bytes 3145732
  99.5 9.8 %collective-permute-start.24 = (bf16[2,512,512]{2,1,0:T(8,128)(2,1)S(1)}, bf16[2,512,512]{2,1,0:T(8,128)(2,1)S(1)}, u32[]{:S(2)}, u32[]{:S(2)}) collective-permute-start(bf16[2,512,512]{2,1,0:T(8,128)(2,1)S(1)} %collective-permute-done.20.refs_3_.refs_7_), channel_id=1, source_target_pairs={{0,4},{1,5},{2,6},{3,7},{4,0},{5,1},{6,2},{7,3},{8,12},{9,13},{10,... | collective-permute-start | bytes 3145736 | tf_op jit(solution)/shard_map/ppermute | solution.py:54
  99.6 27.6 %collective-permute-start.6 = (bf16[2,512,512]{2,1,0:T(8,128)(2,1)S(1)}, bf16[2,512,512]{2,1,0:T(8,128)(2,1)}, u32[]{:S(2)}, u32[]{:S(2)}) collective-permute-start(bf16[2,512,512]{2,1,0:T(8,128)(2,1)S(1)} %collective-permute-done.2.refs_1_.refs_5_), channel_id=1, source_target_pairs={{0,4},{1,5},{2,6},{3,7},{4,0},{5,1},{6,2},{7,3},{8,12},{9,13},{10,... | collective-permute-start | bytes 3145736 | tf_op jit(solution)/shard_map/ppermute | solution.py:54
  106.2 4.0 %copy-start.22 = (bf16[512,512]{1,0:T(8,128)(2,1)}, bf16[512,512]{1,0:T(8,128)(2,1)S(1)}, u32[]{:S(2)}) copy-start(bf16[512,512]{1,0:T(8,128)(2,1)S(1)} %collective-permute-done.30.refs_22_) | copy-start | bytes 1572868
  106.2 21.0 %collective-permute-start.7 = (bf16[2,512,512]{2,1,0:T(8,128)(2,1)}, bf16[2,512,512]{2,1,0:T(8,128)(2,1)}, u32[]{:S(2)}, u32[]{:S(2)}) collective-permute-start(bf16[2,512,512]{2,1,0:T(8,128)(2,1)} %collective-permute-done.3.refs_2_.refs_6_), channel_id=1, source_target_pairs={{0,4},{1,5},{2,6},{3,7},{4,0},{5,1},{6,2},{7,3},{8,12},{9,13},{10,... | collective-permute-start | bytes 3145736 | tf_op jit(solution)/shard_map/ppermute | solution.py:54
  108.7 18.5 %collective-permute-start.8 = (bf16[2,512,512]{2,1,0:T(8,128)(2,1)}, bf16[2,512,512]{2,1,0:T(8,128)(2,1)}, u32[]{:S(2)}, u32[]{:S(2)}) collective-permute-start(bf16[2,512,512]{2,1,0:T(8,128)(2,1)} %collective-permute-done.4.refs_3_.refs_7_), channel_id=1, source_target_pairs={{0,4},{1,5},{2,6},{3,7},{4,0},{5,1},{6,2},{7,3},{8,12},{9,13},{10,... | collective-permute-start | bytes 3145736 | tf_op jit(solution)/shard_map/ppermute | solution.py:54
  108.8 1.0 copy-start.9
  108.8 18.4 %collective-permute-start.12 = (bf16[512,512]{1,0:T(8,128)(2,1)}, bf16[512,512]{1,0:T(8,128)(2,1)}, u32[]{:S(2)}, u32[]{:S(2)}) collective-permute-start(bf16[512,512]{1,0:T(8,128)(2,1)} %collective-permute-done.11.refs_18_), channel_id=1, source_target_pairs={{0,16},{1,17},{2,18},{3,19},{4,52},{5,53},{6,54},{7,55},{8,24},{9,... | collective-permute-start | bytes 1572872 | tf_op jit(solution)/shard_map/ppermute | solution.py:54
  109.8 1.0 copy-start.10
  109.8 17.4 %collective-permute-start.16 = (bf16[512,512]{1,0:T(8,128)(2,1)}, bf16[512,512]{1,0:T(8,128)(2,1)}, u32[]{:S(2)}, u32[]{:S(2)}) collective-permute-start(bf16[512,512]{1,0:T(8,128)(2,1)} %collective-permute-done.15.refs_22_), channel_id=1, source_target_pairs={{0,16},{1,17},{2,18},{3,19},{4,52},{5,53},{6,54},{7,55},{8,24},{9,... | collective-permute-start | bytes 1572872 | tf_op jit(solution)/shard_map/ppermute | solution.py:54

commit v5 on v4

--- a/solution.py
+++ b/solution.py
@@ -108,7 +108,7 @@
     )
     out_ref[...] = (
         decay_rate * factor_ref[...].astype(jnp.float32)
-        + (1.0 - decay_rate) * (product / tokens)
+        + ((1.0 - decay_rate) / tokens) * product
     ).astype(out_ref.dtype)
 
 

time: 143 us -> 143 us (level)
  no operation moved by 1% of the time
where the time goes in v5:
time: 143 us
  starting transfers between devices  59 us (41%)
  waiting for transfers between devices  47.6 us (33%)
  Pallas kernels  31.4 us (22%)
  other arithmetic  2.28 us (2%)
  local copies, waits for them, and re-layouts  1.73 us (1%)
    ppermute x32, starting transfers between devices, send(): return lax.ppermute(block, AXES, moves)  59 us
    ppermute x32, waiting for transfers between devices, send(): return lax.ppermute(block, AXES, moves)  47.6 us
    pallas_call x2, Pallas kernels, update(): pl.pallas_call(functools.partial(update_kernel, tokens, factor_at, groups...  31.4 us
  transfers between devices with their start and end apart: 32, of which 11 were waited for; matrix products, arithmetic and copies ran while one was open for 2% of the time, Pallas kernels for 11%

profile of v5, /device:TPU:1, one launch (start us, length us, event | category | flops | bytes accessed | tf_op | source)
XLA Modules:
  0.0 143.0 jit_solution(13552470556400128519)
XLA Ops:
  0.6 6.8 %collective-permute-start = (bf16[512,512]{1,0:T(8,128)(2,1)}, bf16[512,512]{1,0:T(8,128)(2,1)S(1)}, u32[]{:S(2)}, u32[]{:S(2)}) collective-permute-start(bf16[512,512]{1,0:T(8,128)(2,1)} %param.5), channel_id=1, source_target_pairs={{0,32},{1,48},{2,0},{3,16},{4,96},{5,112},{6,64},{7,80},{8,81},{9,... | collective-permute-start | bytes 1572872 | tf_op jit(solution)/shard_map/ppermute | solution.py:54
  7.5 0.0 collective-permute-start.17
  7.5 3.3 %collective-permute-start.9 = (bf16[512,512]{1,0:T(8,128)(2,1)}, bf16[512,512]{1,0:T(8,128)(2,1)S(1)}, u32[]{:S(2)}, u32[]{:S(2)}) collective-permute-start(bf16[512,512]{1,0:T(8,128)(2,1)} %param.4), channel_id=1, source_target_pairs={{0,32},{1,48},{2,0},{3,16},{4,96},{5,112},{6,64},{7,80},{8,81},{9,... | collective-permute-start | bytes 1572872 | tf_op jit(solution)/shard_map/ppermute | solution.py:54
  10.7 8.9 %collective-permute-done.refs_16_ = bf16[512,512]{1,0:T(8,128)(2,1)S(1)} collective-permute-done((bf16[512,512]{1,0:T(8,128)(2,1)}, bf16[512,512]{1,0:T(8,128)(2,1)S(1)}, u32[]{:S(2)}, u32[]{:S(2)}) %collective-permute-start) | collective-permute-done | bytes 524320 | tf_op jit(solution)/shard_map/ppermute | solution.py:54
  19.6 1.7 %collective-permute-start.25 = (bf16[512,512]{1,0:T(8,128)(2,1)S(1)}, bf16[512,512]{1,0:T(8,128)(2,1)S(1)}, u32[]{:S(2)}, u32[]{:S(2)}) collective-permute-start(bf16[512,512]{1,0:T(8,128)(2,1)S(1)} %collective-permute-done.refs_16_), channel_id=1, source_target_pairs={{0,16},{1,17},{2,18},{3,19},{4,52},{5,53},{6,54},{7,55},{8,24},{9,... | collective-permute-start | bytes 1572872 | tf_op jit(solution)/shard_map/ppermute | solution.py:54
  21.3 2.5 %collective-permute-start.1 = (bf16[512,512]{1,0:T(8,128)(2,1)}, bf16[512,512]{1,0:T(8,128)(2,1)S(1)}, u32[]{:S(2)}, u32[]{:S(2)}) collective-permute-start(bf16[512,512]{1,0:T(8,128)(2,1)} %param.4), channel_id=1, source_target_pairs={{0,8},{1,9},{2,10},{3,11},{4,12},{5,13},{6,14},{7,15},{8,0},{9,1},... | collective-permute-start | bytes 1572872 | tf_op jit(solution)/shard_map/ppermute | solution.py:54
  23.8 8.2 %collective-permute-done.17 = bf16[512,512]{1,0:T(8,128)(2,1)S(1)} collective-permute-done((bf16[512,512]{1,0:T(8,128)(2,1)}, bf16[512,512]{1,0:T(8,128)(2,1)S(1)}, u32[]{:S(2)}, u32[]{:S(2)}) %collective-permute-start.17) | collective-permute-done | bytes 524320 | tf_op jit(solution)/shard_map/ppermute | solution.py:54
  32.0 1.1 pad_maximum_fusion.1.refs_0_.refs_4_
  33.1 0.0 copy-start.1
  33.2 0.1 collective-permute-start.18
  33.2 1.1 collective-permute-start.21
  34.4 0.0 collective-permute-done.9.refs_16_
  34.4 4.8 %collective-permute-start.10 = (bf16[512,512]{1,0:T(8,128)(2,1)S(1)}, bf16[512,512]{1,0:T(8,128)(2,1)S(1)}, u32[]{:S(2)}, u32[]{:S(2)}) collective-permute-start(bf16[512,512]{1,0:T(8,128)(2,1)S(1)} %collective-permute-done.9.refs_16_), channel_id=1, source_target_pairs={{0,16},{1,17},{2,18},{3,19},{4,52},{5,53},{6,54},{7,55},{8,24},{9,... | collective-permute-start | bytes 1572872 | tf_op jit(solution)/shard_map/ppermute | solution.py:54
  39.2 0.0 collective-permute-done.25.refs_17_
  39.2 0.1 collective-permute-start.26
  39.2 3.5 %collective-permute-done.1 = bf16[512,512]{1,0:T(8,128)(2,1)S(1)} collective-permute-done((bf16[512,512]{1,0:T(8,128)(2,1)}, bf16[512,512]{1,0:T(8,128)(2,1)S(1)}, u32[]{:S(2)}, u32[]{:S(2)}) %collective-permute-start.1) | collective-permute-done | bytes 524320 | tf_op jit(solution)/shard_map/ppermute | solution.py:54
  42.7 1.1 pad_maximum_fusion.refs_0_.refs_4_
  43.9 0.6 collective-permute-start.2
  44.5 0.8 collective-permute-done.10.refs_17_
  45.3 2.2 %collective-permute-start.13 = (bf16[512,512]{1,0:T(8,128)(2,1)S(1)}, bf16[512,512]{1,0:T(8,128)(2,1)S(1)}, u32[]{:S(2)}, u32[]{:S(2)}) collective-permute-start(bf16[512,512]{1,0:T(8,128)(2,1)S(1)} %collective-permute-done.9.refs_16_), channel_id=1, source_target_pairs={{0,64},{1,65},{2,66},{3,67},{4,68},{5,69},{6,70},{7,71},{8,72},{9,... | collective-permute-start | bytes 1572872 | tf_op jit(solution)/shard_map/ppermute | solution.py:54
  47.5 3.4 %collective-permute-done.26.refs_18_ = bf16[512,512]{1,0:T(8,128)(2,1)S(1)} collective-permute-done((bf16[512,512]{1,0:T(8,128)(2,1)S(1)}, bf16[512,512]{1,0:T(8,128)(2,1)S(1)}, u32[]{:S(2)}, u32[]{:S(2)}) %collective-permute-start.26) | collective-permute-done | bytes 524320 | tf_op jit(solution)/shard_map/ppermute | solution.py:54
  50.9 3.4 %collective-permute-start.11 = (bf16[512,512]{1,0:T(8,128)(2,1)S(1)}, bf16[512,512]{1,0:T(8,128)(2,1)}, u32[]{:S(2)}, u32[]{:S(2)}) collective-permute-start(bf16[512,512]{1,0:T(8,128)(2,1)S(1)} %collective-permute-done.10.refs_17_), channel_id=1, source_target_pairs={{0,16},{1,17},{2,18},{3,19},{4,52},{5,53},{6,54},{7,55},{8,24},{9,... | collective-permute-start | bytes 1572872 | tf_op jit(solution)/shard_map/ppermute | solution.py:54
  54.3 0.0 collective-permute-done.18.refs_1_.refs_5_
  54.3 2.9 %collective-permute-start.19 = (bf16[2,512,512]{2,1,0:T(8,128)(2,1)S(1)}, bf16[2,512,512]{2,1,0:T(8,128)(2,1)S(1)}, u32[]{:S(2)}, u32[]{:S(2)}) collective-permute-start(bf16[2,512,512]{2,1,0:T(8,128)(2,1)S(1)} %collective-permute-done.18.refs_1_.refs_5_), channel_id=1, source_target_pairs={{0,1},{1,2},{2,3},{3,0},{4,7},{5,4},{6,5},{7,6},{8,9},{9,10},{10,1... | collective-permute-start | bytes 3145736 | tf_op jit(solution)/shard_map/ppermute | solution.py:54
  57.2 0.0 collective-permute-done.21.refs_8_.refs_12_
  57.2 0.0 collective-permute-start.28
  57.2 1.8 %collective-permute-done.13.refs_20_ = bf16[512,512]{1,0:T(8,128)(2,1)S(1)} collective-permute-done((bf16[512,512]{1,0:T(8,128)(2,1)S(1)}, bf16[512,512]{1,0:T(8,128)(2,1)S(1)}, u32[]{:S(2)}, u32[]{:S(2)}) %collective-permute-start.13) | collective-permute-done | bytes 524320 | tf_op jit(solution)/shard_map/ppermute | solution.py:54
  59.0 2.1 %collective-permute-start.5 = (bf16[2,512,512]{2,1,0:T(8,128)(2,1)S(1)}, bf16[2,512,512]{2,1,0:T(8,128)(2,1)S(1)}, u32[]{:S(2)}, u32[]{:S(2)}) collective-permute-start(bf16[2,512,512]{2,1,0:T(8,128)(2,1)S(1)} %pad_maximum_fusion.refs_0_.refs_4_), channel_id=1, source_target_pairs={{0,4},{1,5},{2,6},{3,7},{4,0},{5,1},{6,2},{7,3},{8,12},{9,13},{10,... | collective-permute-start | bytes 3145736 | tf_op jit(solution)/shard_map/ppermute | solution.py:54
  61.2 0.0 collective-permute-done.11.refs_18_
  61.2 3.1 %collective-permute-start.27 = (bf16[512,512]{1,0:T(8,128)(2,1)S(1)}, bf16[512,512]{1,0:T(8,128)(2,1)S(1)}, u32[]{:S(2)}, u32[]{:S(2)}) collective-permute-start(bf16[512,512]{1,0:T(8,128)(2,1)S(1)} %collective-permute-done.26.refs_18_), channel_id=1, source_target_pairs={{0,16},{1,17},{2,18},{3,19},{4,52},{5,53},{6,54},{7,55},{8,24},{9,... | collective-permute-start | bytes 1572872 | tf_op jit(solution)/shard_map/ppermute | solution.py:54
  64.2 0.0 collective-permute-done.2.refs_1_.refs_5_
  64.3 2.5 %collective-permute-start.3 = (bf16[2,512,512]{2,1,0:T(8,128)(2,1)S(1)}, bf16[2,512,512]{2,1,0:T(8,128)(2,1)}, u32[]{:S(2)}, u32[]{:S(2)}) collective-permute-start(bf16[2,512,512]{2,1,0:T(8,128)(2,1)S(1)} %collective-permute-done.2.refs_1_.refs_5_), channel_id=1, source_target_pairs={{0,1},{1,2},{2,3},{3,0},{4,7},{5,4},{6,5},{7,6},{8,9},{9,10},{10,1... | collective-permute-start | bytes 3145736 | tf_op jit(solution)/shard_map/ppermute | solution.py:54
  66.7 5.0 %collective-permute-done.28.refs_20_ = bf16[512,512]{1,0:T(8,128)(2,1)S(1)} collective-permute-done((bf16[512,512]{1,0:T(8,128)(2,1)S(1)}, bf16[512,512]{1,0:T(8,128)(2,1)S(1)}, u32[]{:S(2)}, u32[]{:S(2)}) %collective-permute-start.28) | collective-permute-done | bytes 524320 | tf_op jit(solution)/shard_map/ppermute | solution.py:54
  71.7 2.2 %collective-permute-start.14 = (bf16[512,512]{1,0:T(8,128)(2,1)S(1)}, bf16[512,512]{1,0:T(8,128)(2,1)S(1)}, u32[]{:S(2)}, u32[]{:S(2)}) collective-permute-start(bf16[512,512]{1,0:T(8,128)(2,1)S(1)} %collective-permute-done.13.refs_20_), channel_id=1, source_target_pairs={{0,16},{1,17},{2,18},{3,19},{4,52},{5,53},{6,54},{7,55},{8,24},{9,... | collective-permute-start | bytes 1572872 | tf_op jit(solution)/shard_map/ppermute | solution.py:54
  73.9 0.0 collective-permute-done.27.refs_19_
  73.9 0.0 collective-permute-start.22
  73.9 1.5 %collective-permute-start.20 = (bf16[2,512,512]{2,1,0:T(8,128)(2,1)S(1)}, bf16[2,512,512]{2,1,0:T(8,128)(2,1)S(1)}, u32[]{:S(2)}, u32[]{:S(2)}) collective-permute-start(bf16[2,512,512]{2,1,0:T(8,128)(2,1)S(1)} %collective-permute-done.19.refs_2_.refs_6_), channel_id=1, source_target_pairs={{0,1},{1,2},{2,3},{3,0},{4,7},{5,4},{6,5},{7,6},{8,9},{9,10},{10,1... | collective-permute-start | bytes 3145736 | tf_op jit(solution)/shard_map/ppermute | solution.py:54
  75.4 4.8 %collective-permute-done.14.refs_21_ = bf16[512,512]{1,0:T(8,128)(2,1)S(1)} collective-permute-done((bf16[512,512]{1,0:T(8,128)(2,1)S(1)}, bf16[512,512]{1,0:T(8,128)(2,1)S(1)}, u32[]{:S(2)}, u32[]{:S(2)}) %collective-permute-start.14) | collective-permute-done | bytes 524320 | tf_op jit(solution)/shard_map/ppermute | solution.py:54
  80.1 3.3 %collective-permute-start.29 = (bf16[512,512]{1,0:T(8,128)(2,1)S(1)}, bf16[512,512]{1,0:T(8,128)(2,1)S(1)}, u32[]{:S(2)}, u32[]{:S(2)}) collective-permute-start(bf16[512,512]{1,0:T(8,128)(2,1)S(1)} %collective-permute-done.28.refs_20_), channel_id=1, source_target_pairs={{0,16},{1,17},{2,18},{3,19},{4,52},{5,53},{6,54},{7,55},{8,24},{9,... | collective-permute-start | bytes 1572872 | tf_op jit(solution)/shard_map/ppermute | solution.py:54
  83.5 2.5 %collective-permute-start.31 = (bf16[512,512]{1,0:T(8,128)(2,1)S(1)}, bf16[512,512]{1,0:T(8,128)(2,1)S(1)}, u32[]{:S(2)}, u32[]{:S(2)}) collective-permute-start(bf16[512,512]{1,0:T(8,128)(2,1)S(1)} %collective-permute-done.27.refs_19_), channel_id=1, source_target_pairs={{0,64},{1,65},{2,66},{3,67},{4,68},{5,69},{6,70},{7,71},{8,72},{9,... | collective-permute-start | bytes 1572872 | tf_op jit(solution)/shard_map/ppermute | solution.py:54
  86.0 0.4 collective-permute-start.4
  86.4 3.2 %collective-permute-done.29.refs_21_ = bf16[512,512]{1,0:T(8,128)(2,1)S(1)} collective-permute-done((bf16[512,512]{1,0:T(8,128)(2,1)S(1)}, bf16[512,512]{1,0:T(8,128)(2,1)S(1)}, u32[]{:S(2)}, u32[]{:S(2)}) %collective-permute-start.29) | collective-permute-done | bytes 524320 | tf_op jit(solution)/shard_map/ppermute | solution.py:54
  89.6 3.4 %collective-permute-start.15 = (bf16[512,512]{1,0:T(8,128)(2,1)S(1)}, bf16[512,512]{1,0:T(8,128)(2,1)}, u32[]{:S(2)}, u32[]{:S(2)}) collective-permute-start(bf16[512,512]{1,0:T(8,128)(2,1)S(1)} %collective-permute-done.14.refs_21_), channel_id=1, source_target_pairs={{0,16},{1,17},{2,18},{3,19},{4,52},{5,53},{6,54},{7,55},{8,24},{9,... | collective-permute-start | bytes 1572872 | tf_op jit(solution)/shard_map/ppermute | solution.py:54
  93.0 4.8 %collective-permute-done.31.refs_23_ = bf16[512,512]{1,0:T(8,128)(2,1)S(1)} collective-permute-done((bf16[512,512]{1,0:T(8,128)(2,1)S(1)}, bf16[512,512]{1,0:T(8,128)(2,1)S(1)}, u32[]{:S(2)}, u32[]{:S(2)}) %collective-permute-start.31) | collective-permute-done | bytes 524320 | tf_op jit(solution)/shard_map/ppermute | solution.py:54
  97.8 0.0 collective-permute-start.23
  97.8 0.0 collective-permute-done.22.refs_9_.refs_13_
  97.8 1.6 %collective-permute-start.30 = (bf16[512,512]{1,0:T(8,128)(2,1)S(1)}, bf16[512,512]{1,0:T(8,128)(2,1)S(1)}, u32[]{:S(2)}, u32[]{:S(2)}) collective-permute-start(bf16[512,512]{1,0:T(8,128)(2,1)S(1)} %collective-permute-done.29.refs_21_), channel_id=1, source_target_pairs={{0,16},{1,17},{2,18},{3,19},{4,52},{5,53},{6,54},{7,55},{8,24},{9,... | collective-permute-start | bytes 1572872 | tf_op jit(solution)/shard_map/ppermute | solution.py:54
  99.4 0.0 collective-permute-done.20.refs_3_.refs_7_
  99.5 0.1 collective-permute-start.24
  99.6 3.4 %collective-permute-start.6 = (bf16[2,512,512]{2,1,0:T(8,128)(2,1)S(1)}, bf16[2,512,512]{2,1,0:T(8,128)(2,1)}, u32[]{:S(2)}, u32[]{:S(2)}) collective-permute-start(bf16[2,512,512]{2,1,0:T(8,128)(2,1)S(1)} %collective-permute-done.2.refs_1_.refs_5_), channel_id=1, source_target_pairs={{0,4},{1,5},{2,6},{3,7},{4,0},{5,1},{6,2},{7,3},{8,12},{9,13},{10,... | collective-permute-start | bytes 3145736 | tf_op jit(solution)/shard_map/ppermute | solution.py:54
  103.0 3.2 %collective-permute-done.30.refs_22_ = bf16[512,512]{1,0:T(8,128)(2,1)S(1)} collective-permute-done((bf16[512,512]{1,0:T(8,128)(2,1)S(1)}, bf16[512,512]{1,0:T(8,128)(2,1)S(1)}, u32[]{:S(2)}, u32[]{:S(2)}) %collective-permute-start.30) | collective-permute-done | bytes 524320 | tf_op jit(solution)/shard_map/ppermute | solution.py:54
  106.2 2.5 %collective-permute-start.7 = (bf16[2,512,512]{2,1,0:T(8,128)(2,1)}, bf16[2,512,512]{2,1,0:T(8,128)(2,1)}, u32[]{:S(2)}, u32[]{:S(2)}) collective-permute-start(bf16[2,512,512]{2,1,0:T(8,128)(2,1)} %collective-permute-done.3.refs_2_.refs_6_), channel_id=1, source_target_pairs={{0,4},{1,5},{2,6},{3,7},{4,0},{5,1},{6,2},{7,3},{8,12},{9,13},{10,... | collective-permute-start | bytes 3145736 | tf_op jit(solution)/shard_map/ppermute | solution.py:54
  108.7 0.1 collective-permute-start.8
  108.8 0.0 collective-permute-done.23.refs_10_.refs_14_
  108.8 0.5 collective-permute-start.12
  109.3 0.5 copy-done.9
  109.8 0.4 collective-permute-start.16
  110.2 0.5 copy-done.10
  110.8 0.6 stack.41.place
  111.4 15.7 %shard_map.60 = bf16[2048,1024]{1,0:T(8,128)(2,1)} custom-call(s32[5]{0:T(128)} %stack.41.place, bf16[2,512,512]{2,1,0:T(8,128)(2,1)} %copy-done.1, bf16[2,512,512]{2,1,0:T(8,128)(2,1)} %copy-done.3, bf16[2,512,512]{2,1,0:T(8,128)(2,1)} %copy-done.6, bf16[2,512,512]{2,1,0:T(8,128)(2,1)} %copy-done.8, bf16[2,512,512]{2,1,0:T(8,128)(2,1)} %copy-done.1, ...), custom_call_target="tpu_custom_call" | custom-call | flops 1000 | bytes 1000 | tf_op jit(solution)/shard_map/pallas_call | solution.py:128
  127.1 0.0 collective-permute-done.12.refs_19_
  127.1 0.0 collective-permute-done.16.refs_23_
  127.1 0.0 collective-permute-done.7.refs_10_.refs_14_
  127.1 15.7 %shard_map.59 = bf16[2048,1024]{1,0:T(8,128)(2,1)} custom-call(s32[5]{0:T(128)} %stack.41.place, bf16[2,512,512]{2,1,0:T(8,128)(2,1)} %copy-done, bf16[2,512,512]{2,1,0:T(8,128)(2,1)} %copy-done.2, bf16[2,512,512]{2,1,0:T(8,128)(2,1)} %collective-permute-done.3.refs_2_.refs_6_, bf16[2,512,512]{2,1,0:T(8,128)(2,1)} %collective-permute-done.4.refs_3_.refs_7_, ...), custom_call_target="tpu_custom_call" | custom-call | flops 1000 | bytes 1000 | tf_op jit(solution)/shard_map/pallas_call | solution.py:128
  (51 shorter events, 0.1 us)
Async XLA Ops:
  0.6 19.0 %collective-permute-start = (bf16[512,512]{1,0:T(8,128)(2,1)}, bf16[512,512]{1,0:T(8,128)(2,1)S(1)}, u32[]{:S(2)}, u32[]{:S(2)}) collective-permute-start(bf16[512,512]{1,0:T(8,128)(2,1)} %param.5), channel_id=1, source_target_pairs={{0,32},{1,48},{2,0},{3,16},{4,96},{5,112},{6,64},{7,80},{8,81},{9,... | collective-permute-start | bytes 1572872 | tf_op jit(solution)/shard_map/ppermute | solution.py:54
  7.5 24.5 %collective-permute-start.17 = (bf16[512,512]{1,0:T(8,128)(2,1)}, bf16[512,512]{1,0:T(8,128)(2,1)S(1)}, u32[]{:S(2)}, u32[]{:S(2)}) collective-permute-start(bf16[512,512]{1,0:T(8,128)(2,1)} %param.5), channel_id=1, source_target_pairs={{0,8},{1,9},{2,10},{3,11},{4,12},{5,13},{6,14},{7,15},{8,0},{9,1},... | collective-permute-start | bytes 1572872 | tf_op jit(solution)/shard_map/ppermute | solution.py:54
  7.5 26.9 %collective-permute-start.9 = (bf16[512,512]{1,0:T(8,128)(2,1)}, bf16[512,512]{1,0:T(8,128)(2,1)S(1)}, u32[]{:S(2)}, u32[]{:S(2)}) collective-permute-start(bf16[512,512]{1,0:T(8,128)(2,1)} %param.4), channel_id=1, source_target_pairs={{0,32},{1,48},{2,0},{3,16},{4,96},{5,112},{6,64},{7,80},{8,81},{9,... | collective-permute-start | bytes 1572872 | tf_op jit(solution)/shard_map/ppermute | solution.py:54
  19.6 90.6 %copy-start.12 = (bf16[512,512]{1,0:T(8,128)(2,1)}, bf16[512,512]{1,0:T(8,128)(2,1)S(1)}, u32[]{:S(2)}) copy-start(bf16[512,512]{1,0:T(8,128)(2,1)S(1)} %collective-permute-done.refs_16_) | copy-start | bytes 1572868
  19.6 19.6 %collective-permute-start.25 = (bf16[512,512]{1,0:T(8,128)(2,1)S(1)}, bf16[512,512]{1,0:T(8,128)(2,1)S(1)}, u32[]{:S(2)}, u32[]{:S(2)}) collective-permute-start(bf16[512,512]{1,0:T(8,128)(2,1)S(1)} %collective-permute-done.refs_16_), channel_id=1, source_target_pairs={{0,16},{1,17},{2,18},{3,19},{4,52},{5,53},{6,54},{7,55},{8,24},{9,... | collective-permute-start | bytes 1572872 | tf_op jit(solution)/shard_map/ppermute | solution.py:54
  21.3 21.4 %collective-permute-start.1 = (bf16[512,512]{1,0:T(8,128)(2,1)}, bf16[512,512]{1,0:T(8,128)(2,1)S(1)}, u32[]{:S(2)}, u32[]{:S(2)}) collective-permute-start(bf16[512,512]{1,0:T(8,128)(2,1)} %param.4), channel_id=1, source_target_pairs={{0,8},{1,9},{2,10},{3,11},{4,12},{5,13},{6,14},{7,15},{8,0},{9,1},... | collective-permute-start | bytes 1572872 | tf_op jit(solution)/shard_map/ppermute | solution.py:54
  33.1 78.2 %copy-start.1 = (bf16[2,512,512]{2,1,0:T(8,128)(2,1)}, bf16[2,512,512]{2,1,0:T(8,128)(2,1)S(1)}, u32[]{:S(2)}) copy-start(bf16[2,512,512]{2,1,0:T(8,128)(2,1)S(1)} %pad_maximum_fusion.1.refs_0_.refs_4_) | copy-start | bytes 3145732
  33.2 21.2 %collective-permute-start.18 = (bf16[2,512,512]{2,1,0:T(8,128)(2,1)S(1)}, bf16[2,512,512]{2,1,0:T(8,128)(2,1)S(1)}, u32[]{:S(2)}, u32[]{:S(2)}) collective-permute-start(bf16[2,512,512]{2,1,0:T(8,128)(2,1)S(1)} %pad_maximum_fusion.1.refs_0_.refs_4_), channel_id=1, source_target_pairs={{0,1},{1,2},{2,3},{3,0},{4,7},{5,4},{6,5},{7,6},{8,9},{9,10},{10,1... | collective-permute-start | bytes 3145736 | tf_op jit(solution)/shard_map/ppermute | solution.py:54
  33.2 23.9 %collective-permute-start.21 = (bf16[2,512,512]{2,1,0:T(8,128)(2,1)S(1)}, bf16[2,512,512]{2,1,0:T(8,128)(2,1)S(1)}, u32[]{:S(2)}, u32[]{:S(2)}) collective-permute-start(bf16[2,512,512]{2,1,0:T(8,128)(2,1)S(1)} %pad_maximum_fusion.1.refs_0_.refs_4_), channel_id=1, source_target_pairs={{0,4},{1,5},{2,6},{3,7},{4,0},{5,1},{6,2},{7,3},{8,12},{9,13},{10,... | collective-permute-start | bytes 3145736 | tf_op jit(solution)/shard_map/ppermute | solution.py:54
  34.4 75.8 %copy-start.11 = (bf16[512,512]{1,0:T(8,128)(2,1)}, bf16[512,512]{1,0:T(8,128)(2,1)S(1)}, u32[]{:S(2)}) copy-start(bf16[512,512]{1,0:T(8,128)(2,1)S(1)} %collective-permute-done.9.refs_16_) | copy-start | bytes 1572868
  34.4 10.9 %collective-permute-start.10 = (bf16[512,512]{1,0:T(8,128)(2,1)S(1)}, bf16[512,512]{1,0:T(8,128)(2,1)S(1)}, u32[]{:S(2)}, u32[]{:S(2)}) collective-permute-start(bf16[512,512]{1,0:T(8,128)(2,1)S(1)} %collective-permute-done.9.refs_16_), channel_id=1, source_target_pairs={{0,16},{1,17},{2,18},{3,19},{4,52},{5,53},{6,54},{7,55},{8,24},{9,... | collective-permute-start | bytes 1572872 | tf_op jit(solution)/shard_map/ppermute | solution.py:54
  39.2 71.0 %copy-start.14 = (bf16[512,512]{1,0:T(8,128)(2,1)}, bf16[512,512]{1,0:T(8,128)(2,1)S(1)}, u32[]{:S(2)}) copy-start(bf16[512,512]{1,0:T(8,128)(2,1)S(1)} %collective-permute-done.25.refs_17_) | copy-start | bytes 1572868
  39.2 11.8 %collective-permute-start.26 = (bf16[512,512]{1,0:T(8,128)(2,1)S(1)}, bf16[512,512]{1,0:T(8,128)(2,1)S(1)}, u32[]{:S(2)}, u32[]{:S(2)}) collective-permute-start(bf16[512,512]{1,0:T(8,128)(2,1)S(1)} %collective-permute-done.25.refs_17_), channel_id=1, source_target_pairs={{0,16},{1,17},{2,18},{3,19},{4,52},{5,53},{6,54},{7,55},{8,24},{9,... | collective-permute-start | bytes 1572872 | tf_op jit(solution)/shard_map/ppermute | solution.py:54
  43.9 83.2 %copy-start = (bf16[2,512,512]{2,1,0:T(8,128)(2,1)}, bf16[2,512,512]{2,1,0:T(8,128)(2,1)S(1)}, u32[]{:S(2)}) copy-start(bf16[2,512,512]{2,1,0:T(8,128)(2,1)S(1)} %pad_maximum_fusion.refs_0_.refs_4_) | copy-start | bytes 3145732
  43.9 20.4 %collective-permute-start.2 = (bf16[2,512,512]{2,1,0:T(8,128)(2,1)S(1)}, bf16[2,512,512]{2,1,0:T(8,128)(2,1)S(1)}, u32[]{:S(2)}, u32[]{:S(2)}) collective-permute-start(bf16[2,512,512]{2,1,0:T(8,128)(2,1)S(1)} %pad_maximum_fusion.refs_0_.refs_4_), channel_id=1, source_target_pairs={{0,1},{1,2},{2,3},{3,0},{4,7},{5,4},{6,5},{7,6},{8,9},{9,10},{10,1... | collective-permute-start | bytes 3145736 | tf_op jit(solution)/shard_map/ppermute | solution.py:54
  45.3 64.9 %copy-start.13 = (bf16[512,512]{1,0:T(8,128)(2,1)}, bf16[512,512]{1,0:T(8,128)(2,1)S(1)}, u32[]{:S(2)}) copy-start(bf16[512,512]{1,0:T(8,128)(2,1)S(1)} %collective-permute-done.10.refs_17_) | copy-start | bytes 1572868
  45.3 13.7 %collective-permute-start.13 = (bf16[512,512]{1,0:T(8,128)(2,1)S(1)}, bf16[512,512]{1,0:T(8,128)(2,1)S(1)}, u32[]{:S(2)}, u32[]{:S(2)}) collective-permute-start(bf16[512,512]{1,0:T(8,128)(2,1)S(1)} %collective-permute-done.9.refs_16_), channel_id=1, source_target_pairs={{0,64},{1,65},{2,66},{3,67},{4,68},{5,69},{6,70},{7,71},{8,72},{9,... | collective-permute-start | bytes 1572872 | tf_op jit(solution)/shard_map/ppermute | solution.py:54
  50.9 59.3 %copy-start.16 = (bf16[512,512]{1,0:T(8,128)(2,1)}, bf16[512,512]{1,0:T(8,128)(2,1)S(1)}, u32[]{:S(2)}) copy-start(bf16[512,512]{1,0:T(8,128)(2,1)S(1)} %collective-permute-done.26.refs_18_) | copy-start | bytes 1572868
  50.9 10.2 %collective-permute-start.11 = (bf16[512,512]{1,0:T(8,128)(2,1)S(1)}, bf16[512,512]{1,0:T(8,128)(2,1)}, u32[]{:S(2)}, u32[]{:S(2)}) collective-permute-start(bf16[512,512]{1,0:T(8,128)(2,1)S(1)} %collective-permute-done.10.refs_17_), channel_id=1, source_target_pairs={{0,16},{1,17},{2,18},{3,19},{4,52},{5,53},{6,54},{7,55},{8,24},{9,... | collective-permute-start | bytes 1572872 | tf_op jit(solution)/shard_map/ppermute | solution.py:54
  54.3 45.2 %copy-start.3 = (bf16[2,512,512]{2,1,0:T(8,128)(2,1)}, bf16[2,512,512]{2,1,0:T(8,128)(2,1)S(1)}, u32[]{:S(2)}) copy-start(bf16[2,512,512]{2,1,0:T(8,128)(2,1)S(1)} %collective-permute-done.18.refs_1_.refs_5_) | copy-start | bytes 3145732
  54.3 19.6 %collective-permute-start.19 = (bf16[2,512,512]{2,1,0:T(8,128)(2,1)S(1)}, bf16[2,512,512]{2,1,0:T(8,128)(2,1)S(1)}, u32[]{:S(2)}, u32[]{:S(2)}) collective-permute-start(bf16[2,512,512]{2,1,0:T(8,128)(2,1)S(1)} %collective-permute-done.18.refs_1_.refs_5_), channel_id=1, source_target_pairs={{0,1},{1,2},{2,3},{3,0},{4,7},{5,4},{6,5},{7,6},{8,9},{9,10},{10,1... | collective-permute-start | bytes 3145736 | tf_op jit(solution)/shard_map/ppermute | solution.py:54
  57.2 42.4 %copy-start.4 = (bf16[2,512,512]{2,1,0:T(8,128)(2,1)}, bf16[2,512,512]{2,1,0:T(8,128)(2,1)S(1)}, u32[]{:S(2)}) copy-start(bf16[2,512,512]{2,1,0:T(8,128)(2,1)S(1)} %collective-permute-done.21.refs_8_.refs_12_) | copy-start | bytes 3145732
  57.2 14.5 %collective-permute-start.28 = (bf16[512,512]{1,0:T(8,128)(2,1)S(1)}, bf16[512,512]{1,0:T(8,128)(2,1)S(1)}, u32[]{:S(2)}, u32[]{:S(2)}) collective-permute-start(bf16[512,512]{1,0:T(8,128)(2,1)S(1)} %collective-permute-done.refs_16_), channel_id=1, source_target_pairs={{0,64},{1,65},{2,66},{3,67},{4,68},{5,69},{6,70},{7,71},{8,72},{9,... | collective-permute-start | bytes 1572872 | tf_op jit(solution)/shard_map/ppermute | solution.py:54
  59.0 34.0 %copy-start.15 = (bf16[512,512]{1,0:T(8,128)(2,1)}, bf16[512,512]{1,0:T(8,128)(2,1)S(1)}, u32[]{:S(2)}) copy-start(bf16[512,512]{1,0:T(8,128)(2,1)S(1)} %collective-permute-done.13.refs_20_) | copy-start | bytes 1572868
  59.0 24.5 %collective-permute-start.5 = (bf16[2,512,512]{2,1,0:T(8,128)(2,1)S(1)}, bf16[2,512,512]{2,1,0:T(8,128)(2,1)S(1)}, u32[]{:S(2)}, u32[]{:S(2)}) collective-permute-start(bf16[2,512,512]{2,1,0:T(8,128)(2,1)S(1)} %pad_maximum_fusion.refs_0_.refs_4_), channel_id=1, source_target_pairs={{0,4},{1,5},{2,6},{3,7},{4,0},{5,1},{6,2},{7,3},{8,12},{9,13},{10,... | collective-permute-start | bytes 3145736 | tf_op jit(solution)/shard_map/ppermute | solution.py:54
  61.2 12.7 %collective-permute-start.27 = (bf16[512,512]{1,0:T(8,128)(2,1)S(1)}, bf16[512,512]{1,0:T(8,128)(2,1)S(1)}, u32[]{:S(2)}, u32[]{:S(2)}) collective-permute-start(bf16[512,512]{1,0:T(8,128)(2,1)S(1)} %collective-permute-done.26.refs_18_), channel_id=1, source_target_pairs={{0,16},{1,17},{2,18},{3,19},{4,52},{5,53},{6,54},{7,55},{8,24},{9,... | collective-permute-start | bytes 1572872 | tf_op jit(solution)/shard_map/ppermute | solution.py:54
  64.2 62.8 %copy-start.2 = (bf16[2,512,512]{2,1,0:T(8,128)(2,1)}, bf16[2,512,512]{2,1,0:T(8,128)(2,1)S(1)}, u32[]{:S(2)}) copy-start(bf16[2,512,512]{2,1,0:T(8,128)(2,1)S(1)} %collective-permute-done.2.refs_1_.refs_5_) | copy-start | bytes 3145732
  64.3 21.7 %collective-permute-start.3 = (bf16[2,512,512]{2,1,0:T(8,128)(2,1)S(1)}, bf16[2,512,512]{2,1,0:T(8,128)(2,1)}, u32[]{:S(2)}, u32[]{:S(2)}) collective-permute-start(bf16[2,512,512]{2,1,0:T(8,128)(2,1)S(1)} %collective-permute-done.2.refs_1_.refs_5_), channel_id=1, source_target_pairs={{0,1},{1,2},{2,3},{3,0},{4,7},{5,4},{6,5},{7,6},{8,9},{9,10},{10,1... | collective-permute-start | bytes 3145736 | tf_op jit(solution)/shard_map/ppermute | solution.py:54
  71.7 21.3 %copy-start.18 = (bf16[512,512]{1,0:T(8,128)(2,1)}, bf16[512,512]{1,0:T(8,128)(2,1)S(1)}, u32[]{:S(2)}) copy-start(bf16[512,512]{1,0:T(8,128)(2,1)S(1)} %collective-permute-done.28.refs_20_) | copy-start | bytes 1572868
  71.7 8.4 %collective-permute-start.14 = (bf16[512,512]{1,0:T(8,128)(2,1)S(1)}, bf16[512,512]{1,0:T(8,128)(2,1)S(1)}, u32[]{:S(2)}, u32[]{:S(2)}) collective-permute-start(bf16[512,512]{1,0:T(8,128)(2,1)S(1)} %collective-permute-done.13.refs_20_), channel_id=1, source_target_pairs={{0,16},{1,17},{2,18},{3,19},{4,52},{5,53},{6,54},{7,55},{8,24},{9,... | collective-permute-start | bytes 1572872 | tf_op jit(solution)/shard_map/ppermute | solution.py:54
  73.9 25.6 %copy-start.19 = (bf16[512,512]{1,0:T(8,128)(2,1)}, bf16[512,512]{1,0:T(8,128)(2,1)S(1)}, u32[]{:S(2)}) copy-start(bf16[512,512]{1,0:T(8,128)(2,1)S(1)} %collective-permute-done.27.refs_19_) | copy-start | bytes 1572868
  73.9 23.9 %collective-permute-start.22 = (bf16[2,512,512]{2,1,0:T(8,128)(2,1)S(1)}, bf16[2,512,512]{2,1,0:T(8,128)(2,1)S(1)}, u32[]{:S(2)}, u32[]{:S(2)}) collective-permute-start(bf16[2,512,512]{2,1,0:T(8,128)(2,1)S(1)} %collective-permute-done.18.refs_1_.refs_5_), channel_id=1, source_target_pairs={{0,4},{1,5},{2,6},{3,7},{4,0},{5,1},{6,2},{7,3},{8,12},{9,13},{10,... | collective-permute-start | bytes 3145736 | tf_op jit(solution)/shard_map/ppermute | solution.py:54
  73.9 32.3 %copy-start.6 = (bf16[2,512,512]{2,1,0:T(8,128)(2,1)}, bf16[2,512,512]{2,1,0:T(8,128)(2,1)S(1)}, u32[]{:S(2)}) copy-start(bf16[2,512,512]{2,1,0:T(8,128)(2,1)S(1)} %collective-permute-done.19.refs_2_.refs_6_) | copy-start | bytes 3145732
  73.9 25.6 %collective-permute-start.20 = (bf16[2,512,512]{2,1,0:T(8,128)(2,1)S(1)}, bf16[2,512,512]{2,1,0:T(8,128)(2,1)S(1)}, u32[]{:S(2)}, u32[]{:S(2)}) collective-permute-start(bf16[2,512,512]{2,1,0:T(8,128)(2,1)S(1)} %collective-permute-done.19.refs_2_.refs_6_), channel_id=1, source_target_pairs={{0,1},{1,2},{2,3},{3,0},{4,7},{5,4},{6,5},{7,6},{8,9},{9,10},{10,1... | collective-permute-start | bytes 3145736 | tf_op jit(solution)/shard_map/ppermute | solution.py:54
  80.1 30.1 %copy-start.17 = (bf16[512,512]{1,0:T(8,128)(2,1)}, bf16[512,512]{1,0:T(8,128)(2,1)S(1)}, u32[]{:S(2)}) copy-start(bf16[512,512]{1,0:T(8,128)(2,1)S(1)} %collective-permute-done.14.refs_21_) | copy-start | bytes 1572868
  80.1 9.5 %collective-permute-start.29 = (bf16[512,512]{1,0:T(8,128)(2,1)S(1)}, bf16[512,512]{1,0:T(8,128)(2,1)S(1)}, u32[]{:S(2)}, u32[]{:S(2)}) collective-permute-start(bf16[512,512]{1,0:T(8,128)(2,1)S(1)} %collective-permute-done.28.refs_20_), channel_id=1, source_target_pairs={{0,16},{1,17},{2,18},{3,19},{4,52},{5,53},{6,54},{7,55},{8,24},{9,... | collective-permute-start | bytes 1572872 | tf_op jit(solution)/shard_map/ppermute | solution.py:54
  83.5 19.5 %copy-start.5 = (bf16[2,512,512]{2,1,0:T(8,128)(2,1)}, bf16[2,512,512]{2,1,0:T(8,128)(2,1)S(1)}, u32[]{:S(2)}) copy-start(bf16[2,512,512]{2,1,0:T(8,128)(2,1)S(1)} %collective-permute-done.5.refs_8_.refs_12_) | copy-start | bytes 3145732
  83.5 14.3 %collective-permute-start.31 = (bf16[512,512]{1,0:T(8,128)(2,1)S(1)}, bf16[512,512]{1,0:T(8,128)(2,1)S(1)}, u32[]{:S(2)}, u32[]{:S(2)}) collective-permute-start(bf16[512,512]{1,0:T(8,128)(2,1)S(1)} %collective-permute-done.27.refs_19_), channel_id=1, source_target_pairs={{0,64},{1,65},{2,66},{3,67},{4,68},{5,69},{6,70},{7,71},{8,72},{9,... | collective-permute-start | bytes 1572872 | tf_op jit(solution)/shard_map/ppermute | solution.py:54
  86.0 22.8 %collective-permute-start.4 = (bf16[2,512,512]{2,1,0:T(8,128)(2,1)}, bf16[2,512,512]{2,1,0:T(8,128)(2,1)}, u32[]{:S(2)}, u32[]{:S(2)}) collective-permute-start(bf16[2,512,512]{2,1,0:T(8,128)(2,1)} %collective-permute-done.3.refs_2_.refs_6_), channel_id=1, source_target_pairs={{0,1},{1,2},{2,3},{3,0},{4,7},{5,4},{6,5},{7,6},{8,9},{9,10},{10,1... | collective-permute-start | bytes 3145736 | tf_op jit(solution)/shard_map/ppermute | solution.py:54
  89.6 20.6 %copy-start.20 = (bf16[512,512]{1,0:T(8,128)(2,1)}, bf16[512,512]{1,0:T(8,128)(2,1)S(1)}, u32[]{:S(2)}) copy-start(bf16[512,512]{1,0:T(8,128)(2,1)S(1)} %collective-permute-done.29.refs_21_) | copy-start | bytes 1572868
  89.6 9.9 %collective-permute-start.15 = (bf16[512,512]{1,0:T(8,128)(2,1)S(1)}, bf16[512,512]{1,0:T(8,128)(2,1)}, u32[]{:S(2)}, u32[]{:S(2)}) collective-permute-start(bf16[512,512]{1,0:T(8,128)(2,1)S(1)} %collective-permute-done.14.refs_21_), channel_id=1, source_target_pairs={{0,16},{1,17},{2,18},{3,19},{4,52},{5,53},{6,54},{7,55},{8,24},{9,... | collective-permute-start | bytes 1572872 | tf_op jit(solution)/shard_map/ppermute | solution.py:54
  97.8 1.6 %copy-start.21 = (bf16[512,512]{1,0:T(8,128)(2,1)}, bf16[512,512]{1,0:T(8,128)(2,1)S(1)}, u32[]{:S(2)}) copy-start(bf16[512,512]{1,0:T(8,128)(2,1)S(1)} %collective-permute-done.31.refs_23_) | copy-start | bytes 1572868
  97.8 11.0 %collective-permute-start.23 = (bf16[2,512,512]{2,1,0:T(8,128)(2,1)S(1)}, bf16[2,512,512]{2,1,0:T(8,128)(2,1)S(1)}, u32[]{:S(2)}, u32[]{:S(2)}) collective-permute-start(bf16[2,512,512]{2,1,0:T(8,128)(2,1)S(1)} %collective-permute-done.19.refs_2_.refs_6_), channel_id=1, source_target_pairs={{0,4},{1,5},{2,6},{3,7},{4,0},{5,1},{6,2},{7,3},{8,12},{9,13},{10,... | collective-permute-start | bytes 3145736 | tf_op jit(solution)/shard_map/ppermute | solution.py:54
  97.8 11.0 %copy-start.7 = (bf16[2,512,512]{2,1,0:T(8,128)(2,1)}, bf16[2,512,512]{2,1,0:T(8,128)(2,1)S(1)}, u32[]{:S(2)}) copy-start(bf16[2,512,512]{2,1,0:T(8,128)(2,1)S(1)} %collective-permute-done.22.refs_9_.refs_13_) | copy-start | bytes 3145732
  97.8 8.4 %collective-permute-start.30 = (bf16[512,512]{1,0:T(8,128)(2,1)S(1)}, bf16[512,512]{1,0:T(8,128)(2,1)S(1)}, u32[]{:S(2)}, u32[]{:S(2)}) collective-permute-start(bf16[512,512]{1,0:T(8,128)(2,1)S(1)} %collective-permute-done.29.refs_21_), channel_id=1, source_target_pairs={{0,16},{1,17},{2,18},{3,19},{4,52},{5,53},{6,54},{7,55},{8,24},{9,... | collective-permute-start | bytes 1572872 | tf_op jit(solution)/shard_map/ppermute | solution.py:54
  99.4 9.8 %copy-start.8 = (bf16[2,512,512]{2,1,0:T(8,128)(2,1)}, bf16[2,512,512]{2,1,0:T(8,128)(2,1)S(1)}, u32[]{:S(2)}) copy-start(bf16[2,512,512]{2,1,0:T(8,128)(2,1)S(1)} %collective-permute-done.20.refs_3_.refs_7_) | copy-start | bytes 3145732
  99.5 9.8 %collective-permute-start.24 = (bf16[2,512,512]{2,1,0:T(8,128)(2,1)S(1)}, bf16[2,512,512]{2,1,0:T(8,128)(2,1)S(1)}, u32[]{:S(2)}, u32[]{:S(2)}) collective-permute-start(bf16[2,512,512]{2,1,0:T(8,128)(2,1)S(1)} %collective-permute-done.20.refs_3_.refs_7_), channel_id=1, source_target_pairs={{0,4},{1,5},{2,6},{3,7},{4,0},{5,1},{6,2},{7,3},{8,12},{9,13},{10,... | collective-permute-start | bytes 3145736 | tf_op jit(solution)/shard_map/ppermute | solution.py:54
  99.6 27.5 %collective-permute-start.6 = (bf16[2,512,512]{2,1,0:T(8,128)(2,1)S(1)}, bf16[2,512,512]{2,1,0:T(8,128)(2,1)}, u32[]{:S(2)}, u32[]{:S(2)}) collective-permute-start(bf16[2,512,512]{2,1,0:T(8,128)(2,1)S(1)} %collective-permute-done.2.refs_1_.refs_5_), channel_id=1, source_target_pairs={{0,4},{1,5},{2,6},{3,7},{4,0},{5,1},{6,2},{7,3},{8,12},{9,13},{10,... | collective-permute-start | bytes 3145736 | tf_op jit(solution)/shard_map/ppermute | solution.py:54
  106.2 4.0 %copy-start.22 = (bf16[512,512]{1,0:T(8,128)(2,1)}, bf16[512,512]{1,0:T(8,128)(2,1)S(1)}, u32[]{:S(2)}) copy-start(bf16[512,512]{1,0:T(8,128)(2,1)S(1)} %collective-permute-done.30.refs_22_) | copy-start | bytes 1572868
  106.2 20.9 %collective-permute-start.7 = (bf16[2,512,512]{2,1,0:T(8,128)(2,1)}, bf16[2,512,512]{2,1,0:T(8,128)(2,1)}, u32[]{:S(2)}, u32[]{:S(2)}) collective-permute-start(bf16[2,512,512]{2,1,0:T(8,128)(2,1)} %collective-permute-done.3.refs_2_.refs_6_), channel_id=1, source_target_pairs={{0,4},{1,5},{2,6},{3,7},{4,0},{5,1},{6,2},{7,3},{8,12},{9,13},{10,... | collective-permute-start | bytes 3145736 | tf_op jit(solution)/shard_map/ppermute | solution.py:54
  108.7 18.4 %collective-permute-start.8 = (bf16[2,512,512]{2,1,0:T(8,128)(2,1)}, bf16[2,512,512]{2,1,0:T(8,128)(2,1)}, u32[]{:S(2)}, u32[]{:S(2)}) collective-permute-start(bf16[2,512,512]{2,1,0:T(8,128)(2,1)} %collective-permute-done.4.refs_3_.refs_7_), channel_id=1, source_target_pairs={{0,4},{1,5},{2,6},{3,7},{4,0},{5,1},{6,2},{7,3},{8,12},{9,13},{10,... | collective-permute-start | bytes 3145736 | tf_op jit(solution)/shard_map/ppermute | solution.py:54
  108.8 1.0 copy-start.9
  108.8 18.3 %collective-permute-start.12 = (bf16[512,512]{1,0:T(8,128)(2,1)}, bf16[512,512]{1,0:T(8,128)(2,1)}, u32[]{:S(2)}, u32[]{:S(2)}) collective-permute-start(bf16[512,512]{1,0:T(8,128)(2,1)} %collective-permute-done.11.refs_18_), channel_id=1, source_target_pairs={{0,16},{1,17},{2,18},{3,19},{4,52},{5,53},{6,54},{7,55},{8,24},{9,... | collective-permute-start | bytes 1572872 | tf_op jit(solution)/shard_map/ppermute | solution.py:54
  109.8 1.0 copy-start.10
  109.8 17.3 %collective-permute-start.16 = (bf16[512,512]{1,0:T(8,128)(2,1)}, bf16[512,512]{1,0:T(8,128)(2,1)}, u32[]{:S(2)}, u32[]{:S(2)}) collective-permute-start(bf16[512,512]{1,0:T(8,128)(2,1)} %collective-permute-done.15.refs_22_), channel_id=1, source_target_pairs={{0,16},{1,17},{2,18},{3,19},{4,52},{5,53},{6,54},{7,55},{8,24},{9,... | collective-permute-start | bytes 1572872 | tf_op jit(solution)/shard_map/ppermute | solution.py:54
